TPU v7x, 32 devices: a whole 2x2x4 slice. The times are simulated.
32 devices in a mesh: grp: 2 (over y), orb: 16 (over z, x, core).
Axes of the slice: x: 2, y: 2, z: 4, core: 2. Of those that a mesh axis runs over, the one named last changes fastest.
Arguments:
- occupied: float32 [16, 262144], P('orb'), may hold values from -5 to 5
- targets: float32 [32, 262144], P(('grp', 'orb')), may hold values from -8 to 8
- potential: float32 [262144], P('orb'), may hold values from -4 to 4
Outputs:
- updated: float32 [32, 262144], P('grp', 'orb')
All inputs are finite; a program needn't handle non-finite values.
Results may differ from a plain program's by a relative error of at most 0.0003.
Values sent between devices are 32-bit elements; how exact they have to be, the bound alone decides.
No kernel may reach another device: no remote copies, remote signals or barrier semaphores. Data moves between devices by JAX's collectives and lax.ppermute only.
A program may use at most 64 MiB of HBM per device.

v0:
```python
import functools

import jax
import jax.numpy as jnp
import ml_dtypes
import numpy as np
from jax import lax
from jax.experimental import pallas as pl
from jax.experimental.pallas import tpu as pltpu
from jax.sharding import PartitionSpec as P

NGRID = 64
CELLS = 262144
LANES = 128
ROWS = CELLS // LANES
SLAB = NGRID * NGRID // LANES
CHUNK = 32
HALVES = NGRID // CHUNK

SCREEN_SQ = 0.04
BOX_LENGTH = 20.0
STEP_SIZE = 0.3

bf16 = jnp.bfloat16
f32 = jnp.float32
VMEM = pl.BlockSpec(memory_space=pltpu.VMEM)
SMEM = pl.BlockSpec(memory_space=pltpu.SMEM)


def tables():
    index = np.arange(NGRID)
    angles = 2.0 * np.pi * (index[:, None] * index[None, :] % NGRID) / NGRID
    table = np.cos(angles) + np.sin(angles)
    high = table.astype(ml_dtypes.bfloat16)
    low = (table - high.astype(np.float64)).astype(ml_dtypes.bfloat16)

    def twice(block):
        both = np.zeros((2 * NGRID, 2 * NGRID), ml_dtypes.bfloat16)
        both[:NGRID, :NGRID] = block
        both[NGRID:, NGRID:] = block
        return both

    def stacked(high, low):
        return np.concatenate([high, high, low, low], 1)

    row = np.concatenate([twice(high), twice(low)], 1)
    along_z = np.concatenate([row, row], 0)
    order = np.concatenate([index[0::2], index[1::2]])
    return (
        along_z,
        stacked(high, low),
        stacked(high[:, order], low[:, order]),
        stacked(high[order], low[order]),
    )


def halves(value):
    high = value.astype(bf16)
    return high, (value - high.astype(f32)).astype(bf16)


def dot(left, right):
    return jnp.dot(left, right, preferred_element_type=f32)


def along_lanes(value, table):
    out = dot(jnp.concatenate(halves(value), 1), table)
    return out[:, :LANES] + out[:, LANES:]


def along_rows(value, table):
    high, low = halves(value)
    return dot(table, jnp.concatenate([high, low, high, low], 0))


def beside(blocks):
    return jnp.concatenate(blocks, 1)


def apart(value):
    return [value[:, i : i + LANES] for i in range(0, value.shape[1], LANES)]


def pair_kernel(has_acc, pieces, n_grp, n_orb, flags_ref, t_ref, *refs):
    a_refs, b_refs, refs = refs[:HALVES], refs[HALVES : 2 * HALVES], refs[2 * HALVES :]
    if has_acc:
        acc_ref, refs = refs[0], refs[1:]
    z_ref, x_ref, yf_ref, yi_ref, out_ref, s_ref, s2_ref = refs
    first = lax.broadcasted_iota(jnp.int32, (1, LANES), 1) < NGRID
    rows = SLAB * CHUNK
    scale_b = flags_ref[0]

    for c in range(HALVES):
        t = t_ref[c * rows : (c + 1) * rows, :]
        pa = t * a_refs[c][...]
        pb = t * (b_refs[c][...] * scale_b)
        even = jnp.where(first, pa, pltpu.roll(pb, NGRID, 1)).reshape(CHUNK, SLAB, LANES)
        odd = jnp.where(first, pltpu.roll(pa, NGRID, 1), pb).reshape(CHUNK, SLAB, LANES)
        v = jnp.concatenate([even, odd], 1).reshape(CHUNK * NGRID, LANES)
        v = along_lanes(v, z_ref[...]).reshape(CHUNK, NGRID, LANES)
        v = along_rows(beside([v[i] for i in range(CHUNK)]), yf_ref[...])
        for i, block in enumerate(apart(v)):
            s_ref[(c * CHUNK + i) * NGRID : (c * CHUNK + i + 1) * NGRID, :] = block

    def squared(k):
        wave = jnp.minimum(k, NGRID - k).astype(f32) * (2.0 * np.pi / BOX_LENGTH)
        return wave * wave

    cube = (NGRID, LANES)
    base = (
        squared(lax.broadcasted_iota(jnp.int32, cube, 0))
        + squared(lax.broadcasted_iota(jnp.int32, cube, 1) % NGRID)
        + SCREEN_SQ
    )
    for c in range(HALVES):
        v = beside([s_ref[pl.ds(c * CHUNK + i, NGRID, stride=NGRID), :] for i in range(CHUNK)])
        v = along_rows(v, x_ref[...])
        kernel = []
        for i in range(CHUNK):
            y = c * CHUNK + i
            wave = min(y, NGRID - y) * (2.0 * np.pi / BOX_LENGTH)
            kernel.append((4.0 * np.pi / CELLS) / (base + wave * wave))
        v = along_rows(v * beside(kernel), x_ref[...])
        for i, block in enumerate(apart(v)):
            s2_ref[(c * CHUNK + i) * NGRID : (c * CHUNK + i + 1) * NGRID, :] = block

    for c in range(HALVES):
        v = beside([s2_ref[pl.ds(c * CHUNK + i, NGRID, stride=NGRID), :] for i in range(CHUNK)])
        v = jnp.concatenate(apart(along_rows(v, yi_ref[...])), 0)
        v = along_lanes(v, z_ref[...]).reshape(CHUNK, NGRID, LANES)
        even = v[:, :SLAB].reshape(rows, LANES)
        odd = v[:, SLAB:].reshape(rows, LANES)
        sa = jnp.where(first, even, pltpu.roll(odd, NGRID, 1))
        sb = jnp.where(first, pltpu.roll(even, NGRID, 1), odd)
        added = -(a_refs[c][...] * sa + (b_refs[c][...] * scale_b) * sb)
        if has_acc:
            added = acc_ref[c * rows : (c + 1) * rows, :] + added
        if pieces:
            part = ROWS // (n_grp * n_orb)
            count = n_orb // HALVES
            cut = added.reshape(count, n_grp, part, LANES)
            for g in range(n_grp):
                start = (g * n_orb + c * count) * part
                out_ref[start : start + count * part, :] = cut[:, g].reshape(count * part, LANES)
        else:
            out_ref[c * rows : (c + 1) * rows, :] = added


def pair_step(flag, target, first, second, acc, cut, n_grp, n_orb):
    args = [target, *first, *second] + ([] if acc is None else [acc])
    args += [jnp.asarray(table) for table in tables()]
    return pl.pallas_call(
        functools.partial(pair_kernel, acc is not None, cut, n_grp, n_orb),
        out_shape=jax.ShapeDtypeStruct((ROWS, LANES), f32),
        in_specs=[SMEM] + [VMEM] * len(args),
        out_specs=VMEM,
        scratch_shapes=[pltpu.VMEM((NGRID * NGRID, LANES), f32)] * 2,
        compiler_params=pltpu.CompilerParams(vmem_limit_bytes=40 << 20),
        cost_estimate=pl.CostEstimate(flops=8 * 10**9, bytes_accessed=5 << 20, transcendentals=0),
    )(flag.reshape(1), *args)


def strided(ref, r, count, step):
    return ref[pl.ds(r, count, stride=step), :]


def gram_kernel(n, part, x_ref, t_ref, v_ref, out_ref):
    x = beside([strided(x_ref, r, n, part) for r in range(part)])
    t = beside([strided(t_ref, r, n, part) for r in range(part)])
    v = beside([v_ref[r : r + 1, :] for r in range(part)])
    xh, xl = halves(x)
    th, tl = halves(t)
    wh, wl = halves(t * v)
    left = jnp.concatenate([xh, th, xl, tl], 0)
    right = jnp.concatenate([xh, th, wh, xl, tl, wl], 0)
    full = lax.dot_general(left, right, (((1,), (1,)), ((), ())), preferred_element_type=f32)
    full = full[: 2 * n] + full[2 * n :]
    full = full[:, : 3 * n] + full[:, 3 * n :]
    out_ref[...] = jnp.concatenate([full[:n, : 2 * n], full[n:, 2 * n :]], 1) * (1.0 / CELLS)


def gram_step(x, t, v, n, part):
    return pl.pallas_call(
        functools.partial(gram_kernel, n, part),
        out_shape=jax.ShapeDtypeStruct((n, 3 * n), f32),
        in_specs=[VMEM] * 3,
        out_specs=VMEM,
        compiler_params=pltpu.CompilerParams(vmem_limit_bytes=32 << 20),
        cost_estimate=pl.CostEstimate(flops=10**9, bytes_accessed=2 << 20, transcendentals=0),
    )(x, t, v)


def exact(left, right, dims):
    return lax.dot_general(
        left, right, (dims, ((), ())), precision=lax.Precision.HIGHEST, preferred_element_type=f32
    )


def update_kernel(n, part, out_rows, place_ref, g_ref, x_ref, t_ref, xo_ref, to_ref, v_ref, out_ref, m_ref, r_ref):
    group = place_ref[0]
    ids = lax.broadcasted_iota(jnp.int32, (n, 1), 0)
    columns = lax.broadcasted_iota(jnp.int32, (1, 3 * n), 1)
    eye = (lax.broadcasted_iota(jnp.int32, (n, n), 0) == lax.broadcasted_iota(jnp.int32, (n, n), 1)).astype(f32)
    work = jnp.concatenate([g_ref[:, : 2 * n], eye], 1)

    def eliminate(k, work):
        row = jnp.sum(jnp.where(ids == k, work, 0.0), axis=0, keepdims=True)
        pivot = jnp.sum(jnp.where(columns == k, row, 0.0), axis=1, keepdims=True)
        column = jnp.sum(jnp.where(columns == k, work, 0.0), axis=1, keepdims=True)
        root = lax.rsqrt(pivot)
        row = row * root
        lower = work - jnp.where(ids > k, column * root, 0.0) * row
        return jnp.where(ids == k, row, lower)

    work = lax.fori_loop(0, n, eliminate, work)
    pt = work[:, n : 2 * n]
    m_ref[...] = exact(pt, work[:, 2 * n :], ((0,), (0,)))
    r_ref[...] = g_ref[:, 2 * n :] - exact(pt, pt, ((0,), (0,)))
    start = pl.multiple_of(group * out_rows, 8)
    mix = jnp.concatenate([m_ref[pl.ds(start, out_rows), :], r_ref[pl.ds(start, out_rows), :]], 1) * STEP_SIZE
    high, low = halves(mix)
    mix = jnp.concatenate([jnp.concatenate([high, high], 1), jnp.concatenate([low, low], 1)], 0)

    def half(xs, ts, where):
        x = beside([strided(xs, r, n, part) for r in range(part)])
        t = beside([strided(ts, r, n, part) for r in range(part)])
        own = beside([ts[pl.ds(start * part + r, out_rows, stride=part), :] for r in range(part)])
        v = v_ref[pl.ds(pl.multiple_of(where * part, part), part), :]
        v = beside([v[r : r + 1] for r in range(part)])
        xh, xl = halves(x)
        th, tl = halves(t)
        both = dot(mix, jnp.concatenate([xh, th, xl, tl], 0))
        both = both[:out_rows] + both[out_rows:]
        width = part * LANES
        out_ref[:, pl.ds(pl.multiple_of(where * width, width), width)] = own * (1.0 - STEP_SIZE * v) + both

    half(x_ref, t_ref, group)
    half(xo_ref, to_ref, 1 - group)


def update_step(place, g, x, t, xo, to, v, n, part, out_rows):
    return pl.pallas_call(
        functools.partial(update_kernel, n, part, out_rows),
        out_shape=jax.ShapeDtypeStruct((out_rows, 2 * part * LANES), f32),
        in_specs=[SMEM] + [VMEM] * 6,
        out_specs=VMEM,
        scratch_shapes=[pltpu.VMEM((n, n), f32)] * 2,
        compiler_params=pltpu.CompilerParams(vmem_limit_bytes=32 << 20),
        cost_estimate=pl.CostEstimate(flops=10**9, bytes_accessed=6 << 20, transcendentals=0),
    )(place.reshape(1), g, x, t, xo, to, v)


def moved(x, axes, target):
    size = 1
    for axis in axes:
        size *= lax.axis_size(axis)
    return lax.ppermute(x, axes, [(i, target(i)) for i in range(size)])


def summed_all(x, n_grp, n_orb):
    axes = ("grp", "orb")
    bits = [1, 2, n_orb] + [b for b in (1 << k for k in range(2, 30)) if b < n_orb]
    steps = [bits[:1]] + [bits[k : k + 2] for k in range(1, len(bits), 2)]
    for step in steps:
        masks = step if len(step) == 1 else [step[0], step[1], step[0] ^ step[1]]
        parts = [moved(x, axes, lambda i, m=m: i ^ m) for m in masks]
        for part in parts:
            x = x + part
    return x


def on_device(occupied, targets, potential):
    n_grp, n_orb = lax.axis_size("grp"), lax.axis_size("orb")
    n = n_grp * n_orb
    part = ROWS // n
    group, orb = lax.axis_index("grp"), lax.axis_index("orb")
    one = jnp.ones((), f32)
    crossed = (((orb >> 1) & 1) != (orb & 1)).astype(f32)

    target = targets.reshape(ROWS, LANES)
    occ = occupied.reshape(ROWS, LANES)
    own = [occ[: ROWS // 2], occ[ROWS // 2 :]]
    mate = [moved(v, ("orb",), lambda i: i ^ 1) for v in own]
    near = [moved(v, ("orb",), lambda i: i ^ 2) for v in own]
    far = [moved(v, ("orb",), lambda i: (i + (-4 if i & 2 else 4)) % n_orb) for v in near]
    near_mate = [moved(v, ("orb",), lambda i: i ^ 1) for v in near]
    far_mate = [moved(v, ("orb",), lambda i: i ^ 1) for v in far]

    def spread(value):
        return lax.all_to_all(value.reshape(n, part, LANES), ("grp", "orb"), split_axis=0, concat_axis=0).reshape(ROWS, LANES)

    def swapped(value):
        return moved(value, ("grp",), lambda i: i ^ 1)

    cut = target.reshape(n_orb, n_grp, part, LANES).transpose(1, 0, 2, 3)
    t_half = spread(cut)
    t_other = swapped(t_half)

    acc = pair_step(one, target, own, mate, None, False, n_grp, n_orb)
    acc = pair_step(crossed, target, near, near_mate, acc, False, n_grp, n_orb)
    acc = pair_step(one - crossed, target, far, far_mate, acc, True, n_grp, n_orb)
    x_half = spread(acc)
    x_other = swapped(x_half)

    v = potential.reshape(n_grp * part, LANES)
    gram = gram_step(x_half, t_half, lax.dynamic_slice_in_dim(v, group * part, part, 0), n, part)
    gram = summed_all(gram, n_grp, n_orb)
    return update_step(group, gram, x_half, t_half, x_other, t_other, v, n, part, n_orb)


def solution(mesh):
    placed = (P("orb", None), P(("grp", "orb"), None), P("orb"))
    return jax.shard_map(
        on_device, mesh=mesh, in_specs=placed, out_specs=P("grp", "orb"), check_vma=False
    )
```

profile of v0, /device:TPU:0, one launch (start us, length us, event | category | flops | bytes accessed | tf_op | source)
XLA Modules:
  0.0 157.0 jit_solution(4340747857924821713)
XLA Ops:
  0.0 0.0 copy-start
  0.0 1.4 fusion
  1.4 3.0 %collective-permute-start = (f32[1024,128]{1,0:T(8,128)S(1)}, f32[1024,128]{1,0:T(8,128)}, u32[]{:S(2)}, u32[]{:S(2)}) collective-permute-start(f32[1024,128]{1,0:T(8,128)S(1)} %bitcast.27), channel_id=1, source_target_pairs={{0,2},{1,3},{2,0},{3,1},{4,6},{5,7},{6,4},{7,5},{8,10},{9,11},{10,... | collective-permute-start | bytes 1572872 | tf_op jit(solution)/shard_map/ppermute | solution.py:257
  4.4 0.1 collective-permute-start.2
  4.4 0.0 collective-permute-start.8
  4.5 0.5 collective-permute-start.9
  5.0 0.0 copy-done
  5.0 1.1 copy.16
  6.0 0.0 copy-start.2
  6.0 0.0 copy-start.3
  6.0 0.0 copy-start.4
  6.0 0.0 copy-start.5
  6.0 6.3 %all-to-all-start.1 = ((f32[32,64,128]{2,1,0:T(8,128)}), f32[32,64,128]{2,1,0:T(8,128)S(1)}, u32[]{:S(2)}, u32[]{:S(2)}) async-start(f32[32,64,128]{2,1,0:T(8,128)} %bitcast.32), calls=%async_computation.1 | async-start | bytes 2097152 | tf_op jit(solution)/shard_map/all_to_all | solution.py:290
  12.4 6.7 %collective-permute-done.refs_0_ = f32[1024,128]{1,0:T(8,128)} collective-permute-done((f32[1024,128]{1,0:T(8,128)S(1)}, f32[1024,128]{1,0:T(8,128)}, u32[]{:S(2)}, u32[]{:S(2)}) %collective-permute-start) | collective-permute-done | bytes 524320 | tf_op jit(solution)/shard_map/ppermute | solution.py:257
  19.0 0.0 collective-permute-start.6
  19.0 1.7 %collective-permute-start.1 = (f32[1024,128]{1,0:T(8,128)}, f32[1024,128]{1,0:T(8,128)S(1)}, u32[]{:S(2)}, u32[]{:S(2)}) collective-permute-start(f32[1024,128]{1,0:T(8,128)} %collective-permute-done.refs_0_), channel_id=1, source_target_pairs={{0,4},{1,5},{2,14},{3,15},{4,8},{5,9},{6,2},{7,3},{8,12},{9,13},{1... | collective-permute-start | bytes 1572872 | tf_op jit(solution)/shard_map/ppermute | solution.py:257
  20.8 15.0 %collective-permute-done.2.refs_1_ = f32[1024,128]{1,0:T(8,128)} collective-permute-done((f32[1024,128]{1,0:T(8,128)S(1)}, f32[1024,128]{1,0:T(8,128)}, u32[]{:S(2)}, u32[]{:S(2)}) %collective-permute-start.2) | collective-permute-done | bytes 524320 | tf_op jit(solution)/shard_map/ppermute | solution.py:257
  35.8 0.0 collective-permute-start.7
  35.8 0.0 collective-permute-done.8.refs_2_
  35.8 2.9 %collective-permute-start.3 = (f32[1024,128]{1,0:T(8,128)}, f32[1024,128]{1,0:T(8,128)S(1)}, u32[]{:S(2)}, u32[]{:S(2)}) collective-permute-start(f32[1024,128]{1,0:T(8,128)} %collective-permute-done.2.refs_1_), channel_id=1, source_target_pairs={{0,4},{1,5},{2,14},{3,15},{4,8},{5,9},{6,2},{7,3},{8,12},{9,13},{1... | collective-permute-start | bytes 1572872 | tf_op jit(solution)/shard_map/ppermute | solution.py:257
  38.7 0.0 collective-permute-done.9.refs_3_
  38.7 0.0 copy-done.2
  38.7 0.0 copy-done.3
  38.7 0.0 copy-done.4
  38.7 0.0 copy-done.5
  38.7 7.4 %shard_map.145.refs_4_ = f32[2048,128]{1,0:T(8,128)S(1)} custom-call(f32[1]{0:T(128)} %constant.12.clone.1.flags_ref, f32[2048,128]{1,0:T(8,128)S(1)} %bitcast.21, f32[1024,128]{1,0:T(8,128)S(1)} %bitcast.29, f32[1024,128]{1,0:T(8,128)S(1)} %bitcast.26, f32[1024,128]{1,0:T(8,128)} %collective-permute-done.8.refs_2_, ...), custom_call_target="tpu_custom_call" | custom-call | flops 8000000000 | bytes 5242880 | tf_op jit(solution)/shard_map/pallas_call | solution.py:152
  46.1 0.0 collective-permute-done.1.refs_0_
  46.1 0.3 collective-permute-start.4
  46.4 10.2 %collective-permute-done.3.refs_1_ = f32[1024,128]{1,0:T(8,128)S(1)} collective-permute-done((f32[1024,128]{1,0:T(8,128)}, f32[1024,128]{1,0:T(8,128)S(1)}, u32[]{:S(2)}, u32[]{:S(2)}) %collective-permute-start.3) | collective-permute-done | bytes 524320 | tf_op jit(solution)/shard_map/ppermute | solution.py:257
  56.6 0.0 collective-permute-start.5
  56.6 0.0 collective-permute-done.6.refs_2_
  56.6 0.0 collective-permute-done.7.refs_3_
  56.6 7.4 %shard_map.146.refs_4_ = f32[2048,128]{1,0:T(8,128)S(1)} custom-call(f32[1]{0:T(128)} %bitcast.5.flags_ref, f32[2048,128]{1,0:T(8,128)S(1)} %bitcast.22, f32[1024,128]{1,0:T(8,128)} %collective-permute-done.refs_0_, f32[1024,128]{1,0:T(8,128)} %collective-permute-done.2.refs_1_, f32[1024,128]{1,0:T(8,128)S(1)} %collective-permute-done.6.refs_2_, ...), custom_call_target="tpu_custom_call" | custom-call | flops 8000000000 | bytes 5242880 | tf_op jit(solution)/shard_map/pallas_call | solution.py:152
  64.0 0.0 collective-permute-done.4.refs_2_
  64.0 0.0 collective-permute-done.5.refs_3_
  64.0 7.3 %shard_map.147 = f32[2048,128]{1,0:T(8,128)} custom-call(f32[1]{0:T(128)} %bitcast.1.flags_ref, f32[2048,128]{1,0:T(8,128)S(1)} %bitcast.23, f32[1024,128]{1,0:T(8,128)S(1)} %collective-permute-done.1.refs_0_, f32[1024,128]{1,0:T(8,128)S(1)} %collective-permute-done.3.refs_1_, f32[1024,128]{1,0:T(8,128)S(1)} %collective-permute-done.4.refs_2_, ...), custom_call_target="tpu_custom_call" | custom-call | flops 8000000000 | bytes 5242880 | tf_op jit(solution)/shard_map/pallas_call | solution.py:152
  71.4 0.0 all-to-all-done.1
  71.4 0.0 copy-start.1
  71.4 7.4 %all-to-all-start = ((f32[32,64,128]{2,1,0:T(8,128)}), f32[32,64,128]{2,1,0:T(8,128)S(1)}, u32[]{:S(2)}, u32[]{:S(2)}) async-start(f32[32,64,128]{2,1,0:T(8,128)} %bitcast.6), calls=%async_computation | async-start | bytes 2097152 | tf_op jit(solution)/shard_map/all_to_all | solution.py:290
  78.8 1.8 %collective-permute-start.18 = (f32[2048,128]{1,0:T(8,128)S(1)}, f32[2048,128]{1,0:T(8,128)S(1)}, u32[]{:S(2)}, u32[]{:S(2)}) collective-permute-start(f32[2048,128]{1,0:T(8,128)S(1)} %bitcast.14), channel_id=1, source_target_pairs={{0,16},{16,0},{1,17},{17,1},{2,18},{18,2},{3,19},{19,3},{4,20},{20... | collective-permute-start | bytes 3145736 | tf_op jit(solution)/shard_map/ppermute | solution.py:257
  80.6 25.5 %all-to-all-done = f32[32,64,128]{2,1,0:T(8,128)S(1)} async-done(((f32[32,64,128]{2,1,0:T(8,128)}), f32[32,64,128]{2,1,0:T(8,128)S(1)}, u32[]{:S(2)}, u32[]{:S(2)}) %all-to-all-start) | async-done | bytes 1048608 | tf_op jit(solution)/shard_map/all_to_all | solution.py:290
  106.1 0.9 collective-permute-start.17
  106.9 0.0 copy-done.1
  106.9 1.8 %shard_map.148 = f32[32,96]{1,0:T(8,128)S(1)} custom-call(f32[2048,128]{1,0:T(8,128)S(1)} %bitcast.18, f32[2048,128]{1,0:T(8,128)S(1)} %bitcast.15, f32[64,128]{1,0:T(8,128)S(1)} %constant_dynamic-slice_fusion.v_ref), custom_call_target="tpu_custom_call" | custom-call | flops 1000000000 | bytes 2097152 | tf_op jit(solution)/shard_map/pallas_call | solution.py:183
  108.8 0.1 collective-permute-start.10
  108.8 1.2 collective-permute-done.10
  110.0 1.1 collective-permute-start.11
  111.1 1.5 collective-permute-start.12
  112.6 0.9 collective-permute-start.13
  113.5 0.2 collective-permute-done.11
  113.7 24.8 %collective-permute-done.12 = f32[32,96]{1,0:T(8,128)S(1)} collective-permute-done((f32[32,96]{1,0:T(8,128)S(1)}, f32[32,96]{1,0:T(8,128)S(1)}, u32[]{:S(2)}, u32[]{:S(2)}) %collective-permute-start.12) | collective-permute-done | bytes 12320 | tf_op jit(solution)/shard_map/ppermute | solution.py:257
  138.5 0.0 collective-permute-done.13
  138.5 1.5 collective-permute-start.14
  140.1 2.4 %collective-permute-start.15 = (f32[32,96]{1,0:T(8,128)S(1)}, f32[32,96]{1,0:T(8,128)S(1)}, u32[]{:S(2)}, u32[]{:S(2)}) collective-permute-start(f32[32,96]{1,0:T(8,128)S(1)} %add_add_fusion.1), channel_id=1, source_target_pairs={{0,8},{1,9},{2,10},{3,11},{4,12},{5,13},{6,14},{7,15},{8,0},{9,1},... | collective-permute-start | bytes 36872 | tf_op jit(solution)/shard_map/ppermute | solution.py:257
  142.5 0.5 collective-permute-start.16
  143.0 0.0 collective-permute-done.14
  143.0 1.9 %collective-permute-done.15 = f32[32,96]{1,0:T(8,128)S(1)} collective-permute-done((f32[32,96]{1,0:T(8,128)S(1)}, f32[32,96]{1,0:T(8,128)S(1)}, u32[]{:S(2)}, u32[]{:S(2)}) %collective-permute-start.15) | collective-permute-done | bytes 12320 | tf_op jit(solution)/shard_map/ppermute | solution.py:257
  144.9 3.2 %collective-permute-done.16 = f32[32,96]{1,0:T(8,128)S(1)} collective-permute-done((f32[32,96]{1,0:T(8,128)S(1)}, f32[32,96]{1,0:T(8,128)S(1)}, u32[]{:S(2)}, u32[]{:S(2)}) %collective-permute-start.16) | collective-permute-done | bytes 12320 | tf_op jit(solution)/shard_map/ppermute | solution.py:257
  148.1 0.0 collective-permute-done.18.to_ref
  148.1 0.0 collective-permute-done.17.xo_ref
  148.1 8.9 %shard_map.149 = f32[16,16384]{1,0:T(8,128)} custom-call(s32[1]{0:T(128)} %bitcast.place_ref, f32[32,96]{1,0:T(8,128)S(1)} %add_add_fusion.g_ref, f32[2048,128]{1,0:T(8,128)S(1)} %bitcast.19, f32[2048,128]{1,0:T(8,128)S(1)} %bitcast.16, f32[2048,128]{1,0:T(8,128)} %collective-permute-done.17.xo_ref, f32[2048,128]{1,0:T(8,128)S(1)} %collective-permute-done.18.to_ref, ...), custom_call_target="tpu_custom_call" | custom-call | flops 1000000000 | bytes 6291456 | tf_op jit(solution)/shard_map/pallas_call | solution.py:242
  (4 shorter events, 0.0 us)
Async XLA Ops:
  0.0 5.0 %copy-start = (f32[1,262144]{1,0:T(1,128)S(1)}, f32[1,262144]{1,0:T(1,128)}, u32[]{:S(2)}) copy-start(f32[1,262144]{1,0:T(1,128)} %param.16) | copy-start | bytes 3145732
  1.4 17.7 %collective-permute-start = (f32[1024,128]{1,0:T(8,128)S(1)}, f32[1024,128]{1,0:T(8,128)}, u32[]{:S(2)}, u32[]{:S(2)}) collective-permute-start(f32[1024,128]{1,0:T(8,128)S(1)} %bitcast.27), channel_id=1, source_target_pairs={{0,2},{1,3},{2,0},{3,1},{4,6},{5,7},{6,4},{7,5},{8,10},{9,11},{10,... | collective-permute-start | bytes 1572872 | tf_op jit(solution)/shard_map/ppermute | solution.py:257
  4.4 31.4 %collective-permute-start.2 = (f32[1024,128]{1,0:T(8,128)S(1)}, f32[1024,128]{1,0:T(8,128)}, u32[]{:S(2)}, u32[]{:S(2)}) collective-permute-start(f32[1024,128]{1,0:T(8,128)S(1)} %bitcast.24), channel_id=1, source_target_pairs={{0,2},{1,3},{2,0},{3,1},{4,6},{5,7},{6,4},{7,5},{8,10},{9,11},{10,... | collective-permute-start | bytes 1572872 | tf_op jit(solution)/shard_map/ppermute | solution.py:257
  4.4 31.3 %collective-permute-start.8 = (f32[1024,128]{1,0:T(8,128)S(1)}, f32[1024,128]{1,0:T(8,128)}, u32[]{:S(2)}, u32[]{:S(2)}) collective-permute-start(f32[1024,128]{1,0:T(8,128)S(1)} %bitcast.28), channel_id=1, source_target_pairs={{0,1},{1,0},{2,3},{3,2},{4,5},{5,4},{6,7},{7,6},{8,9},{9,8},{10,11... | collective-permute-start | bytes 1572872 | tf_op jit(solution)/shard_map/ppermute | solution.py:257
  4.5 34.2 %collective-permute-start.9 = (f32[1024,128]{1,0:T(8,128)S(1)}, f32[1024,128]{1,0:T(8,128)}, u32[]{:S(2)}, u32[]{:S(2)}) collective-permute-start(f32[1024,128]{1,0:T(8,128)S(1)} %bitcast.25), channel_id=1, source_target_pairs={{0,1},{1,0},{2,3},{3,2},{4,5},{5,4},{6,7},{7,6},{8,9},{9,8},{10,11... | collective-permute-start | bytes 1572872 | tf_op jit(solution)/shard_map/ppermute | solution.py:257
  6.0 32.7 %copy-start.2 = (bf16[256,256]{1,0:T(8,128)(2,1)S(1)}, bf16[256,256]{1,0:T(8,128)(2,1)}, u32[]{:S(2)}) copy-start(bf16[256,256]{1,0:T(8,128)(2,1)} %constant.29.clone.refs_4_.refs_5_) | copy-start | bytes 393220
  6.0 32.7 %copy-start.3 = (bf16[64,256]{1,0:T(8,128)(2,1)S(1)}, bf16[64,256]{1,0:T(8,128)(2,1)}, u32[]{:S(2)}) copy-start(bf16[64,256]{1,0:T(8,128)(2,1)} %constant.30.clone.refs_5_.refs_6_) | copy-start | bytes 98308
  6.0 32.7 %copy-start.4 = (bf16[64,256]{1,0:T(8,128)(2,1)S(1)}, bf16[64,256]{1,0:T(8,128)(2,1)}, u32[]{:S(2)}) copy-start(bf16[64,256]{1,0:T(8,128)(2,1)} %constant.31.clone.refs_6_.refs_7_) | copy-start | bytes 98308
  6.0 32.7 %copy-start.5 = (bf16[64,256]{1,0:T(8,128)(2,1)S(1)}, bf16[64,256]{1,0:T(8,128)(2,1)}, u32[]{:S(2)}) copy-start(bf16[64,256]{1,0:T(8,128)(2,1)} %constant.32.clone.refs_7_.refs_8_) | copy-start | bytes 98308
  6.0 65.3 %all-to-all-start.1 = ((f32[32,64,128]{2,1,0:T(8,128)}), f32[32,64,128]{2,1,0:T(8,128)S(1)}, u32[]{:S(2)}, u32[]{:S(2)}) async-start(f32[32,64,128]{2,1,0:T(8,128)} %bitcast.32), calls=%async_computation.1 | async-start | bytes 2097152 | tf_op jit(solution)/shard_map/all_to_all | solution.py:290
  19.0 37.5 %collective-permute-start.6 = (f32[1024,128]{1,0:T(8,128)}, f32[1024,128]{1,0:T(8,128)S(1)}, u32[]{:S(2)}, u32[]{:S(2)}) collective-permute-start(f32[1024,128]{1,0:T(8,128)} %collective-permute-done.refs_0_), channel_id=1, source_target_pairs={{0,1},{1,0},{2,3},{3,2},{4,5},{5,4},{6,7},{7,6},{8,9},{9,8},{10,11... | collective-permute-start | bytes 1572872 | tf_op jit(solution)/shard_map/ppermute | solution.py:257
  19.0 27.1 %collective-permute-start.1 = (f32[1024,128]{1,0:T(8,128)}, f32[1024,128]{1,0:T(8,128)S(1)}, u32[]{:S(2)}, u32[]{:S(2)}) collective-permute-start(f32[1024,128]{1,0:T(8,128)} %collective-permute-done.refs_0_), channel_id=1, source_target_pairs={{0,4},{1,5},{2,14},{3,15},{4,8},{5,9},{6,2},{7,3},{8,12},{9,13},{1... | collective-permute-start | bytes 1572872 | tf_op jit(solution)/shard_map/ppermute | solution.py:257
  35.8 20.8 %collective-permute-start.7 = (f32[1024,128]{1,0:T(8,128)}, f32[1024,128]{1,0:T(8,128)S(1)}, u32[]{:S(2)}, u32[]{:S(2)}) collective-permute-start(f32[1024,128]{1,0:T(8,128)} %collective-permute-done.2.refs_1_), channel_id=1, source_target_pairs={{0,1},{1,0},{2,3},{3,2},{4,5},{5,4},{6,7},{7,6},{8,9},{9,8},{10,11... | collective-permute-start | bytes 1572872 | tf_op jit(solution)/shard_map/ppermute | solution.py:257
  35.8 20.8 %collective-permute-start.3 = (f32[1024,128]{1,0:T(8,128)}, f32[1024,128]{1,0:T(8,128)S(1)}, u32[]{:S(2)}, u32[]{:S(2)}) collective-permute-start(f32[1024,128]{1,0:T(8,128)} %collective-permute-done.2.refs_1_), channel_id=1, source_target_pairs={{0,4},{1,5},{2,14},{3,15},{4,8},{5,9},{6,2},{7,3},{8,12},{9,13},{1... | collective-permute-start | bytes 1572872 | tf_op jit(solution)/shard_map/ppermute | solution.py:257
  46.1 17.9 %collective-permute-start.4 = (f32[1024,128]{1,0:T(8,128)S(1)}, f32[1024,128]{1,0:T(8,128)S(1)}, u32[]{:S(2)}, u32[]{:S(2)}) collective-permute-start(f32[1024,128]{1,0:T(8,128)S(1)} %collective-permute-done.1.refs_0_), channel_id=1, source_target_pairs={{0,1},{1,0},{2,3},{3,2},{4,5},{5,4},{6,7},{7,6},{8,9},{9,8},{10,11... | collective-permute-start | bytes 1572872 | tf_op jit(solution)/shard_map/ppermute | solution.py:257
  56.6 7.4 %collective-permute-start.5 = (f32[1024,128]{1,0:T(8,128)S(1)}, f32[1024,128]{1,0:T(8,128)S(1)}, u32[]{:S(2)}, u32[]{:S(2)}) collective-permute-start(f32[1024,128]{1,0:T(8,128)S(1)} %collective-permute-done.3.refs_1_), channel_id=1, source_target_pairs={{0,1},{1,0},{2,3},{3,2},{4,5},{5,4},{6,7},{7,6},{8,9},{9,8},{10,11... | collective-permute-start | bytes 1572872 | tf_op jit(solution)/shard_map/ppermute | solution.py:257
  71.4 35.6 %copy-start.1 = (f32[16384]{0:T(1024)S(1)}, f32[16384]{0:T(1024)}, u32[]{:S(2)}) copy-start(f32[16384]{0:T(1024)} %param.17) | copy-start | bytes 196612
  71.4 34.7 %all-to-all-start = ((f32[32,64,128]{2,1,0:T(8,128)}), f32[32,64,128]{2,1,0:T(8,128)S(1)}, u32[]{:S(2)}, u32[]{:S(2)}) async-start(f32[32,64,128]{2,1,0:T(8,128)} %bitcast.6), calls=%async_computation | async-start | bytes 2097152 | tf_op jit(solution)/shard_map/all_to_all | solution.py:290
  78.8 69.3 %collective-permute-start.18 = (f32[2048,128]{1,0:T(8,128)S(1)}, f32[2048,128]{1,0:T(8,128)S(1)}, u32[]{:S(2)}, u32[]{:S(2)}) collective-permute-start(f32[2048,128]{1,0:T(8,128)S(1)} %bitcast.14), channel_id=1, source_target_pairs={{0,16},{16,0},{1,17},{17,1},{2,18},{18,2},{3,19},{19,3},{4,20},{20... | collective-permute-start | bytes 3145736 | tf_op jit(solution)/shard_map/ppermute | solution.py:257
  106.1 42.0 %collective-permute-start.17 = (f32[2048,128]{1,0:T(8,128)S(1)}, f32[2048,128]{1,0:T(8,128)}, u32[]{:S(2)}, u32[]{:S(2)}) collective-permute-start(f32[2048,128]{1,0:T(8,128)S(1)} %bitcast.17), channel_id=1, source_target_pairs={{0,16},{16,0},{1,17},{17,1},{2,18},{18,2},{3,19},{19,3},{4,20},{20... | collective-permute-start | bytes 3145736 | tf_op jit(solution)/shard_map/ppermute | solution.py:257
  108.8 1.2 collective-permute-start.10
  110.0 3.7 %collective-permute-start.11 = (f32[32,96]{1,0:T(8,128)S(1)}, f32[32,96]{1,0:T(8,128)S(1)}, u32[]{:S(2)}, u32[]{:S(2)}) collective-permute-start(f32[32,96]{1,0:T(8,128)S(1)} %add.25), channel_id=1, source_target_pairs={{0,2},{1,3},{2,0},{3,1},{4,6},{5,7},{6,4},{7,5},{8,10},{9,11},{10,... | collective-permute-start | bytes 36872 | tf_op jit(solution)/shard_map/ppermute | solution.py:257
  111.1 27.4 %collective-permute-start.12 = (f32[32,96]{1,0:T(8,128)S(1)}, f32[32,96]{1,0:T(8,128)S(1)}, u32[]{:S(2)}, u32[]{:S(2)}) collective-permute-start(f32[32,96]{1,0:T(8,128)S(1)} %add.25), channel_id=1, source_target_pairs={{0,16},{1,17},{2,18},{3,19},{4,20},{5,21},{6,22},{7,23},{8,24},{9,... | collective-permute-start | bytes 36872 | tf_op jit(solution)/shard_map/ppermute | solution.py:257
  112.6 25.9 %collective-permute-start.13 = (f32[32,96]{1,0:T(8,128)S(1)}, f32[32,96]{1,0:T(8,128)S(1)}, u32[]{:S(2)}, u32[]{:S(2)}) collective-permute-start(f32[32,96]{1,0:T(8,128)S(1)} %add.25), channel_id=1, source_target_pairs={{0,18},{1,19},{2,16},{3,17},{4,22},{5,23},{6,20},{7,21},{8,26},{9,... | collective-permute-start | bytes 36872 | tf_op jit(solution)/shard_map/ppermute | solution.py:257
  138.5 4.5 %collective-permute-start.14 = (f32[32,96]{1,0:T(8,128)S(1)}, f32[32,96]{1,0:T(8,128)S(1)}, u32[]{:S(2)}, u32[]{:S(2)}) collective-permute-start(f32[32,96]{1,0:T(8,128)S(1)} %add_add_fusion.1), channel_id=1, source_target_pairs={{0,4},{1,5},{2,6},{3,7},{4,0},{5,1},{6,2},{7,3},{8,12},{9,13},{10,... | collective-permute-start | bytes 36872 | tf_op jit(solution)/shard_map/ppermute | solution.py:257
  140.1 4.8 %collective-permute-start.15 = (f32[32,96]{1,0:T(8,128)S(1)}, f32[32,96]{1,0:T(8,128)S(1)}, u32[]{:S(2)}, u32[]{:S(2)}) collective-permute-start(f32[32,96]{1,0:T(8,128)S(1)} %add_add_fusion.1), channel_id=1, source_target_pairs={{0,8},{1,9},{2,10},{3,11},{4,12},{5,13},{6,14},{7,15},{8,0},{9,1},... | collective-permute-start | bytes 36872 | tf_op jit(solution)/shard_map/ppermute | solution.py:257
  142.5 5.5 %collective-permute-start.16 = (f32[32,96]{1,0:T(8,128)S(1)}, f32[32,96]{1,0:T(8,128)S(1)}, u32[]{:S(2)}, u32[]{:S(2)}) collective-permute-start(f32[32,96]{1,0:T(8,128)S(1)} %add_add_fusion.1), channel_id=1, source_target_pairs={{0,12},{1,13},{2,14},{3,15},{4,8},{5,9},{6,10},{7,11},{8,4},{9,5},... | collective-permute-start | bytes 36872 | tf_op jit(solution)/shard_map/ppermute | solution.py:257
where the time goes:
time: 157 us
  waiting for transfers between devices  88.6 us (56%)
  starting transfers between devices  32.9 us (21%)
  Pallas kernels  32.9 us (21%)
  local copies, waits for them, and re-layouts  2.45 us (2%)
    ppermute x19, waiting for transfers between devices, moved(): return lax.ppermute(x, axes, [(i, target(i)) for i in range(size)])  63.1 us
    all_to_all x2, waiting for transfers between devices, spread(): lax.all_to_all(value.reshape(n, part, LANES), ('grp', 'orb'), split_axis=...  25.5 us
    pallas_call x3, Pallas kernels, pair_step(): pl.pallas_call(functools.partial(pair_kernel, acc is not None, cut, n_grp...  22.1 us
    ppermute x19, starting transfers between devices, moved(): return lax.ppermute(x, axes, [(i, target(i)) for i in range(size)])  19.2 us
    all_to_all x2, starting transfers between devices, spread(): lax.all_to_all(value.reshape(n, part, LANES), ('grp', 'orb'), split_axis=...  13.7 us
    pallas_call x1, Pallas kernels, update_step(): pl.pallas_call(functools.partial(update_kernel, n, part, out_rows), out_s...  8.93 us
  transfers between devices with their start and end apart: 21, of which 9 were waited for; matrix products, arithmetic and copies ran while one was open for 1% of the time, Pallas kernels for 15%

commit v1 on v0

v1 whole, which is shorter than its diff:
```python
import functools

import jax
import jax.numpy as jnp
import ml_dtypes
import numpy as np
from jax import lax
from jax.experimental import pallas as pl
from jax.experimental.pallas import tpu as pltpu
from jax.sharding import PartitionSpec as P

NGRID = 64
CELLS = 262144
LANES = 128
ROWS = CELLS // LANES
SLAB = NGRID * NGRID // LANES
CHUNK = 64
LOOPS = NGRID // CHUNK

SCREEN_SQ = 0.04
BOX_LENGTH = 20.0
STEP_SIZE = 0.3

bf16 = jnp.bfloat16
f32 = jnp.float32
VMEM = pl.BlockSpec(memory_space=pltpu.VMEM)
SMEM = pl.BlockSpec(memory_space=pltpu.SMEM)


def tables():
    index = np.arange(NGRID)
    angles = 2.0 * np.pi * (index[:, None] * index[None, :] % NGRID) / NGRID
    table = np.cos(angles) + np.sin(angles)
    high = table.astype(ml_dtypes.bfloat16)
    low = (table - high.astype(np.float64)).astype(ml_dtypes.bfloat16)

    def twice(block):
        both = np.zeros((2 * NGRID, 2 * NGRID), ml_dtypes.bfloat16)
        both[:NGRID, :NGRID] = block
        both[NGRID:, NGRID:] = block
        return both

    def stacked(high, low):
        return np.concatenate([high, high, low, low], 1)

    row = np.concatenate([twice(high), twice(low)], 1)
    along_z = np.concatenate([row, row], 0)
    order = np.concatenate([index[0::2], index[1::2]])
    return (
        along_z,
        stacked(high, low),
        stacked(high[:, order], low[:, order]),
        stacked(high[order], low[order]),
    )


def halves(value):
    high = value.astype(bf16)
    return high, (value - high.astype(f32)).astype(bf16)


def dot(left, right):
    return jnp.dot(left, right, preferred_element_type=f32)


def along_lanes(value, table):
    out = dot(jnp.concatenate(halves(value), 1), table)
    return out[:, :LANES] + out[:, LANES:]


def along_rows(value, table):
    high, low = halves(value)
    return dot(table, jnp.concatenate([high, low, high, low], 0))


def beside(blocks):
    return jnp.concatenate(blocks, 1)


def apart(value):
    return [value[:, i : i + LANES] for i in range(0, value.shape[1], LANES)]


def pair_kernel(counts, has_acc, pieces, n_grp, n_orb, flags_ref, group_ref, t_ref, *refs):
    a_refs, b_refs, refs = refs[: counts[0]], refs[counts[0] : sum(counts)], refs[sum(counts) :]
    if has_acc:
        acc_ref, refs = refs[0], refs[1:]
    z_ref, x_ref, yf_ref, yi_ref, out_ref, s_ref, s2_ref = refs
    first = lax.broadcasted_iota(jnp.int32, (1, LANES), 1) < NGRID
    rows = SLAB * CHUNK
    scale_b = flags_ref[0]

    leading = group_ref[0] == 0

    def chosen(pieces):
        if len(pieces) == 1:
            return pieces[0][...]
        own, other = pieces[0][...], pieces[1][...]
        return jnp.concatenate([jnp.where(leading, own, other), jnp.where(leading, other, own)], 0)

    for c in range(LOOPS):
        t = t_ref[c * rows : (c + 1) * rows, :]
        pa = t * chosen(a_refs)
        pb = t * (chosen(b_refs) * scale_b)
        even = jnp.where(first, pa, pltpu.roll(pb, NGRID, 1)).reshape(CHUNK, SLAB, LANES)
        odd = jnp.where(first, pltpu.roll(pa, NGRID, 1), pb).reshape(CHUNK, SLAB, LANES)
        v = jnp.concatenate([even, odd], 1).reshape(CHUNK * NGRID, LANES)
        v = along_lanes(v, z_ref[...]).reshape(CHUNK, NGRID, LANES)
        v = along_rows(beside([v[i] for i in range(CHUNK)]), yf_ref[...])
        for i, block in enumerate(apart(v)):
            s_ref[(c * CHUNK + i) * NGRID : (c * CHUNK + i + 1) * NGRID, :] = block

    def squared(k):
        wave = jnp.minimum(k, NGRID - k).astype(f32) * (2.0 * np.pi / BOX_LENGTH)
        return wave * wave

    cube = (NGRID, LANES)
    base = (
        squared(lax.broadcasted_iota(jnp.int32, cube, 0))
        + squared(lax.broadcasted_iota(jnp.int32, cube, 1) % NGRID)
        + SCREEN_SQ
    )
    for c in range(LOOPS):
        v = beside([s_ref[pl.ds(c * CHUNK + i, NGRID, stride=NGRID), :] for i in range(CHUNK)])
        v = along_rows(v, x_ref[...])
        kernel = []
        for i in range(CHUNK):
            y = c * CHUNK + i
            wave = min(y, NGRID - y) * (2.0 * np.pi / BOX_LENGTH)
            kernel.append((4.0 * np.pi / CELLS) / (base + wave * wave))
        v = along_rows(v * beside(kernel), x_ref[...])
        for i, block in enumerate(apart(v)):
            s2_ref[(c * CHUNK + i) * NGRID : (c * CHUNK + i + 1) * NGRID, :] = block

    for c in range(LOOPS):
        v = beside([s2_ref[pl.ds(c * CHUNK + i, NGRID, stride=NGRID), :] for i in range(CHUNK)])
        v = jnp.concatenate(apart(along_rows(v, yi_ref[...])), 0)
        v = along_lanes(v, z_ref[...]).reshape(CHUNK, NGRID, LANES)
        even = v[:, :SLAB].reshape(rows, LANES)
        odd = v[:, SLAB:].reshape(rows, LANES)
        sa = jnp.where(first, even, pltpu.roll(odd, NGRID, 1))
        sb = jnp.where(first, pltpu.roll(even, NGRID, 1), odd)
        added = -(chosen(a_refs) * sa + (chosen(b_refs) * scale_b) * sb)
        if has_acc:
            added = acc_ref[c * rows : (c + 1) * rows, :] + added
        if pieces:
            part = ROWS // (n_grp * n_orb)
            count = n_orb // LOOPS
            cut = added.reshape(count, n_grp, part, LANES)
            for g in range(n_grp):
                start = (g * n_orb + c * count) * part
                out_ref[start : start + count * part, :] = cut[:, g].reshape(count * part, LANES)
        else:
            out_ref[c * rows : (c + 1) * rows, :] = added


def pair_step(flag, group, target, first, second, acc, cut, n_grp, n_orb):
    args = [target, *first, *second] + ([] if acc is None else [acc])
    args += [jnp.asarray(table) for table in tables()]
    return pl.pallas_call(
        functools.partial(pair_kernel, (len(first), len(second)), acc is not None, cut, n_grp, n_orb),
        out_shape=jax.ShapeDtypeStruct((ROWS, LANES), f32),
        in_specs=[SMEM] * 2 + [VMEM] * len(args),
        out_specs=VMEM,
        scratch_shapes=[pltpu.VMEM((NGRID * NGRID, LANES), f32)] * 2,
        compiler_params=pltpu.CompilerParams(vmem_limit_bytes=40 << 20),
        cost_estimate=pl.CostEstimate(flops=8 * 10**9, bytes_accessed=5 << 20, transcendentals=0),
    )(flag.reshape(1), group.reshape(1), *args)


def strided(ref, r, count, step):
    return ref[pl.ds(r, count, stride=step), :]


def gram_kernel(n, part, place_ref, x_ref, tg_ref, th_ref, v_ref, out_ref, t_ref):
    group = place_ref[0]
    x = beside([strided(x_ref, r, n, part) for r in range(part)])
    rows = th_ref.shape[0] // part
    own = beside([strided(tg_ref, group * part + r, rows, 2 * part) for r in range(part)])
    other = beside([strided(th_ref, r, rows, part) for r in range(part)])
    t = jnp.concatenate([jnp.where(group == 0, own, other), jnp.where(group == 0, other, own)], 0)
    t_ref[...] = t
    v = beside([v_ref[r : r + 1, :] for r in range(part)])
    xh, xl = halves(x)
    th, tl = halves(t)
    wh, wl = halves(t * v)
    left = jnp.concatenate([xh, th, xl, tl], 0)
    right = jnp.concatenate([xh, th, wh, xl, tl, wl], 0)
    full = lax.dot_general(left, right, (((1,), (1,)), ((), ())), preferred_element_type=f32)
    full = full[: 2 * n] + full[2 * n :]
    full = full[:, : 3 * n] + full[:, 3 * n :]
    out_ref[...] = jnp.concatenate([full[:n, : 2 * n], full[n:, 2 * n :]], 1) * (1.0 / CELLS)


def gram_step(group, x, tg, th, v, n, part):
    return pl.pallas_call(
        functools.partial(gram_kernel, n, part),
        out_shape=(
            jax.ShapeDtypeStruct((n, 3 * n), f32),
            jax.ShapeDtypeStruct((n, part * LANES), f32),
        ),
        in_specs=[SMEM] + [VMEM] * 4,
        out_specs=(VMEM, VMEM),
        compiler_params=pltpu.CompilerParams(vmem_limit_bytes=32 << 20),
        cost_estimate=pl.CostEstimate(flops=10**9, bytes_accessed=2 << 20, transcendentals=0),
    )(group.reshape(1), x, tg, th, v)


def exact(left, right, dims):
    return lax.dot_general(
        left, right, (dims, ((), ())), precision=lax.Precision.HIGHEST, preferred_element_type=f32
    )


def mixed_rows(n, part, out_rows, first, mix, x_ref, t_ref, v_ref):
    x = beside([strided(x_ref, r, n, part) for r in range(part)])
    t = t_ref[...]
    own = t_ref[pl.ds(first, out_rows), :]
    v = beside([v_ref[r : r + 1] for r in range(part)])
    xh, xl = halves(x)
    th, tl = halves(t)
    both = dot(mix, jnp.concatenate([xh, th, xl, tl], 0))
    return own * (1.0 - STEP_SIZE * v) + both[:out_rows] + both[out_rows:]


def partner_kernel(n, part, out_rows, place_ref, g_ref, x_ref, t_ref, v_ref, out_ref, mix_ref, m_ref, r_ref):
    group = place_ref[0]
    ids = lax.broadcasted_iota(jnp.int32, (n, 1), 0)
    columns = lax.broadcasted_iota(jnp.int32, (1, 3 * n), 1)
    eye = (lax.broadcasted_iota(jnp.int32, (n, n), 0) == lax.broadcasted_iota(jnp.int32, (n, n), 1)).astype(f32)
    work = jnp.concatenate([g_ref[:, : 2 * n], eye], 1)

    def eliminate(k, work):
        row = jnp.sum(jnp.where(ids == k, work, 0.0), axis=0, keepdims=True)
        pivot = jnp.sum(jnp.where(columns == k, row, 0.0), axis=1, keepdims=True)
        column = jnp.sum(jnp.where(columns == k, work, 0.0), axis=1, keepdims=True)
        root = lax.rsqrt(pivot)
        row = row * root
        lower = work - jnp.where(ids > k, column * root, 0.0) * row
        return jnp.where(ids == k, row, lower)

    work = lax.fori_loop(0, n, eliminate, work)
    pt = work[:, n : 2 * n]
    m_ref[...] = exact(pt, work[:, 2 * n :], ((0,), (0,)))
    r_ref[...] = g_ref[:, 2 * n :] - exact(pt, pt, ((0,), (0,)))

    def mixer(start):
        rows = pl.ds(start, out_rows)
        mix = jnp.concatenate([m_ref[rows, :], r_ref[rows, :]], 1) * STEP_SIZE
        high, low = halves(mix)
        return jnp.concatenate([jnp.concatenate([high, high], 1), jnp.concatenate([low, low], 1)], 0)

    mix_ref[...] = mixer(pl.multiple_of(group * out_rows, 8))
    first = pl.multiple_of((1 - group) * out_rows, 8)
    out_ref[...] = mixed_rows(n, part, out_rows, first, mixer(first), x_ref, t_ref, v_ref)


def partner_step(group, g, x, t, v, n, part, out_rows):
    return pl.pallas_call(
        functools.partial(partner_kernel, n, part, out_rows),
        out_shape=(
            jax.ShapeDtypeStruct((out_rows, part * LANES), f32),
            jax.ShapeDtypeStruct((2 * out_rows, 4 * n), bf16),
        ),
        in_specs=[SMEM] + [VMEM] * 4,
        out_specs=(VMEM, VMEM),
        scratch_shapes=[pltpu.VMEM((n, n), f32)] * 2,
        compiler_params=pltpu.CompilerParams(vmem_limit_bytes=32 << 20),
        cost_estimate=pl.CostEstimate(flops=4 * 10**9, bytes_accessed=2 << 20, transcendentals=0),
    )(group.reshape(1), g, x, t, v)


def own_kernel(n, part, out_rows, place_ref, mix_ref, x_ref, t_ref, v_ref, out_ref):
    group = place_ref[0]
    width = part * LANES
    first = pl.multiple_of(group * out_rows, 8)
    out_ref[:, pl.ds(pl.multiple_of(group * width, width), width)] = mixed_rows(
        n, part, out_rows, first, mix_ref[...], x_ref, t_ref, v_ref
    )


def own_step(group, mix, x, t, v, n, part, out_rows):
    return pl.pallas_call(
        functools.partial(own_kernel, n, part, out_rows),
        out_shape=jax.ShapeDtypeStruct((out_rows, 2 * part * LANES), f32),
        in_specs=[SMEM] + [VMEM] * 4,
        out_specs=VMEM,
        compiler_params=pltpu.CompilerParams(vmem_limit_bytes=32 << 20),
        cost_estimate=pl.CostEstimate(flops=4 * 10**9, bytes_accessed=2 << 20, transcendentals=0),
    )(group.reshape(1), mix, x, t, v)


def moved(x, axes, target):
    size = 1
    for axis in axes:
        size *= lax.axis_size(axis)
    return lax.ppermute(x, axes, [(i, target(i)) for i in range(size)])


def summed_over(x, bits):
    masks = bits if len(bits) == 1 else [bits[0], bits[1], bits[0] ^ bits[1]]
    parts = [moved(x, ("grp", "orb"), lambda i, m=m: i ^ m) for m in masks]
    for part in parts:
        x = x + part
    return x


def on_device(occupied, targets, potential):
    n_grp, n_orb = lax.axis_size("grp"), lax.axis_size("orb")
    n = n_grp * n_orb
    part = ROWS // n
    group, orb = lax.axis_index("grp"), lax.axis_index("orb")
    one = jnp.ones((), f32)
    crossed = (((orb >> 1) & 1) != (orb & 1)).astype(f32)

    def spread(value):
        return lax.all_to_all(value.reshape(n, part, LANES), ("grp", "orb"), split_axis=0, concat_axis=0).reshape(ROWS, LANES)

    def swapped(value):
        return moved(value, ("grp",), lambda i: i ^ 1)

    def mates(pieces):
        return [moved(v, ("orb",), lambda i: i ^ 1) for v in pieces]

    target = targets.reshape(ROWS, LANES)
    own = occupied.reshape(ROWS, LANES)
    mine = lax.dynamic_slice_in_dim(own, group * (ROWS // 2), ROWS // 2, 0)
    near = moved(mine, ("orb",), lambda i: i ^ 2)
    mate = mates([own])

    acc = pair_step(one, group, target, [own], mate, None, False, n_grp, n_orb)
    near, acc = lax.optimization_barrier((near, acc))
    far = moved(near, ("orb",), lambda i: (i + (-4 if i & 2 else 4)) % n_orb)
    near = [near, swapped(near)]
    far, near, target = lax.optimization_barrier((far, near, target))
    far = [far, swapped(far)]
    t_own = lax.all_to_all(target.reshape(n_orb, n_grp * part, LANES), ("orb",), split_axis=0, concat_axis=0)
    acc = pair_step(crossed, group, target, near, mates(near), acc, False, n_grp, n_orb)
    far, acc = lax.optimization_barrier((far, acc))
    acc = pair_step(one - crossed, group, target, far, mates(far), acc, True, n_grp, n_orb)
    acc, t_own = lax.optimization_barrier((acc, t_own))
    t_other = swapped(lax.dynamic_slice_in_dim(t_own, (1 - group) * part, part, 1))
    x_half = spread(acc)

    v = lax.dynamic_slice_in_dim(potential.reshape(n_grp * part, LANES), group * part, part, 0)
    gram, t_half = gram_step(
        group, x_half, t_own.reshape(ROWS, LANES), t_other.reshape(ROWS // 2, LANES), v, n, part
    )
    rest = [b for b in (1 << k for k in range(2, 30)) if b < n_orb]
    for step in [[1], [2, n_orb]] + [rest[k : k + 2] for k in range(0, len(rest), 2)]:
        gram = summed_over(gram, step)
    partner, mix = partner_step(group, gram, x_half, t_half, v, n, part, n_orb)
    update = own_step(group, mix, x_half, t_half, v, n, part, n_orb)
    width = part * LANES
    return lax.dynamic_update_slice(update, swapped(partner), (0, (1 - group) * width))


def solution(mesh):
    placed = (P("orb", None), P(("grp", "orb"), None), P("orb"))
    return jax.shard_map(
        on_device, mesh=mesh, in_specs=placed, out_specs=P("grp", "orb"), check_vma=False
    )
```

time: 157 us -> 130 us (0.83)
  waiting for transfers between devices: 88.6 us -> 53.7 us
  local copies, waits for them, and re-layouts: 2.45 us -> 9.99 us
    all_to_all x2 -> x1, waiting for transfers between devices: 25.5 us -> 2.94 us  [spread(): lax.all_to_all(value.reshape(n, part, LANES), ('grp', 'orb'), split_axis=...]
    ppermute x19 -> x18, waiting for transfers between devices: 63.1 us -> 50.8 us  [moved(): return lax.ppermute(x, axes, [(i, target(i)) for i in range(size)])]
    all_to_all x2 -> x1, starting transfers between devices: 13.7 us -> 4.81 us  [spread(): lax.all_to_all(value.reshape(n, part, LANES), ('grp', 'orb'), split_axis=...]
    unnamed x12 -> x30, local copies, waits for them, and re-layouts: 0.02 us -> 8.04 us
    all_to_all x0 -> x1, starting transfers between devices: none -> 6.16 us  [on_device(): lax.all_to_all(target.reshape(n_orb, n_grp * part, LANES), ('orb',), spli...]
    pallas_call x5 -> x6, Pallas kernels: 32.9 us -> 34.3 us  [the longest x3 25.8 us: pair_step(): pl.pallas_call(functools.partial(pair_kernel, (len(first), len(second)),...]
    ppermute x19 -> x18, starting transfers between devices: 19.2 us -> 20.6 us  [moved(): return lax.ppermute(x, axes, [(i, target(i)) for i in range(size)])]
  transfers between devices with their start and end apart: 21 -> 20, of which waited for: 9 -> 13; matrix products, arithmetic and copies ran while one was open for 1% -> 1% of each run, Pallas kernels for 15% -> 21%
where the time goes in v1:
time: 130 us
  waiting for transfers between devices  53.7 us (41%)
  Pallas kernels  34.3 us (26%)
  starting transfers between devices  31.6 us (24%)
  local copies, waits for them, and re-layouts  9.99 us (8%)
    ppermute x18, waiting for transfers between devices, moved(): return lax.ppermute(x, axes, [(i, target(i)) for i in range(size)])  50.8 us
    pallas_call x3, Pallas kernels, pair_step(): pl.pallas_call(functools.partial(pair_kernel, (len(first), len(second)),...  25.8 us
    ppermute x18, starting transfers between devices, moved(): return lax.ppermute(x, axes, [(i, target(i)) for i in range(size)])  20.6 us
    unnamed x30, local copies, waits for them, and re-layouts  8.04 us
    all_to_all x1, starting transfers between devices, on_device(): lax.all_to_all(target.reshape(n_orb, n_grp * part, LANES), ('orb',), spli...  6.16 us
    all_to_all x1, starting transfers between devices, spread(): lax.all_to_all(value.reshape(n, part, LANES), ('grp', 'orb'), split_axis=...  4.81 us
    pallas_call x1, Pallas kernels, partner_step(): pl.pallas_call(functools.partial(partner_kernel, n, part, out_rows), out_...  4.62 us
    all_to_all x1, waiting for transfers between devices, spread(): lax.all_to_all(value.reshape(n, part, LANES), ('grp', 'orb'), split_axis=...  2.94 us
  transfers between devices with their start and end apart: 20, of which 13 were waited for; matrix products, arithmetic and copies ran while one was open for 1% of the time, Pallas kernels for 21%

profile of v1, /device:TPU:0, one launch (start us, length us, event | category | flops | bytes accessed | tf_op | source)
XLA Modules:
  0.0 129.8 jit_solution(15860507699236290038)
XLA Ops:
  0.0 0.5 collective-permute-start.1
  0.5 1.1 constant_dynamic-slice_fusion.2
  1.6 2.7 %collective-permute-start = (f32[1024,128]{1,0:T(8,128)S(1)}, f32[1024,128]{1,0:T(8,128)S(1)}, u32[]{:S(2)}, u32[]{:S(2)}) collective-permute-start(f32[1024,128]{1,0:T(8,128)S(1)} %constant_dynamic-slice_fusion.2), channel_id=1, source_target_pairs={{0,2},{1,3},{2,0},{3,1},{4,6},{5,7},{6,4},{7,5},{8,10},{9,11},{10,... | collective-permute-start | bytes 1572872 | tf_op jit(solution)/shard_map/ppermute | solution.py:297
  4.3 0.0 collective-permute-done.1.refs_1_
  4.3 0.0 copy-done.4
  4.3 0.0 copy-start.2
  4.3 0.9 copy-done.2
  5.2 0.8 copy-done.5
  5.9 0.8 copy-done.7
  6.7 8.1 %shard_map.145.refs_4_ = f32[2048,128]{1,0:T(8,128)S(1)} custom-call(f32[1]{0:T(128)} %constant.15.clone.1.flags_ref, s32[1]{0:T(128)} %bitcast.group_ref.place_ref, f32[2048,128]{1,0:T(8,128)} %bitcast.3.t_ref, f32[2048,128]{1,0:T(8,128)S(1)} %bitcast.18, f32[2048,128]{1,0:T(8,128)S(1)} %collective-permute-done.1.refs_1_, bf16[256,256]{1,0:T(8,128)(2,1)S(1)} %copy-done.2, ...), custom_call_target="tpu_custom_call" | custom-call | flops 8000000000 | bytes 5242880 | tf_op jit(solution)/shard_map/pallas_call | solution.py:160
  14.8 0.0 copy-start.11
  14.8 1.0 copy-done.11
  15.8 1.0 collective-permute-done.refs_0_
  16.8 1.9 %collective-permute-start.2 = (f32[1024,128]{1,0:T(8,128)S(1)}, f32[1024,128]{1,0:T(8,128)S(1)}, u32[]{:S(2)}, u32[]{:S(2)}) collective-permute-start(f32[1024,128]{1,0:T(8,128)S(1)} %collective-permute-done.refs_0_), channel_id=1, source_target_pairs={{0,4},{1,5},{2,14},{3,15},{4,8},{5,9},{6,2},{7,3},{8,12},{9,13},{1... | collective-permute-start | bytes 1572872 | tf_op jit(solution)/shard_map/ppermute | solution.py:297
  18.6 1.5 %collective-permute-start.3 = (f32[1024,128]{1,0:T(8,128)S(1)}, f32[1024,128]{1,0:T(8,128)S(1)}, u32[]{:S(2)}, u32[]{:S(2)}) collective-permute-start(f32[1024,128]{1,0:T(8,128)S(1)} %collective-permute-done.refs_0_), channel_id=1, source_target_pairs={{0,16},{16,0},{1,17},{17,1},{2,18},{18,2},{3,19},{19,3},{4,20},{20... | collective-permute-start | bytes 1572872 | tf_op jit(solution)/shard_map/ppermute | solution.py:297
  20.1 12.2 %collective-permute-done.2.refs_0_ = f32[1024,128]{1,0:T(8,128)S(1)} collective-permute-done((f32[1024,128]{1,0:T(8,128)S(1)}, f32[1024,128]{1,0:T(8,128)S(1)}, u32[]{:S(2)}, u32[]{:S(2)}) %collective-permute-start.2) | collective-permute-done | bytes 524320 | tf_op jit(solution)/shard_map/ppermute | solution.py:297
  32.4 0.0 collective-permute-done.3.refs_1_
  32.4 0.0 collective-permute-start.5
  32.4 0.5 collective-permute-start.6
  32.9 1.5 %collective-permute-start.4 = (f32[1024,128]{1,0:T(8,128)S(1)}, f32[1024,128]{1,0:T(8,128)S(1)}, u32[]{:S(2)}, u32[]{:S(2)}) collective-permute-start(f32[1024,128]{1,0:T(8,128)S(1)} %collective-permute-done.2.refs_0_), channel_id=1, source_target_pairs={{0,16},{16,0},{1,17},{17,1},{2,18},{18,2},{3,19},{19,3},{4,20},{20... | collective-permute-start | bytes 1572872 | tf_op jit(solution)/shard_map/ppermute | solution.py:297
  34.4 6.2 %all-to-all-start = ((f32[16,128,128]{2,1,0:T(8,128)}), f32[16,128,128]{2,1,0:T(8,128)S(1)}, u32[]{:S(2)}, u32[]{:S(2)}) async-start(f32[16,128,128]{2,1,0:T(8,128)} %bitcast.5), calls=%async_computation | async-start | bytes 2097152 | tf_op jit(solution)/shard_map/all_to_all | solution.py:337
  40.6 0.0 collective-permute-done.5.refs_2_
  40.6 0.0 collective-permute-done.6.refs_3_
  40.6 0.0 copy-start.12
  40.6 1.2 copy-done.12
  41.9 8.4 %shard_map.146.refs_4_ = f32[2048,128]{1,0:T(8,128)S(1)} custom-call(f32[1]{0:T(128)} %bitcast.4.flags_ref, s32[1]{0:T(128)} %bitcast.group_ref.place_ref, f32[2048,128]{1,0:T(8,128)} %bitcast.3.t_ref, f32[1024,128]{1,0:T(8,128)S(1)} %collective-permute-done.refs_0_, f32[1024,128]{1,0:T(8,128)S(1)} %collective-permute-done.3.refs_1_, ...), custom_call_target="tpu_custom_call" | custom-call | flops 8000000000 | bytes 5242880 | tf_op jit(solution)/shard_map/pallas_call | solution.py:160
  50.3 0.0 copy-start.13
  50.3 1.0 copy-done.13
  51.2 0.0 collective-permute-done.4.refs_1_
  51.2 0.2 collective-permute-start.7
  51.5 0.3 collective-permute-start.8
  51.8 1.4 %collective-permute-done.7.refs_2_ = f32[1024,128]{1,0:T(8,128)S(1)} collective-permute-done((f32[1024,128]{1,0:T(8,128)S(1)}, f32[1024,128]{1,0:T(8,128)S(1)}, u32[]{:S(2)}, u32[]{:S(2)}) %collective-permute-start.7) | collective-permute-done | bytes 524320 | tf_op jit(solution)/shard_map/ppermute | solution.py:297
  53.2 0.7 collective-permute-done.8.refs_3_
  53.9 1.2 copy-done.14
  55.1 9.3 %shard_map.147 = f32[2048,128]{1,0:T(8,128)} custom-call(f32[1]{0:T(128)} %bitcast.1.flags_ref, s32[1]{0:T(128)} %bitcast.group_ref.place_ref, f32[2048,128]{1,0:T(8,128)} %bitcast.3.t_ref, f32[1024,128]{1,0:T(8,128)S(1)} %collective-permute-done.2.refs_0_, f32[1024,128]{1,0:T(8,128)S(1)} %collective-permute-done.4.refs_1_, ...), custom_call_target="tpu_custom_call" | custom-call | flops 8000000000 | bytes 5242880 | tf_op jit(solution)/shard_map/pallas_call | solution.py:160
  64.4 0.0 all-to-all-done
  64.4 4.8 %all-to-all-start.1 = ((f32[32,64,128]{2,1,0:T(8,128)}), f32[32,64,128]{2,1,0:T(8,128)S(1)}, u32[]{:S(2)}, u32[]{:S(2)}) async-start(f32[32,64,128]{2,1,0:T(8,128)} %bitcast.6), calls=%async_computation.1 | async-start | bytes 2097152 | tf_op jit(solution)/shard_map/all_to_all | solution.py:317
  69.3 1.8 %collective-permute-start.9 = (f32[16,64,128]{2,1,0:T(8,128)S(1)}, f32[16,64,128]{2,1,0:T(8,128)S(1)}, u32[]{:S(2)}, u32[]{:S(2)}) collective-permute-start(f32[16,64,128]{2,1,0:T(8,128)S(1)} %constant_dynamic-slice_fusion.1), channel_id=1, source_target_pairs={{0,16},{16,0},{1,17},{17,1},{2,18},{18,2},{3,19},{19,3},{4,20},{20... | collective-permute-start | bytes 1572872 | tf_op jit(solution)/shard_map/ppermute | solution.py:297
  71.2 0.0 copy-done
  71.2 22.3 %collective-permute-done.9 = f32[16,64,128]{2,1,0:T(8,128)S(1)} collective-permute-done((f32[16,64,128]{2,1,0:T(8,128)S(1)}, f32[16,64,128]{2,1,0:T(8,128)S(1)}, u32[]{:S(2)}, u32[]{:S(2)}) %collective-permute-start.9) | collective-permute-done | bytes 524320 | tf_op jit(solution)/shard_map/ppermute | solution.py:297
  93.5 2.9 %all-to-all-done.1 = f32[32,64,128]{2,1,0:T(8,128)S(1)} async-done(((f32[32,64,128]{2,1,0:T(8,128)}), f32[32,64,128]{2,1,0:T(8,128)S(1)}, u32[]{:S(2)}, u32[]{:S(2)}) %all-to-all-start.1) | async-done | bytes 1048608 | tf_op jit(solution)/shard_map/all_to_all | solution.py:317
  96.4 2.0 %shard_map.148 = (f32[32,96]{1,0:T(8,128)S(1)}, f32[32,8192]{1,0:T(8,128)S(1)}) custom-call(s32[1]{0:T(128)} %bitcast.group_ref.place_ref, f32[2048,128]{1,0:T(8,128)S(1)} %bitcast.13, f32[2048,128]{1,0:T(8,128)S(1)} %bitcast.12, f32[1024,128]{1,0:T(8,128)S(1)} %bitcast.19, f32[64,128]{1,0:T(8,128)S(1)} %constant_dynamic-slice_fusion.v_ref), custom_call_target="tpu_custom_call" | custom-call | flops 1000000000 | bytes 2097152 | tf_op jit(solution)/shard_map/pallas_call | solution.py:196
  98.4 0.0 copy-start.9
  98.4 0.1 collective-permute-start.10
  98.5 1.2 collective-permute-done.10
  99.7 1.4 %collective-permute-start.11 = (f32[32,96]{1,0:T(8,128)S(1)}, f32[32,96]{1,0:T(8,128)S(1)}, u32[]{:S(2)}, u32[]{:S(2)}) collective-permute-start(f32[32,96]{1,0:T(8,128)S(1)} %add.36), channel_id=1, source_target_pairs={{0,2},{1,3},{2,0},{3,1},{4,6},{5,7},{6,4},{7,5},{8,10},{9,11},{10,... | collective-permute-start | bytes 36872 | tf_op jit(solution)/shard_map/ppermute | solution.py:297
  101.1 0.5 collective-permute-start.12
  101.7 1.5 %collective-permute-start.13 = (f32[32,96]{1,0:T(8,128)S(1)}, f32[32,96]{1,0:T(8,128)S(1)}, u32[]{:S(2)}, u32[]{:S(2)}) collective-permute-start(f32[32,96]{1,0:T(8,128)S(1)} %add.36), channel_id=1, source_target_pairs={{0,18},{1,19},{2,16},{3,17},{4,22},{5,23},{6,20},{7,21},{8,26},{9,... | collective-permute-start | bytes 36872 | tf_op jit(solution)/shard_map/ppermute | solution.py:297
  103.2 0.2 collective-permute-done.11
  103.4 1.6 %collective-permute-done.12 = f32[32,96]{1,0:T(8,128)S(1)} collective-permute-done((f32[32,96]{1,0:T(8,128)S(1)}, f32[32,96]{1,0:T(8,128)S(1)}, u32[]{:S(2)}, u32[]{:S(2)}) %collective-permute-start.12) | collective-permute-done | bytes 12320 | tf_op jit(solution)/shard_map/ppermute | solution.py:297
  105.0 1.3 collective-permute-done.13
  106.3 0.0 collective-permute-start.14
  106.3 1.8 %collective-permute-start.15 = (f32[32,96]{1,0:T(8,128)S(1)}, f32[32,96]{1,0:T(8,128)S(1)}, u32[]{:S(2)}, u32[]{:S(2)}) collective-permute-start(f32[32,96]{1,0:T(8,128)S(1)} %add_add_fusion.1), channel_id=1, source_target_pairs={{0,8},{1,9},{2,10},{3,11},{4,12},{5,13},{6,14},{7,15},{8,0},{9,1},... | collective-permute-start | bytes 36872 | tf_op jit(solution)/shard_map/ppermute | solution.py:297
  108.1 2.6 %collective-permute-start.16 = (f32[32,96]{1,0:T(8,128)S(1)}, f32[32,96]{1,0:T(8,128)S(1)}, u32[]{:S(2)}, u32[]{:S(2)}) collective-permute-start(f32[32,96]{1,0:T(8,128)S(1)} %add_add_fusion.1), channel_id=1, source_target_pairs={{0,12},{1,13},{2,14},{3,15},{4,8},{5,9},{6,10},{7,11},{8,4},{9,5},... | collective-permute-start | bytes 36872 | tf_op jit(solution)/shard_map/ppermute | solution.py:297
  110.7 0.0 collective-permute-done.14
  110.7 0.3 collective-permute-done.15
  111.0 2.7 %collective-permute-done.16 = f32[32,96]{1,0:T(8,128)S(1)} collective-permute-done((f32[32,96]{1,0:T(8,128)S(1)}, f32[32,96]{1,0:T(8,128)S(1)}, u32[]{:S(2)}, u32[]{:S(2)}) %collective-permute-start.16) | collective-permute-done | bytes 12320 | tf_op jit(solution)/shard_map/ppermute | solution.py:297
  113.7 4.6 %shard_map.149 = (f32[16,8192]{1,0:T(8,128)S(1)}, bf16[32,128]{1,0:T(8,128)(2,1)S(1)}) custom-call(s32[1]{0:T(128)} %bitcast.group_ref.place_ref, f32[32,96]{1,0:T(8,128)S(1)} %add_add_fusion.g_ref, f32[2048,128]{1,0:T(8,128)S(1)} %bitcast.14, f32[32,8192]{1,0:T(8,128)S(1)} %get-tuple-element.32.t_ref, f32[64,128]{1,0:T(8,128)S(1)} %constant_dynamic-slice_fusion.v_ref), custom_call_target="tpu_custom_call" | custom-call | flops 4000000000 | bytes 2097152 | tf_op jit(solution)/shard_map/pallas_call | solution.py:259
  118.3 0.0 copy-done.9
  118.3 1.7 %collective-permute-start.17 = (f32[16,8192]{1,0:T(8,128)S(1)}, f32[16,8192]{1,0:T(8,128)S(1)}, u32[]{:S(2)}, u32[]{:S(2)}) collective-permute-start(f32[16,8192]{1,0:T(8,128)S(1)} %get-tuple-element.34), channel_id=1, source_target_pairs={{0,16},{16,0},{1,17},{17,1},{2,18},{18,2},{3,19},{19,3},{4,20},{20... | collective-permute-start | bytes 1572872 | tf_op jit(solution)/shard_map/ppermute | solution.py:297
  120.0 1.2 copy-done.10
  121.3 1.9 %shard_map.150 = f32[16,16384]{1,0:T(8,128)} custom-call(s32[1]{0:T(128)} %bitcast.group_ref.place_ref, bf16[32,128]{1,0:T(8,128)(2,1)S(1)} %get-tuple-element.33.mix_ref, f32[2048,128]{1,0:T(8,128)S(1)} %bitcast.15, f32[32,8192]{1,0:T(8,128)S(1)} %copy-done.10, f32[64,128]{1,0:T(8,128)S(1)} %constant_dynamic-slice_fusion.v_ref), custom_call_target="tpu_custom_call" | custom-call | flops 4000000000 | bytes 2097152 | tf_op jit(solution)/shard_map/pallas_call | solution.py:283
  123.2 5.8 %collective-permute-done.17 = f32[16,8192]{1,0:T(8,128)S(1)} collective-permute-done((f32[16,8192]{1,0:T(8,128)S(1)}, f32[16,8192]{1,0:T(8,128)S(1)}, u32[]{:S(2)}, u32[]{:S(2)}) %collective-permute-start.17) | collective-permute-done | bytes 524320 | tf_op jit(solution)/shard_map/ppermute | solution.py:297
  129.0 0.8 constant_dynamic-update-slice_fusion
  (19 shorter events, 0.1 us)
Async XLA Ops:
  0.0 71.2 %copy-start = (f32[16384]{0:T(1024)S(1)}, f32[16384]{0:T(1024)}, u32[]{:S(2)}) copy-start(f32[16384]{0:T(1024)} %param.17) | copy-start | bytes 196612
  0.0 4.3 %copy-start.4 = (bf16[64,256]{1,0:T(8,128)(2,1)S(1)}, bf16[64,256]{1,0:T(8,128)(2,1)}, u32[]{:S(2)}) copy-start(bf16[64,256]{1,0:T(8,128)(2,1)} %constant.38.clone.refs_3_.refs_6_) | copy-start | bytes 98308
  0.0 4.3 %copy-start.1 = (f32[1,262144]{1,0:T(1,128)S(1)}, f32[1,262144]{1,0:T(1,128)}, u32[]{:S(2)}) copy-start(f32[1,262144]{1,0:T(1,128)} %param.15) | copy-start | bytes 3145732
  0.0 4.3 %collective-permute-start.1 = (f32[2048,128]{1,0:T(8,128)}, f32[2048,128]{1,0:T(8,128)S(1)}, u32[]{:S(2)}, u32[]{:S(2)}) collective-permute-start(f32[2048,128]{1,0:T(8,128)} %bitcast.16), channel_id=1, source_target_pairs={{0,1},{1,0},{2,3},{3,2},{4,5},{5,4},{6,7},{7,6},{8,9},{9,8},{10,11... | collective-permute-start | bytes 3145736 | tf_op jit(solution)/shard_map/ppermute | solution.py:297
  1.6 15.2 %collective-permute-start = (f32[1024,128]{1,0:T(8,128)S(1)}, f32[1024,128]{1,0:T(8,128)S(1)}, u32[]{:S(2)}, u32[]{:S(2)}) collective-permute-start(f32[1024,128]{1,0:T(8,128)S(1)} %constant_dynamic-slice_fusion.2), channel_id=1, source_target_pairs={{0,2},{1,3},{2,0},{3,1},{4,6},{5,7},{6,4},{7,5},{8,10},{9,11},{10,... | collective-permute-start | bytes 1572872 | tf_op jit(solution)/shard_map/ppermute | solution.py:297
  4.3 0.9 copy-start.2
  5.2 0.8 copy-start.5
  5.9 0.8 copy-start.7
  14.8 1.0 copy-start.11
  16.8 15.6 %collective-permute-start.2 = (f32[1024,128]{1,0:T(8,128)S(1)}, f32[1024,128]{1,0:T(8,128)S(1)}, u32[]{:S(2)}, u32[]{:S(2)}) collective-permute-start(f32[1024,128]{1,0:T(8,128)S(1)} %collective-permute-done.refs_0_), channel_id=1, source_target_pairs={{0,4},{1,5},{2,14},{3,15},{4,8},{5,9},{6,2},{7,3},{8,12},{9,13},{1... | collective-permute-start | bytes 1572872 | tf_op jit(solution)/shard_map/ppermute | solution.py:297
  18.6 13.8 %collective-permute-start.3 = (f32[1024,128]{1,0:T(8,128)S(1)}, f32[1024,128]{1,0:T(8,128)S(1)}, u32[]{:S(2)}, u32[]{:S(2)}) collective-permute-start(f32[1024,128]{1,0:T(8,128)S(1)} %collective-permute-done.refs_0_), channel_id=1, source_target_pairs={{0,16},{16,0},{1,17},{17,1},{2,18},{18,2},{3,19},{19,3},{4,20},{20... | collective-permute-start | bytes 1572872 | tf_op jit(solution)/shard_map/ppermute | solution.py:297
  32.4 8.2 %collective-permute-start.5 = (f32[1024,128]{1,0:T(8,128)S(1)}, f32[1024,128]{1,0:T(8,128)}, u32[]{:S(2)}, u32[]{:S(2)}) collective-permute-start(f32[1024,128]{1,0:T(8,128)S(1)} %collective-permute-done.refs_0_), channel_id=1, source_target_pairs={{0,1},{1,0},{2,3},{3,2},{4,5},{5,4},{6,7},{7,6},{8,9},{9,8},{10,11... | collective-permute-start | bytes 1572872 | tf_op jit(solution)/shard_map/ppermute | solution.py:297
  32.4 8.2 %collective-permute-start.6 = (f32[1024,128]{1,0:T(8,128)S(1)}, f32[1024,128]{1,0:T(8,128)}, u32[]{:S(2)}, u32[]{:S(2)}) collective-permute-start(f32[1024,128]{1,0:T(8,128)S(1)} %collective-permute-done.3.refs_1_), channel_id=1, source_target_pairs={{0,1},{1,0},{2,3},{3,2},{4,5},{5,4},{6,7},{7,6},{8,9},{9,8},{10,11... | collective-permute-start | bytes 1572872 | tf_op jit(solution)/shard_map/ppermute | solution.py:297
  32.9 18.4 %collective-permute-start.4 = (f32[1024,128]{1,0:T(8,128)S(1)}, f32[1024,128]{1,0:T(8,128)S(1)}, u32[]{:S(2)}, u32[]{:S(2)}) collective-permute-start(f32[1024,128]{1,0:T(8,128)S(1)} %collective-permute-done.2.refs_0_), channel_id=1, source_target_pairs={{0,16},{16,0},{1,17},{17,1},{2,18},{18,2},{3,19},{19,3},{4,20},{20... | collective-permute-start | bytes 1572872 | tf_op jit(solution)/shard_map/ppermute | solution.py:297
  34.4 6.2 %copy-start.3 = (bf16[256,256]{1,0:T(8,128)(2,1)S(1)}, bf16[256,256]{1,0:T(8,128)(2,1)}, u32[]{:S(2)}) copy-start(bf16[256,256]{1,0:T(8,128)(2,1)} %constant.37.clone.refs_2_.refs_5_) | copy-start | bytes 393220
  34.4 6.2 %copy-start.6 = (bf16[64,256]{1,0:T(8,128)(2,1)S(1)}, bf16[64,256]{1,0:T(8,128)(2,1)}, u32[]{:S(2)}) copy-start(bf16[64,256]{1,0:T(8,128)(2,1)} %constant.39.clone.refs_4_.refs_7_) | copy-start | bytes 98308
  34.4 6.2 %copy-start.8 = (bf16[64,256]{1,0:T(8,128)(2,1)S(1)}, bf16[64,256]{1,0:T(8,128)(2,1)}, u32[]{:S(2)}) copy-start(bf16[64,256]{1,0:T(8,128)(2,1)} %constant.40.clone.refs_5_.refs_8_) | copy-start | bytes 98308
  34.4 30.0 %all-to-all-start = ((f32[16,128,128]{2,1,0:T(8,128)}), f32[16,128,128]{2,1,0:T(8,128)S(1)}, u32[]{:S(2)}, u32[]{:S(2)}) async-start(f32[16,128,128]{2,1,0:T(8,128)} %bitcast.5), calls=%async_computation | async-start | bytes 2097152 | tf_op jit(solution)/shard_map/all_to_all | solution.py:337
  40.6 1.2 copy-start.12
  50.3 1.0 copy-start.13
  51.2 1.9 %collective-permute-start.7 = (f32[1024,128]{1,0:T(8,128)S(1)}, f32[1024,128]{1,0:T(8,128)S(1)}, u32[]{:S(2)}, u32[]{:S(2)}) collective-permute-start(f32[1024,128]{1,0:T(8,128)S(1)} %collective-permute-done.2.refs_0_), channel_id=1, source_target_pairs={{0,1},{1,0},{2,3},{3,2},{4,5},{5,4},{6,7},{7,6},{8,9},{9,8},{10,11... | collective-permute-start | bytes 1572872 | tf_op jit(solution)/shard_map/ppermute | solution.py:297
  51.5 2.4 %collective-permute-start.8 = (f32[1024,128]{1,0:T(8,128)S(1)}, f32[1024,128]{1,0:T(8,128)S(1)}, u32[]{:S(2)}, u32[]{:S(2)}) collective-permute-start(f32[1024,128]{1,0:T(8,128)S(1)} %collective-permute-done.4.refs_1_), channel_id=1, source_target_pairs={{0,1},{1,0},{2,3},{3,2},{4,5},{5,4},{6,7},{7,6},{8,9},{9,8},{10,11... | collective-permute-start | bytes 1572872 | tf_op jit(solution)/shard_map/ppermute | solution.py:297
  53.9 1.2 copy-start.14
  64.4 32.0 %all-to-all-start.1 = ((f32[32,64,128]{2,1,0:T(8,128)}), f32[32,64,128]{2,1,0:T(8,128)S(1)}, u32[]{:S(2)}, u32[]{:S(2)}) async-start(f32[32,64,128]{2,1,0:T(8,128)} %bitcast.6), calls=%async_computation.1 | async-start | bytes 2097152 | tf_op jit(solution)/shard_map/all_to_all | solution.py:317
  69.3 24.2 %collective-permute-start.9 = (f32[16,64,128]{2,1,0:T(8,128)S(1)}, f32[16,64,128]{2,1,0:T(8,128)S(1)}, u32[]{:S(2)}, u32[]{:S(2)}) collective-permute-start(f32[16,64,128]{2,1,0:T(8,128)S(1)} %constant_dynamic-slice_fusion.1), channel_id=1, source_target_pairs={{0,16},{16,0},{1,17},{17,1},{2,18},{18,2},{3,19},{19,3},{4,20},{20... | collective-permute-start | bytes 1572872 | tf_op jit(solution)/shard_map/ppermute | solution.py:297
  98.4 19.9 %copy-start.9 = (f32[32,8192]{1,0:T(8,128)}, f32[32,8192]{1,0:T(8,128)S(1)}, u32[]{:S(2)}) copy-start(f32[32,8192]{1,0:T(8,128)S(1)} %get-tuple-element.32.t_ref) | copy-start | bytes 3145732
  98.4 1.2 collective-permute-start.10
  99.7 3.7 %collective-permute-start.11 = (f32[32,96]{1,0:T(8,128)S(1)}, f32[32,96]{1,0:T(8,128)S(1)}, u32[]{:S(2)}, u32[]{:S(2)}) collective-permute-start(f32[32,96]{1,0:T(8,128)S(1)} %add.36), channel_id=1, source_target_pairs={{0,2},{1,3},{2,0},{3,1},{4,6},{5,7},{6,4},{7,5},{8,10},{9,11},{10,... | collective-permute-start | bytes 36872 | tf_op jit(solution)/shard_map/ppermute | solution.py:297
  101.1 3.9 %collective-permute-start.12 = (f32[32,96]{1,0:T(8,128)S(1)}, f32[32,96]{1,0:T(8,128)S(1)}, u32[]{:S(2)}, u32[]{:S(2)}) collective-permute-start(f32[32,96]{1,0:T(8,128)S(1)} %add.36), channel_id=1, source_target_pairs={{0,16},{1,17},{2,18},{3,19},{4,20},{5,21},{6,22},{7,23},{8,24},{9,... | collective-permute-start | bytes 36872 | tf_op jit(solution)/shard_map/ppermute | solution.py:297
  101.7 4.6 %collective-permute-start.13 = (f32[32,96]{1,0:T(8,128)S(1)}, f32[32,96]{1,0:T(8,128)S(1)}, u32[]{:S(2)}, u32[]{:S(2)}) collective-permute-start(f32[32,96]{1,0:T(8,128)S(1)} %add.36), channel_id=1, source_target_pairs={{0,18},{1,19},{2,16},{3,17},{4,22},{5,23},{6,20},{7,21},{8,26},{9,... | collective-permute-start | bytes 36872 | tf_op jit(solution)/shard_map/ppermute | solution.py:297
  106.3 4.4 %collective-permute-start.14 = (f32[32,96]{1,0:T(8,128)S(1)}, f32[32,96]{1,0:T(8,128)S(1)}, u32[]{:S(2)}, u32[]{:S(2)}) collective-permute-start(f32[32,96]{1,0:T(8,128)S(1)} %add_add_fusion.1), channel_id=1, source_target_pairs={{0,4},{1,5},{2,6},{3,7},{4,0},{5,1},{6,2},{7,3},{8,12},{9,13},{10,... | collective-permute-start | bytes 36872 | tf_op jit(solution)/shard_map/ppermute | solution.py:297
  106.3 4.7 %collective-permute-start.15 = (f32[32,96]{1,0:T(8,128)S(1)}, f32[32,96]{1,0:T(8,128)S(1)}, u32[]{:S(2)}, u32[]{:S(2)}) collective-permute-start(f32[32,96]{1,0:T(8,128)S(1)} %add_add_fusion.1), channel_id=1, source_target_pairs={{0,8},{1,9},{2,10},{3,11},{4,12},{5,13},{6,14},{7,15},{8,0},{9,1},... | collective-permute-start | bytes 36872 | tf_op jit(solution)/shard_map/ppermute | solution.py:297
  108.1 5.5 %collective-permute-start.16 = (f32[32,96]{1,0:T(8,128)S(1)}, f32[32,96]{1,0:T(8,128)S(1)}, u32[]{:S(2)}, u32[]{:S(2)}) collective-permute-start(f32[32,96]{1,0:T(8,128)S(1)} %add_add_fusion.1), channel_id=1, source_target_pairs={{0,12},{1,13},{2,14},{3,15},{4,8},{5,9},{6,10},{7,11},{8,4},{9,5},... | collective-permute-start | bytes 36872 | tf_op jit(solution)/shard_map/ppermute | solution.py:297
  118.3 10.6 %collective-permute-start.17 = (f32[16,8192]{1,0:T(8,128)S(1)}, f32[16,8192]{1,0:T(8,128)S(1)}, u32[]{:S(2)}, u32[]{:S(2)}) collective-permute-start(f32[16,8192]{1,0:T(8,128)S(1)} %get-tuple-element.34), channel_id=1, source_target_pairs={{0,16},{16,0},{1,17},{17,1},{2,18},{18,2},{3,19},{19,3},{4,20},{20... | collective-permute-start | bytes 1572872 | tf_op jit(solution)/shard_map/ppermute | solution.py:297
  120.0 1.2 copy-start.10

commit v2 on v1

--- a/solution.py
+++ b/solution.py
@@ -14,8 +14,8 @@
 LANES = 128
 ROWS = CELLS // LANES
 SLAB = NGRID * NGRID // LANES
-CHUNK = 64
-LOOPS = NGRID // CHUNK
+HALF = ROWS // 2
+GROUP = 32
 
 SCREEN_SQ = 0.04
 BOX_LENGTH = 20.0
@@ -41,17 +41,12 @@
         return both
 
     def stacked(high, low):
-        return np.concatenate([high, high, low, low], 1)
+        return np.concatenate([high, high, low, np.zeros_like(low)], 1)
 
     row = np.concatenate([twice(high), twice(low)], 1)
-    along_z = np.concatenate([row, row], 0)
     order = np.concatenate([index[0::2], index[1::2]])
-    return (
-        along_z,
-        stacked(high, low),
-        stacked(high[:, order], low[:, order]),
-        stacked(high[order], low[order]),
-    )
+    parts = [row, row, stacked(high, low), stacked(high[:, order], low[:, order])]
+    return np.concatenate(parts + [stacked(high[order], low[order])], 0)
 
 
 def halves(value):
@@ -70,7 +65,7 @@
 
 def along_rows(value, table):
     high, low = halves(value)
-    return dot(table, jnp.concatenate([high, low, high, low], 0))
+    return dot(table, jnp.concatenate([high, low, high], 0))
 
 
 def beside(blocks):
@@ -81,102 +76,215 @@
     return [value[:, i : i + LANES] for i in range(0, value.shape[1], LANES)]
 
 
-def pair_kernel(counts, has_acc, pieces, n_grp, n_orb, flags_ref, group_ref, t_ref, *refs):
-    a_refs, b_refs, refs = refs[: counts[0]], refs[counts[0] : sum(counts)], refs[sum(counts) :]
-    if has_acc:
-        acc_ref, refs = refs[0], refs[1:]
-    z_ref, x_ref, yf_ref, yi_ref, out_ref, s_ref, s2_ref = refs
-    first = lax.broadcasted_iota(jnp.int32, (1, LANES), 1) < NGRID
-    rows = SLAB * CHUNK
-    scale_b = flags_ref[0]
-
-    leading = group_ref[0] == 0
-
-    def chosen(pieces):
-        if len(pieces) == 1:
-            return pieces[0][...]
-        own, other = pieces[0][...], pieces[1][...]
-        return jnp.concatenate([jnp.where(leading, own, other), jnp.where(leading, other, own)], 0)
-
-    for c in range(LOOPS):
-        t = t_ref[c * rows : (c + 1) * rows, :]
-        pa = t * chosen(a_refs)
-        pb = t * (chosen(b_refs) * scale_b)
-        even = jnp.where(first, pa, pltpu.roll(pb, NGRID, 1)).reshape(CHUNK, SLAB, LANES)
-        odd = jnp.where(first, pltpu.roll(pa, NGRID, 1), pb).reshape(CHUNK, SLAB, LANES)
-        v = jnp.concatenate([even, odd], 1).reshape(CHUNK * NGRID, LANES)
-        v = along_lanes(v, z_ref[...]).reshape(CHUNK, NGRID, LANES)
-        v = along_rows(beside([v[i] for i in range(CHUNK)]), yf_ref[...])
-        for i, block in enumerate(apart(v)):
-            s_ref[(c * CHUNK + i) * NGRID : (c * CHUNK + i + 1) * NGRID, :] = block
-
+def in_order(leading, pieces):
+    if len(pieces) == 1:
+        return pieces[0][...]
+    own, other = pieces[0][...], pieces[1][...]
+    return jnp.concatenate([jnp.where(leading, own, other), jnp.where(leading, other, own)], 0)
+
+
+def split_table(table_ref):
+    along_z = table_ref[: 4 * NGRID, :]
+    rest = [table_ref[(4 + i) * NGRID : (5 + i) * NGRID, : 3 * NGRID] for i in range(3)]
+    return along_z, *rest
+
+
+def first_half():
+    return lax.broadcasted_iota(jnp.int32, (1, LANES), 1) < NGRID
+
+
+def woven(first, a, b):
+    return jnp.where(first, a, pltpu.roll(b, NGRID, 1)), jnp.where(first, pltpu.roll(a, NGRID, 1), b)
+
+
+def wave(k):
+    return min(k, NGRID - k) * (2.0 * np.pi / BOX_LENGTH)
+
+
+def kernel_base():
     def squared(k):
-        wave = jnp.minimum(k, NGRID - k).astype(f32) * (2.0 * np.pi / BOX_LENGTH)
-        return wave * wave
+        line = jnp.minimum(k, NGRID - k).astype(f32) * (2.0 * np.pi / BOX_LENGTH)
+        return line * line
 
     cube = (NGRID, LANES)
-    base = (
+    return (
         squared(lax.broadcasted_iota(jnp.int32, cube, 0))
         + squared(lax.broadcasted_iota(jnp.int32, cube, 1) % NGRID)
         + SCREEN_SQ
     )
-    for c in range(LOOPS):
-        v = beside([s_ref[pl.ds(c * CHUNK + i, NGRID, stride=NGRID), :] for i in range(CHUNK)])
-        v = along_rows(v, x_ref[...])
-        kernel = []
-        for i in range(CHUNK):
-            y = c * CHUNK + i
-            wave = min(y, NGRID - y) * (2.0 * np.pi / BOX_LENGTH)
-            kernel.append((4.0 * np.pi / CELLS) / (base + wave * wave))
-        v = along_rows(v * beside(kernel), x_ref[...])
-        for i, block in enumerate(apart(v)):
-            s2_ref[(c * CHUNK + i) * NGRID : (c * CHUNK + i + 1) * NGRID, :] = block
-
-    for c in range(LOOPS):
-        v = beside([s2_ref[pl.ds(c * CHUNK + i, NGRID, stride=NGRID), :] for i in range(CHUNK)])
-        v = jnp.concatenate(apart(along_rows(v, yi_ref[...])), 0)
-        v = along_lanes(v, z_ref[...]).reshape(CHUNK, NGRID, LANES)
-        even = v[:, :SLAB].reshape(rows, LANES)
-        odd = v[:, SLAB:].reshape(rows, LANES)
-        sa = jnp.where(first, even, pltpu.roll(odd, NGRID, 1))
-        sb = jnp.where(first, pltpu.roll(even, NGRID, 1), odd)
-        added = -(chosen(a_refs) * sa + (chosen(b_refs) * scale_b) * sb)
-        if has_acc:
-            added = acc_ref[c * rows : (c + 1) * rows, :] + added
-        if pieces:
+
+
+def forward_zy(first, pa, pb, along_z, along_y, s_ref):
+    slabs = pa.shape[0] // SLAB
+    even, odd = woven(first, pa, pb)
+    v = jnp.concatenate([even.reshape(slabs, SLAB, LANES), odd.reshape(slabs, SLAB, LANES)], 1)
+    v = along_lanes(v.reshape(slabs * NGRID, LANES), along_z).reshape(slabs, NGRID, LANES)
+    v = along_rows(beside([v[i] for i in range(slabs)]), along_y)
+    for i, block in enumerate(apart(v)):
+        s_ref[i * NGRID : (i + 1) * NGRID, :] = block
+
+
+def backward_yz(first, start, count, step, along_y, along_z, s_ref):
+    v = beside([s_ref[pl.ds(start + i, NGRID, stride=step), :] for i in range(count)])
+    v = jnp.concatenate(apart(along_rows(v, along_y)), 0)
+    v = along_lanes(v, along_z).reshape(count, NGRID, LANES)
+    return woven(first, v[:, :SLAB].reshape(count * SLAB, LANES), v[:, SLAB:].reshape(count * SLAB, LANES))
+
+
+def pair_kernel(counts, n_acc, cut, n_grp, n_orb, flag_ref, group_ref, earlier_ref, table_ref, t_ref, *refs):
+    refs = list(refs)
+    groups = [[refs.pop(0) for _ in range(count)] for count in counts]
+    acc_refs = [refs.pop(0) for _ in range(n_acc)]
+    out_ref, token_ref, s_ref, s2_ref, out_buf, out_sems = refs[:6]
+    acc_bufs, acc_sems = refs[6:-1], refs[-1]
+    token_ref[...] = earlier_ref[:8, :]
+    loads = [
+        pltpu.make_async_copy(ref, buf, acc_sems.at[i])
+        for i, (ref, buf) in enumerate(zip(acc_refs, acc_bufs))
+    ]
+    for load in loads:
+        load.start()
+    first = first_half()
+    leading = group_ref[0] == 0
+    along_z, along_x, along_y, back_y = split_table(table_ref)
+
+    def fields():
+        b = in_order(leading, groups[1])
+        if len(groups) == 3:
+            b = jnp.where(flag_ref[0] > 0, b, in_order(leading, groups[2]))
+        return in_order(leading, groups[0]), b
+
+    t = t_ref[...]
+    a, b = fields()
+    forward_zy(first, t * a, t * b, along_z, along_y, s_ref)
+
+    base = kernel_base()
+    kernels = {}
+    for y in range(NGRID // 2 + 1):
+        kernels[y] = (4.0 * np.pi / CELLS) / (base + wave(y) * wave(y))
+    v = beside([s_ref[pl.ds(y, NGRID, stride=NGRID), :] for y in range(NGRID)])
+    v = along_rows(v, along_x) * beside([kernels[min(y, NGRID - y)] for y in range(NGRID)])
+    for y, block in enumerate(apart(along_rows(v, along_x))):
+        s2_ref[y * NGRID : (y + 1) * NGRID, :] = block
+
+    for load in loads:
+        load.wait()
+    a, b = fields()
+    stores = []
+    for c in range(NGRID // GROUP):
+        rows = slice(c * GROUP * SLAB, (c + 1) * GROUP * SLAB)
+        sa, sb = backward_yz(first, c * GROUP, GROUP, NGRID, back_y, along_z, s2_ref)
+        added = -(a[rows] * sa + b[rows] * sb)
+        for buf in acc_bufs:
+            added = added + buf[rows, :]
+        if cut:
             part = ROWS // (n_grp * n_orb)
-            count = n_orb // LOOPS
-            cut = added.reshape(count, n_grp, part, LANES)
+            count = n_orb * GROUP // NGRID
+            pieces = added.reshape(count, n_grp, part, LANES)
             for g in range(n_grp):
                 start = (g * n_orb + c * count) * part
-                out_ref[start : start + count * part, :] = cut[:, g].reshape(count * part, LANES)
+                out_ref[start : start + count * part, :] = pieces[:, g].reshape(count * part, LANES)
         else:
-            out_ref[c * rows : (c + 1) * rows, :] = added
-
-
-def pair_step(flag, group, target, first, second, acc, cut, n_grp, n_orb):
-    args = [target, *first, *second] + ([] if acc is None else [acc])
-    args += [jnp.asarray(table) for table in tables()]
+            out_buf[rows, :] = added
+            stores.append(pltpu.make_async_copy(out_buf.at[rows], out_ref.at[rows], out_sems.at[c]))
+            stores[-1].start()
+    for store in stores:
+        store.wait()
+
+
+def single_kernel(
+    group_ref, earlier_ref, table_ref, t_ref, own_ref, other_ref, out_ref, token_ref, s_ref, s2_ref, out_buf, out_sems
+):
+    token_ref[...] = earlier_ref[:8, :]
+    first = first_half()
+    leading = group_ref[0] == 0
+    along_z, along_x, along_y, back_y = split_table(table_ref)
+    middle = NGRID // 2
+
+    def both():
+        own, other = own_ref[...], other_ref[...]
+        return jnp.where(leading, own, other), jnp.where(leading, other, own)
+
+    low, high = both()
+    forward_zy(first, t_ref[:HALF, :] * low, t_ref[HALF:, :] * high, along_z, along_y, s_ref)
+
+    base = kernel_base()
+    ys = [(0, middle)] + [(y, NGRID - y) for y in range(1, middle)]
+    kernel, blocks = [], []
+    for y, z in ys:
+        square = wave(y) * wave(y)
+        if wave(y) != wave(z):
+            square = jnp.where(first, square, wave(z) * wave(z))
+        kernel.append((4.0 * np.pi / CELLS) / (base + square))
+        top, bottom = woven(
+            first, s_ref[pl.ds(y, middle, stride=NGRID), :], s_ref[pl.ds(z, middle, stride=NGRID), :]
+        )
+        blocks.append(jnp.concatenate([top, bottom], 0))
+    v = along_rows(along_rows(beside(blocks), along_x) * beside(kernel), along_x)
+    for (y, z), block in zip(ys, apart(v)):
+        at_y, at_z = woven(first, block[:middle], block[middle:])
+        s2_ref[y * middle : (y + 1) * middle, :] = at_y
+        s2_ref[z * middle : (z + 1) * middle, :] = at_z
+
+    low, high = both()
+    sa, sb = backward_yz(first, 0, middle, middle, back_y, along_z, s2_ref)
+    stores = []
+    for c, value in enumerate((-(low * sa), -(high * sb))):
+        rows = slice(c * HALF, (c + 1) * HALF)
+        out_buf[rows, :] = value
+        stores.append(pltpu.make_async_copy(out_buf.at[rows], out_ref.at[rows], out_sems.at[c]))
+        stores[-1].start()
+    for store in stores:
+        store.wait()
+
+
+ANY = pl.BlockSpec(memory_space=pl.ANY)
+TOKEN = jax.ShapeDtypeStruct((8, LANES), f32)
+FIELD = pltpu.HBM((ROWS, LANES), f32)
+
+
+def pair_step(flag, group, token, target, fields, accs, cut, n_grp, n_orb):
+    operands = [token, jnp.asarray(tables()), target] + [piece for field in fields for piece in field]
+    counts = tuple(len(field) for field in fields)
+    held = [pltpu.with_memory_space_constraint(acc, pltpu.HBM) for acc in accs]
     return pl.pallas_call(
-        functools.partial(pair_kernel, (len(first), len(second)), acc is not None, cut, n_grp, n_orb),
-        out_shape=jax.ShapeDtypeStruct((ROWS, LANES), f32),
-        in_specs=[SMEM] * 2 + [VMEM] * len(args),
-        out_specs=VMEM,
-        scratch_shapes=[pltpu.VMEM((NGRID * NGRID, LANES), f32)] * 2,
+        functools.partial(pair_kernel, counts, len(accs), cut, n_grp, n_orb),
+        out_shape=(jax.ShapeDtypeStruct((ROWS, LANES), f32) if cut else FIELD, TOKEN),
+        in_specs=[SMEM] * 2 + [VMEM] * len(operands) + [ANY] * len(accs),
+        out_specs=(VMEM if cut else ANY, VMEM),
+        scratch_shapes=[pltpu.VMEM((NGRID * NGRID, LANES), f32)] * 2
+        + [pltpu.VMEM((ROWS, LANES), f32), pltpu.SemaphoreType.DMA((2,))]
+        + [pltpu.VMEM((ROWS, LANES), f32)] * len(accs)
+        + [pltpu.SemaphoreType.DMA((max(len(accs), 1),))],
+        compiler_params=pltpu.CompilerParams(vmem_limit_bytes=44 << 20),
+        cost_estimate=pl.CostEstimate(flops=10**8 if cut else 8 * 10**9, bytes_accessed=1 << 18, transcendentals=0),
+    )(flag.reshape(1), group.reshape(1), *operands, *held)
+
+
+def single_step(group, token, target, pieces):
+    return pl.pallas_call(
+        single_kernel,
+        out_shape=(FIELD, TOKEN),
+        in_specs=[SMEM] + [VMEM] * 5,
+        out_specs=(ANY, VMEM),
+        scratch_shapes=[pltpu.VMEM((NGRID * NGRID // 2, LANES), f32)] * 2
+        + [pltpu.VMEM((ROWS, LANES), f32), pltpu.SemaphoreType.DMA((2,))],
         compiler_params=pltpu.CompilerParams(vmem_limit_bytes=40 << 20),
-        cost_estimate=pl.CostEstimate(flops=8 * 10**9, bytes_accessed=5 << 20, transcendentals=0),
-    )(flag.reshape(1), group.reshape(1), *args)
+        cost_estimate=pl.CostEstimate(flops=10**10, bytes_accessed=4 << 20, transcendentals=0),
+    )(group.reshape(1), token, jnp.asarray(tables()), target, *pieces)
 
 
 def strided(ref, r, count, step):
     return ref[pl.ds(r, count, stride=step), :]
 
 
-def gram_kernel(n, part, place_ref, x_ref, tg_ref, th_ref, v_ref, out_ref, t_ref):
+def gram_kernel(n, part, place_ref, x_ref, tl_ref, tu_ref, th_ref, v_ref, out_ref, t_ref):
     group = place_ref[0]
     x = beside([strided(x_ref, r, n, part) for r in range(part)])
     rows = th_ref.shape[0] // part
-    own = beside([strided(tg_ref, group * part + r, rows, 2 * part) for r in range(part)])
+    low = beside([strided(tl_ref, r, rows, part) for r in range(part)])
+    high = beside([strided(tu_ref, r, rows, part) for r in range(part)])
+    own = jnp.where(group == 0, low, high)
     other = beside([strided(th_ref, r, rows, part) for r in range(part)])
     t = jnp.concatenate([jnp.where(group == 0, own, other), jnp.where(group == 0, other, own)], 0)
     t_ref[...] = t
@@ -192,18 +300,18 @@
     out_ref[...] = jnp.concatenate([full[:n, : 2 * n], full[n:, 2 * n :]], 1) * (1.0 / CELLS)
 
 
-def gram_step(group, x, tg, th, v, n, part):
+def gram_step(group, x, tl, tu, th, v, n, part):
     return pl.pallas_call(
         functools.partial(gram_kernel, n, part),
         out_shape=(
             jax.ShapeDtypeStruct((n, 3 * n), f32),
             jax.ShapeDtypeStruct((n, part * LANES), f32),
         ),
-        in_specs=[SMEM] + [VMEM] * 4,
+        in_specs=[SMEM] + [VMEM] * 5,
         out_specs=(VMEM, VMEM),
         compiler_params=pltpu.CompilerParams(vmem_limit_bytes=32 << 20),
         cost_estimate=pl.CostEstimate(flops=10**9, bytes_accessed=2 << 20, transcendentals=0),
-    )(group.reshape(1), x, tg, th, v)
+    )(group.reshape(1), x, tl, tu, th, v)
 
 
 def exact(left, right, dims):
@@ -223,6 +331,24 @@
     return own * (1.0 - STEP_SIZE * v) + both[:out_rows] + both[out_rows:]
 
 
+def eliminated(work, n):
+    ids = lax.broadcasted_iota(jnp.int32, (8, 1), 0)
+    blocks = [work[i : i + 8] for i in range(0, n, 8)]
+    for k in range(n):
+        at, inside = divmod(k, 8)
+        row = blocks[at][inside : inside + 1]
+        root = lax.rsqrt(row[:, k : k + 1])
+        row = row * root
+        for i in range(at, len(blocks)):
+            column = blocks[i][:, k : k + 1] * root
+            if i > at:
+                blocks[i] = blocks[i] - column * row
+            else:
+                lower = blocks[i] - jnp.where(ids > inside, column, 0.0) * row
+                blocks[i] = jnp.where(ids == inside, row, lower)
+    return jnp.concatenate(blocks, 0)
+
+
 def partner_kernel(n, part, out_rows, place_ref, g_ref, x_ref, t_ref, v_ref, out_ref, mix_ref, m_ref, r_ref):
     group = place_ref[0]
     ids = lax.broadcasted_iota(jnp.int32, (n, 1), 0)
@@ -239,7 +365,7 @@
         lower = work - jnp.where(ids > k, column * root, 0.0) * row
         return jnp.where(ids == k, row, lower)
 
-    work = lax.fori_loop(0, n, eliminate, work)
+    work = eliminated(work, n) if n <= 32 else lax.fori_loop(0, n, eliminate, work)
     pt = work[:, n : 2 * n]
     m_ref[...] = exact(pt, work[:, 2 * n :], ((0,), (0,)))
     r_ref[...] = g_ref[:, 2 * n :] - exact(pt, pt, ((0,), (0,)))
@@ -328,24 +454,29 @@
     near = moved(mine, ("orb",), lambda i: i ^ 2)
     mate = mates([own])
 
-    acc = pair_step(one, group, target, [own], mate, None, False, n_grp, n_orb)
-    near, acc = lax.optimization_barrier((near, acc))
+    def owned(value, start):
+        piece = value.reshape(n_orb, n_grp * part, LANES)[:, start : start + part]
+        return lax.all_to_all(piece, ("orb",), split_axis=0, concat_axis=0).reshape(HALF, LANES)
+
+    t_low = owned(target, 0)
+    near, token = lax.optimization_barrier((near, potential.reshape(-1, LANES)))
+    begun, token = pair_step(one, group, token, target, [[own], mate], [], False, n_grp, n_orb)
     far = moved(near, ("orb",), lambda i: (i + (-4 if i & 2 else 4)) % n_orb)
     near = [near, swapped(near)]
-    far, near, target = lax.optimization_barrier((far, near, target))
+    far, near, late, token, t_low = lax.optimization_barrier((far, near, target, token, t_low))
     far = [far, swapped(far)]
-    t_own = lax.all_to_all(target.reshape(n_orb, n_grp * part, LANES), ("orb",), split_axis=0, concat_axis=0)
-    acc = pair_step(crossed, group, target, near, mates(near), acc, False, n_grp, n_orb)
-    far, acc = lax.optimization_barrier((far, acc))
-    acc = pair_step(one - crossed, group, target, far, mates(far), acc, True, n_grp, n_orb)
-    acc, t_own = lax.optimization_barrier((acc, t_own))
-    t_other = swapped(lax.dynamic_slice_in_dim(t_own, (1 - group) * part, part, 1))
+    near_mate = mates(near)
+    t_high = owned(late, part)
+    going, token = single_step(group, token, target, near)
+    far, token = lax.optimization_barrier((far, token))
+    fields = [far, near_mate, mates(far)]
+    acc, token = pair_step(crossed, group, token, target, fields, [begun, going], True, n_grp, n_orb)
+    acc, t_low, t_high = lax.optimization_barrier((acc, t_low, t_high))
+    t_other = swapped(jnp.where(group == 0, t_high, t_low))
     x_half = spread(acc)
 
     v = lax.dynamic_slice_in_dim(potential.reshape(n_grp * part, LANES), group * part, part, 0)
-    gram, t_half = gram_step(
-        group, x_half, t_own.reshape(ROWS, LANES), t_other.reshape(ROWS // 2, LANES), v, n, part
-    )
+    gram, t_half = gram_step(group, x_half, t_low, t_high, t_other, v, n, part)
     rest = [b for b in (1 << k for k in range(2, 30)) if b < n_orb]
     for step in [[1], [2, n_orb]] + [rest[k : k + 2] for k in range(0, len(rest), 2)]:
         gram = summed_over(gram, step)

time: 130 us -> 128 us (0.985)
  starting transfers between devices: 31.6 us -> 35.7 us
  local copies, waits for them, and re-layouts: 9.99 us -> 6.04 us
  Pallas kernels: 34.3 us -> 31.4 us
    unnamed x30 -> x12, local copies, waits for them, and re-layouts: 8.04 us -> 2.47 us
    all_to_all x1 -> x2, starting transfers between devices: 6.16 us -> 10.2 us  [owned(): lax.all_to_all(piece, ('orb',), split_axis=0, concat_axis=0)]
    pallas_call x3, Pallas kernels: 25.8 us -> 23 us  [the longest x2 17.2 us: pair_step(): pl.pallas_call(functools.partial(pair_kernel, counts, len(accs), cut, n_g...]
    slice x0 -> x2, local copies, waits for them, and re-layouts: none -> 1.67 us  [owned(): piece = value.reshape(n_orb, n_grp * part, LANES)[:, start:start + part]]
  transfers between devices with their start and end apart: 20 -> 21, of which waited for: 13 -> 13; matrix products, arithmetic and copies ran while one was open for 1% -> 2% of each run, Pallas kernels for 21% -> 19%
where the time goes in v2:
time: 128 us
  waiting for transfers between devices  54.3 us (42%)
  starting transfers between devices  35.7 us (28%)
  Pallas kernels  31.4 us (25%)
  local copies, waits for them, and re-layouts  6.04 us (5%)
    ppermute x18, waiting for transfers between devices, moved(): return lax.ppermute(x, axes, [(i, target(i)) for i in range(size)])  51.4 us
    ppermute x18, starting transfers between devices, moved(): return lax.ppermute(x, axes, [(i, target(i)) for i in range(size)])  20.3 us
    pallas_call x2, Pallas kernels, pair_step(): pl.pallas_call(functools.partial(pair_kernel, counts, len(accs), cut, n_g...  17.2 us
    all_to_all x2, starting transfers between devices, owned(): lax.all_to_all(piece, ('orb',), split_axis=0, concat_axis=0)  10.2 us
    pallas_call x1, Pallas kernels, single_step(): pl.pallas_call(single_kernel, out_shape=(FIELD, TOKEN), in_specs=[SMEM] +...  5.8 us
    all_to_all x1, starting transfers between devices, spread(): lax.all_to_all(value.reshape(n, part, LANES), ('grp', 'orb'), split_axis=...  5.18 us
    pallas_call x1, Pallas kernels, partner_step(): pl.pallas_call(functools.partial(partner_kernel, n, part, out_rows), out_...  4.05 us
    all_to_all x1, waiting for transfers between devices, spread(): lax.all_to_all(value.reshape(n, part, LANES), ('grp', 'orb'), split_axis=...  2.92 us
  transfers between devices with their start and end apart: 21, of which 13 were waited for; matrix products, arithmetic and copies ran while one was open for 2% of the time, Pallas kernels for 19%

profile of v2, /device:TPU:0, one launch (start us, length us, event | category | flops | bytes accessed | tf_op | source)
XLA Modules:
  0.0 127.7 jit_solution(192011670017905600)
XLA Ops:
  0.0 0.0 copy-start
  0.0 0.5 collective-permute-start.3
  0.5 1.1 constant_dynamic-slice_fusion.1
  1.5 2.6 %collective-permute-start = (f32[1024,128]{1,0:T(8,128)S(1)}, f32[1024,128]{1,0:T(8,128)}, u32[]{:S(2)}, u32[]{:S(2)}) collective-permute-start(f32[1024,128]{1,0:T(8,128)S(1)} %constant_dynamic-slice_fusion.1), channel_id=1, source_target_pairs={{0,2},{1,3},{2,0},{3,1},{4,6},{5,7},{6,4},{7,5},{8,10},{9,11},{10,... | collective-permute-start | bytes 1572872 | tf_op jit(solution)/shard_map/ppermute | solution.py:423
  4.2 0.0 copy-done
  4.2 0.8 slice.8
  5.0 0.0 copy-start.2
  5.0 0.0 copy-start.3
  5.0 5.1 %all-to-all-start = ((f32[16,64,128]{2,1,0:T(8,128)}), f32[16,64,128]{2,1,0:T(8,128)S(1)}, u32[]{:S(2)}, u32[]{:S(2)}) async-start(f32[16,64,128]{2,1,0:T(8,128)} %slice.8), calls=%async_computation | async-start | bytes 1048576 | tf_op jit(solution)/shard_map/all_to_all | solution.py:459
  10.1 9.2 %collective-permute-done.own_ref = f32[1024,128]{1,0:T(8,128)} collective-permute-done((f32[1024,128]{1,0:T(8,128)S(1)}, f32[1024,128]{1,0:T(8,128)}, u32[]{:S(2)}, u32[]{:S(2)}) %collective-permute-start) | collective-permute-done | bytes 524320 | tf_op jit(solution)/shard_map/ppermute | solution.py:423
  19.3 1.8 %collective-permute-start.1 = (f32[1024,128]{1,0:T(8,128)}, f32[1024,128]{1,0:T(8,128)S(1)}, u32[]{:S(2)}, u32[]{:S(2)}) collective-permute-start(f32[1024,128]{1,0:T(8,128)} %collective-permute-done.own_ref), channel_id=1, source_target_pairs={{0,4},{1,5},{2,14},{3,15},{4,8},{5,9},{6,2},{7,3},{8,12},{9,13},{1... | collective-permute-start | bytes 1572872 | tf_op jit(solution)/shard_map/ppermute | solution.py:423
  21.1 1.5 %collective-permute-start.2 = (f32[1024,128]{1,0:T(8,128)}, f32[1024,128]{1,0:T(8,128)}, u32[]{:S(2)}, u32[]{:S(2)}) collective-permute-start(f32[1024,128]{1,0:T(8,128)} %collective-permute-done.own_ref), channel_id=1, source_target_pairs={{0,16},{16,0},{1,17},{17,1},{2,18},{18,2},{3,19},{19,3},{4,20},{20... | collective-permute-start | bytes 1572872 | tf_op jit(solution)/shard_map/ppermute | solution.py:423
  22.7 0.0 collective-permute-done.3.refs_1_
  22.7 0.0 copy-done.2
  22.7 0.0 copy-done.3
  22.7 0.0 copy-start.1
  22.7 1.2 copy-done.1
  23.9 7.5 %shard_map.64 = (f32[2048,128]{1,0:T(8,128)}, f32[8,128]{1,0:T(8,128)S(1)}) custom-call(f32[1]{0:T(128)} %constant.11.clone.1.flag_ref, s32[1]{0:T(128)} %bitcast.group_ref.place_ref, f32[128,128]{1,0:T(8,128)S(1)} %bitcast.26, bf16[448,256]{1,0:T(8,128)(2,1)S(1)} %copy-done.2, f32[2048,128]{1,0:T(8,128)S(1)} %bitcast.12, f32[2048,128]{1,0:T(8,128)S(1)} %bitcast.25, ...), custom_call_target="tpu_custom_call" | custom-call | flops 8000000000 | bytes 262144 | tf_op jit(solution)/shard_map/pallas_call | solution.py:250
  31.4 0.0 all-to-all-done
  31.5 4.4 %collective-permute-done.1.refs_0_ = f32[1024,128]{1,0:T(8,128)S(1)} collective-permute-done((f32[1024,128]{1,0:T(8,128)}, f32[1024,128]{1,0:T(8,128)S(1)}, u32[]{:S(2)}, u32[]{:S(2)}) %collective-permute-start.1) | collective-permute-done | bytes 524320 | tf_op jit(solution)/shard_map/ppermute | solution.py:423
  35.9 0.0 collective-permute-done.2.other_ref
  35.9 1.5 %collective-permute-start.4 = (f32[1024,128]{1,0:T(8,128)S(1)}, f32[1024,128]{1,0:T(8,128)S(1)}, u32[]{:S(2)}, u32[]{:S(2)}) collective-permute-start(f32[1024,128]{1,0:T(8,128)S(1)} %collective-permute-done.1.refs_0_), channel_id=1, source_target_pairs={{0,16},{16,0},{1,17},{17,1},{2,18},{18,2},{3,19},{19,3},{4,20},{20... | collective-permute-start | bytes 1572872 | tf_op jit(solution)/shard_map/ppermute | solution.py:423
  37.4 0.0 collective-permute-start.5
  37.4 0.5 collective-permute-start.6
  37.9 0.8 slice.9
  38.7 5.1 %all-to-all-start.1 = ((f32[16,64,128]{2,1,0:T(8,128)}), f32[16,64,128]{2,1,0:T(8,128)S(1)}, u32[]{:S(2)}, u32[]{:S(2)}) async-start(f32[16,64,128]{2,1,0:T(8,128)} %slice.9), calls=%async_computation.1 | async-start | bytes 1048576 | tf_op jit(solution)/shard_map/all_to_all | solution.py:459
  43.9 5.8 %shard_map.65 = (f32[2048,128]{1,0:T(8,128)}, f32[8,128]{1,0:T(8,128)S(1)}) custom-call(s32[1]{0:T(128)} %bitcast.group_ref.place_ref, f32[8,128]{1,0:T(8,128)S(1)} %get-tuple-element.32.earlier_ref, bf16[448,256]{1,0:T(8,128)(2,1)S(1)} %copy-done.2, f32[2048,128]{1,0:T(8,128)S(1)} %bitcast.14, f32[1024,128]{1,0:T(8,128)} %collective-permute-done.own_ref, ...), custom_call_target="tpu_custom_call" | custom-call | flops 10000000000 | bytes 4194304 | tf_op jit(solution)/shard_map/pallas_call | solution.py:265
  49.7 0.0 collective-permute-done.4.refs_1_
  49.7 0.5 collective-permute-start.7
  50.1 0.1 collective-permute-start.8
  50.3 0.0 collective-permute-done.5.refs_2_
  50.3 0.0 collective-permute-done.6.refs_3_
  50.3 1.6 %collective-permute-done.7.refs_4_ = f32[1024,128]{1,0:T(8,128)} collective-permute-done((f32[1024,128]{1,0:T(8,128)S(1)}, f32[1024,128]{1,0:T(8,128)}, u32[]{:S(2)}, u32[]{:S(2)}) %collective-permute-start.7) | collective-permute-done | bytes 524320 | tf_op jit(solution)/shard_map/ppermute | solution.py:423
  51.8 0.7 collective-permute-done.8.refs_5_
  52.6 9.7 %shard_map.66 = (f32[2048,128]{1,0:T(8,128)}, f32[8,128]{1,0:T(8,128)}) custom-call(f32[1]{0:T(128)} %bitcast.1.flag_ref, s32[1]{0:T(128)} %bitcast.group_ref.place_ref, f32[8,128]{1,0:T(8,128)S(1)} %get-tuple-element.36.earlier_ref, bf16[448,256]{1,0:T(8,128)(2,1)S(1)} %copy-done.2, f32[2048,128]{1,0:T(8,128)S(1)} %bitcast.15, ...), custom_call_target="tpu_custom_call" | custom-call | flops 100000000 | bytes 262144 | tf_op jit(solution)/shard_map/pallas_call | solution.py:250
  62.2 0.0 all-to-all-done.1
  62.2 5.2 %all-to-all-start.2 = ((f32[32,64,128]{2,1,0:T(8,128)}), f32[32,64,128]{2,1,0:T(8,128)S(1)}, u32[]{:S(2)}, u32[]{:S(2)}) async-start(f32[32,64,128]{2,1,0:T(8,128)} %bitcast.9), calls=%async_computation.2 | async-start | bytes 2097152 | tf_op jit(solution)/shard_map/all_to_all | solution.py:443
  67.4 0.1 broadcast_select_fusion
  67.5 1.6 %collective-permute-start.9 = (f32[1024,128]{1,0:T(8,128)S(1)}, f32[1024,128]{1,0:T(8,128)S(1)}, u32[]{:S(2)}, u32[]{:S(2)}) collective-permute-start(f32[1024,128]{1,0:T(8,128)S(1)} %broadcast_select_fusion), channel_id=1, source_target_pairs={{0,16},{16,0},{1,17},{17,1},{2,18},{18,2},{3,19},{19,3},{4,20},{20... | collective-permute-start | bytes 1572872 | tf_op jit(solution)/shard_map/ppermute | solution.py:423
  69.1 22.4 %collective-permute-done.9.th_ref = f32[1024,128]{1,0:T(8,128)S(1)} collective-permute-done((f32[1024,128]{1,0:T(8,128)S(1)}, f32[1024,128]{1,0:T(8,128)S(1)}, u32[]{:S(2)}, u32[]{:S(2)}) %collective-permute-start.9) | collective-permute-done | bytes 524320 | tf_op jit(solution)/shard_map/ppermute | solution.py:423
  91.5 2.9 %all-to-all-done.2 = f32[32,64,128]{2,1,0:T(8,128)S(1)} async-done(((f32[32,64,128]{2,1,0:T(8,128)}), f32[32,64,128]{2,1,0:T(8,128)S(1)}, u32[]{:S(2)}, u32[]{:S(2)}) %all-to-all-start.2) | async-done | bytes 1048608 | tf_op jit(solution)/shard_map/all_to_all | solution.py:443
  94.4 2.5 %shard_map.67 = (f32[32,96]{1,0:T(8,128)S(1)}, f32[32,8192]{1,0:T(8,128)S(1)}) custom-call(s32[1]{0:T(128)} %bitcast.group_ref.place_ref, f32[2048,128]{1,0:T(8,128)S(1)} %bitcast.20, f32[1024,128]{1,0:T(8,128)S(1)} %bitcast.17, f32[1024,128]{1,0:T(8,128)S(1)} %bitcast.19, f32[1024,128]{1,0:T(8,128)S(1)} %collective-permute-done.9.th_ref, ...), custom_call_target="tpu_custom_call" | custom-call | flops 1000000000 | bytes 2097152 | tf_op jit(solution)/shard_map/pallas_call | solution.py:304
  96.9 0.0 copy-start.4
  96.9 0.1 collective-permute-start.10
  97.0 1.2 collective-permute-done.10
  98.2 1.4 %collective-permute-start.11 = (f32[32,96]{1,0:T(8,128)S(1)}, f32[32,96]{1,0:T(8,128)S(1)}, u32[]{:S(2)}, u32[]{:S(2)}) collective-permute-start(f32[32,96]{1,0:T(8,128)S(1)} %add.32), channel_id=1, source_target_pairs={{0,2},{1,3},{2,0},{3,1},{4,6},{5,7},{6,4},{7,5},{8,10},{9,11},{10,... | collective-permute-start | bytes 36872 | tf_op jit(solution)/shard_map/ppermute | solution.py:423
  99.6 0.5 collective-permute-start.12
  100.1 1.5 %collective-permute-start.13 = (f32[32,96]{1,0:T(8,128)S(1)}, f32[32,96]{1,0:T(8,128)S(1)}, u32[]{:S(2)}, u32[]{:S(2)}) collective-permute-start(f32[32,96]{1,0:T(8,128)S(1)} %add.32), channel_id=1, source_target_pairs={{0,18},{1,19},{2,16},{3,17},{4,22},{5,23},{6,20},{7,21},{8,26},{9,... | collective-permute-start | bytes 36872 | tf_op jit(solution)/shard_map/ppermute | solution.py:423
  101.6 0.2 collective-permute-done.11
  101.9 1.6 %collective-permute-done.12 = f32[32,96]{1,0:T(8,128)S(1)} collective-permute-done((f32[32,96]{1,0:T(8,128)S(1)}, f32[32,96]{1,0:T(8,128)S(1)}, u32[]{:S(2)}, u32[]{:S(2)}) %collective-permute-start.12) | collective-permute-done | bytes 12320 | tf_op jit(solution)/shard_map/ppermute | solution.py:423
  103.5 1.3 collective-permute-done.13
  104.8 0.0 collective-permute-start.14
  104.8 1.8 %collective-permute-start.15 = (f32[32,96]{1,0:T(8,128)S(1)}, f32[32,96]{1,0:T(8,128)S(1)}, u32[]{:S(2)}, u32[]{:S(2)}) collective-permute-start(f32[32,96]{1,0:T(8,128)S(1)} %add_add_fusion.1), channel_id=1, source_target_pairs={{0,8},{1,9},{2,10},{3,11},{4,12},{5,13},{6,14},{7,15},{8,0},{9,1},... | collective-permute-start | bytes 36872 | tf_op jit(solution)/shard_map/ppermute | solution.py:423
  106.6 2.6 %collective-permute-start.16 = (f32[32,96]{1,0:T(8,128)S(1)}, f32[32,96]{1,0:T(8,128)S(1)}, u32[]{:S(2)}, u32[]{:S(2)}) collective-permute-start(f32[32,96]{1,0:T(8,128)S(1)} %add_add_fusion.1), channel_id=1, source_target_pairs={{0,12},{1,13},{2,14},{3,15},{4,8},{5,9},{6,10},{7,11},{8,4},{9,5},... | collective-permute-start | bytes 36872 | tf_op jit(solution)/shard_map/ppermute | solution.py:423
  109.2 0.0 collective-permute-done.14
  109.2 0.3 collective-permute-done.15
  109.5 2.7 %collective-permute-done.16 = f32[32,96]{1,0:T(8,128)S(1)} collective-permute-done((f32[32,96]{1,0:T(8,128)S(1)}, f32[32,96]{1,0:T(8,128)S(1)}, u32[]{:S(2)}, u32[]{:S(2)}) %collective-permute-start.16) | collective-permute-done | bytes 12320 | tf_op jit(solution)/shard_map/ppermute | solution.py:423
  112.2 4.1 %shard_map.68 = (f32[16,8192]{1,0:T(8,128)S(1)}, bf16[32,128]{1,0:T(8,128)(2,1)S(1)}) custom-call(s32[1]{0:T(128)} %bitcast.group_ref.place_ref, f32[32,96]{1,0:T(8,128)S(1)} %add_add_fusion.g_ref, f32[2048,128]{1,0:T(8,128)S(1)} %bitcast.21, f32[32,8192]{1,0:T(8,128)S(1)} %get-tuple-element.48.t_ref, f32[64,128]{1,0:T(8,128)S(1)} %constant_dynamic-slice_fusion.v_ref), custom_call_target="tpu_custom_call" | custom-call | flops 4000000000 | bytes 2097152 | tf_op jit(solution)/shard_map/pallas_call | solution.py:385
  116.2 0.0 copy-done.4
  116.2 1.7 %collective-permute-start.17 = (f32[16,8192]{1,0:T(8,128)S(1)}, f32[16,8192]{1,0:T(8,128)S(1)}, u32[]{:S(2)}, u32[]{:S(2)}) collective-permute-start(f32[16,8192]{1,0:T(8,128)S(1)} %get-tuple-element.50), channel_id=1, source_target_pairs={{0,16},{16,0},{1,17},{17,1},{2,18},{18,2},{3,19},{19,3},{4,20},{20... | collective-permute-start | bytes 1572872 | tf_op jit(solution)/shard_map/ppermute | solution.py:423
  117.9 1.2 copy-done.5
  119.2 1.8 %shard_map.69 = f32[16,16384]{1,0:T(8,128)} custom-call(s32[1]{0:T(128)} %bitcast.group_ref.place_ref, bf16[32,128]{1,0:T(8,128)(2,1)S(1)} %get-tuple-element.49.mix_ref, f32[2048,128]{1,0:T(8,128)S(1)} %bitcast.22, f32[32,8192]{1,0:T(8,128)S(1)} %copy-done.5, f32[64,128]{1,0:T(8,128)S(1)} %constant_dynamic-slice_fusion.v_ref), custom_call_target="tpu_custom_call" | custom-call | flops 4000000000 | bytes 2097152 | tf_op jit(solution)/shard_map/pallas_call | solution.py:409
  121.0 5.9 %collective-permute-done.17 = f32[16,8192]{1,0:T(8,128)S(1)} collective-permute-done((f32[16,8192]{1,0:T(8,128)S(1)}, f32[16,8192]{1,0:T(8,128)S(1)}, u32[]{:S(2)}, u32[]{:S(2)}) %collective-permute-start.17) | collective-permute-done | bytes 524320 | tf_op jit(solution)/shard_map/ppermute | solution.py:423
  126.9 0.8 constant_dynamic-update-slice_fusion
  (5 shorter events, 0.0 us)
Async XLA Ops:
  0.0 4.2 %copy-start = (f32[1,262144]{1,0:T(1,128)S(1)}, f32[1,262144]{1,0:T(1,128)}, u32[]{:S(2)}) copy-start(f32[1,262144]{1,0:T(1,128)} %param.7) | copy-start | bytes 3145732
  0.0 22.7 %collective-permute-start.3 = (f32[2048,128]{1,0:T(8,128)}, f32[2048,128]{1,0:T(8,128)}, u32[]{:S(2)}, u32[]{:S(2)}) collective-permute-start(f32[2048,128]{1,0:T(8,128)} %bitcast.23), channel_id=1, source_target_pairs={{0,1},{1,0},{2,3},{3,2},{4,5},{5,4},{6,7},{7,6},{8,9},{9,8},{10,11... | collective-permute-start | bytes 3145736 | tf_op jit(solution)/shard_map/ppermute | solution.py:423
  1.5 17.8 %collective-permute-start = (f32[1024,128]{1,0:T(8,128)S(1)}, f32[1024,128]{1,0:T(8,128)}, u32[]{:S(2)}, u32[]{:S(2)}) collective-permute-start(f32[1024,128]{1,0:T(8,128)S(1)} %constant_dynamic-slice_fusion.1), channel_id=1, source_target_pairs={{0,2},{1,3},{2,0},{3,1},{4,6},{5,7},{6,4},{7,5},{8,10},{9,11},{10,... | collective-permute-start | bytes 1572872 | tf_op jit(solution)/shard_map/ppermute | solution.py:423
  5.0 17.6 %copy-start.2 = (bf16[448,256]{1,0:T(8,128)(2,1)S(1)}, bf16[448,256]{1,0:T(8,128)(2,1)}, u32[]{:S(2)}) copy-start(bf16[448,256]{1,0:T(8,128)(2,1)} %constant.29.clone.table_ref) | copy-start | bytes 688132
  5.0 17.6 %copy-start.3 = (f32[16384]{0:T(1024)S(1)}, f32[16384]{0:T(1024)}, u32[]{:S(2)}) copy-start(f32[16384]{0:T(1024)} %param.8) | copy-start | bytes 196612
  5.0 26.4 %all-to-all-start = ((f32[16,64,128]{2,1,0:T(8,128)}), f32[16,64,128]{2,1,0:T(8,128)S(1)}, u32[]{:S(2)}, u32[]{:S(2)}) async-start(f32[16,64,128]{2,1,0:T(8,128)} %slice.8), calls=%async_computation | async-start | bytes 1048576 | tf_op jit(solution)/shard_map/all_to_all | solution.py:459
  19.3 16.6 %collective-permute-start.1 = (f32[1024,128]{1,0:T(8,128)}, f32[1024,128]{1,0:T(8,128)S(1)}, u32[]{:S(2)}, u32[]{:S(2)}) collective-permute-start(f32[1024,128]{1,0:T(8,128)} %collective-permute-done.own_ref), channel_id=1, source_target_pairs={{0,4},{1,5},{2,14},{3,15},{4,8},{5,9},{6,2},{7,3},{8,12},{9,13},{1... | collective-permute-start | bytes 1572872 | tf_op jit(solution)/shard_map/ppermute | solution.py:423
  21.1 14.7 %collective-permute-start.2 = (f32[1024,128]{1,0:T(8,128)}, f32[1024,128]{1,0:T(8,128)}, u32[]{:S(2)}, u32[]{:S(2)}) collective-permute-start(f32[1024,128]{1,0:T(8,128)} %collective-permute-done.own_ref), channel_id=1, source_target_pairs={{0,16},{16,0},{1,17},{17,1},{2,18},{18,2},{3,19},{19,3},{4,20},{20... | collective-permute-start | bytes 1572872 | tf_op jit(solution)/shard_map/ppermute | solution.py:423
  22.7 1.2 copy-start.1
  35.9 13.8 %collective-permute-start.4 = (f32[1024,128]{1,0:T(8,128)S(1)}, f32[1024,128]{1,0:T(8,128)S(1)}, u32[]{:S(2)}, u32[]{:S(2)}) collective-permute-start(f32[1024,128]{1,0:T(8,128)S(1)} %collective-permute-done.1.refs_0_), channel_id=1, source_target_pairs={{0,16},{16,0},{1,17},{17,1},{2,18},{18,2},{3,19},{19,3},{4,20},{20... | collective-permute-start | bytes 1572872 | tf_op jit(solution)/shard_map/ppermute | solution.py:423
  37.4 12.9 %collective-permute-start.5 = (f32[1024,128]{1,0:T(8,128)}, f32[1024,128]{1,0:T(8,128)}, u32[]{:S(2)}, u32[]{:S(2)}) collective-permute-start(f32[1024,128]{1,0:T(8,128)} %collective-permute-done.own_ref), channel_id=1, source_target_pairs={{0,1},{1,0},{2,3},{3,2},{4,5},{5,4},{6,7},{7,6},{8,9},{9,8},{10,11... | collective-permute-start | bytes 1572872 | tf_op jit(solution)/shard_map/ppermute | solution.py:423
  37.4 12.9 %collective-permute-start.6 = (f32[1024,128]{1,0:T(8,128)}, f32[1024,128]{1,0:T(8,128)}, u32[]{:S(2)}, u32[]{:S(2)}) collective-permute-start(f32[1024,128]{1,0:T(8,128)} %collective-permute-done.2.other_ref), channel_id=1, source_target_pairs={{0,1},{1,0},{2,3},{3,2},{4,5},{5,4},{6,7},{7,6},{8,9},{9,8},{10,11... | collective-permute-start | bytes 1572872 | tf_op jit(solution)/shard_map/ppermute | solution.py:423
  38.7 23.5 %all-to-all-start.1 = ((f32[16,64,128]{2,1,0:T(8,128)}), f32[16,64,128]{2,1,0:T(8,128)S(1)}, u32[]{:S(2)}, u32[]{:S(2)}) async-start(f32[16,64,128]{2,1,0:T(8,128)} %slice.9), calls=%async_computation.1 | async-start | bytes 1048576 | tf_op jit(solution)/shard_map/all_to_all | solution.py:459
  49.7 2.1 %collective-permute-start.7 = (f32[1024,128]{1,0:T(8,128)S(1)}, f32[1024,128]{1,0:T(8,128)}, u32[]{:S(2)}, u32[]{:S(2)}) collective-permute-start(f32[1024,128]{1,0:T(8,128)S(1)} %collective-permute-done.1.refs_0_), channel_id=1, source_target_pairs={{0,1},{1,0},{2,3},{3,2},{4,5},{5,4},{6,7},{7,6},{8,9},{9,8},{10,11... | collective-permute-start | bytes 1572872 | tf_op jit(solution)/shard_map/ppermute | solution.py:423
  50.1 2.4 %collective-permute-start.8 = (f32[1024,128]{1,0:T(8,128)S(1)}, f32[1024,128]{1,0:T(8,128)}, u32[]{:S(2)}, u32[]{:S(2)}) collective-permute-start(f32[1024,128]{1,0:T(8,128)S(1)} %collective-permute-done.4.refs_1_), channel_id=1, source_target_pairs={{0,1},{1,0},{2,3},{3,2},{4,5},{5,4},{6,7},{7,6},{8,9},{9,8},{10,11... | collective-permute-start | bytes 1572872 | tf_op jit(solution)/shard_map/ppermute | solution.py:423
  62.2 32.2 %all-to-all-start.2 = ((f32[32,64,128]{2,1,0:T(8,128)}), f32[32,64,128]{2,1,0:T(8,128)S(1)}, u32[]{:S(2)}, u32[]{:S(2)}) async-start(f32[32,64,128]{2,1,0:T(8,128)} %bitcast.9), calls=%async_computation.2 | async-start | bytes 2097152 | tf_op jit(solution)/shard_map/all_to_all | solution.py:443
  67.5 24.0 %collective-permute-start.9 = (f32[1024,128]{1,0:T(8,128)S(1)}, f32[1024,128]{1,0:T(8,128)S(1)}, u32[]{:S(2)}, u32[]{:S(2)}) collective-permute-start(f32[1024,128]{1,0:T(8,128)S(1)} %broadcast_select_fusion), channel_id=1, source_target_pairs={{0,16},{16,0},{1,17},{17,1},{2,18},{18,2},{3,19},{19,3},{4,20},{20... | collective-permute-start | bytes 1572872 | tf_op jit(solution)/shard_map/ppermute | solution.py:423
  96.9 19.3 %copy-start.4 = (f32[32,8192]{1,0:T(8,128)}, f32[32,8192]{1,0:T(8,128)S(1)}, u32[]{:S(2)}) copy-start(f32[32,8192]{1,0:T(8,128)S(1)} %get-tuple-element.48.t_ref) | copy-start | bytes 3145732
  96.9 1.2 collective-permute-start.10
  98.2 3.7 %collective-permute-start.11 = (f32[32,96]{1,0:T(8,128)S(1)}, f32[32,96]{1,0:T(8,128)S(1)}, u32[]{:S(2)}, u32[]{:S(2)}) collective-permute-start(f32[32,96]{1,0:T(8,128)S(1)} %add.32), channel_id=1, source_target_pairs={{0,2},{1,3},{2,0},{3,1},{4,6},{5,7},{6,4},{7,5},{8,10},{9,11},{10,... | collective-permute-start | bytes 36872 | tf_op jit(solution)/shard_map/ppermute | solution.py:423
  99.6 3.9 %collective-permute-start.12 = (f32[32,96]{1,0:T(8,128)S(1)}, f32[32,96]{1,0:T(8,128)S(1)}, u32[]{:S(2)}, u32[]{:S(2)}) collective-permute-start(f32[32,96]{1,0:T(8,128)S(1)} %add.32), channel_id=1, source_target_pairs={{0,16},{1,17},{2,18},{3,19},{4,20},{5,21},{6,22},{7,23},{8,24},{9,... | collective-permute-start | bytes 36872 | tf_op jit(solution)/shard_map/ppermute | solution.py:423
  100.1 4.6 %collective-permute-start.13 = (f32[32,96]{1,0:T(8,128)S(1)}, f32[32,96]{1,0:T(8,128)S(1)}, u32[]{:S(2)}, u32[]{:S(2)}) collective-permute-start(f32[32,96]{1,0:T(8,128)S(1)} %add.32), channel_id=1, source_target_pairs={{0,18},{1,19},{2,16},{3,17},{4,22},{5,23},{6,20},{7,21},{8,26},{9,... | collective-permute-start | bytes 36872 | tf_op jit(solution)/shard_map/ppermute | solution.py:423
  104.8 4.4 %collective-permute-start.14 = (f32[32,96]{1,0:T(8,128)S(1)}, f32[32,96]{1,0:T(8,128)S(1)}, u32[]{:S(2)}, u32[]{:S(2)}) collective-permute-start(f32[32,96]{1,0:T(8,128)S(1)} %add_add_fusion.1), channel_id=1, source_target_pairs={{0,4},{1,5},{2,6},{3,7},{4,0},{5,1},{6,2},{7,3},{8,12},{9,13},{10,... | collective-permute-start | bytes 36872 | tf_op jit(solution)/shard_map/ppermute | solution.py:423
  104.8 4.7 %collective-permute-start.15 = (f32[32,96]{1,0:T(8,128)S(1)}, f32[32,96]{1,0:T(8,128)S(1)}, u32[]{:S(2)}, u32[]{:S(2)}) collective-permute-start(f32[32,96]{1,0:T(8,128)S(1)} %add_add_fusion.1), channel_id=1, source_target_pairs={{0,8},{1,9},{2,10},{3,11},{4,12},{5,13},{6,14},{7,15},{8,0},{9,1},... | collective-permute-start | bytes 36872 | tf_op jit(solution)/shard_map/ppermute | solution.py:423
  106.6 5.5 %collective-permute-start.16 = (f32[32,96]{1,0:T(8,128)S(1)}, f32[32,96]{1,0:T(8,128)S(1)}, u32[]{:S(2)}, u32[]{:S(2)}) collective-permute-start(f32[32,96]{1,0:T(8,128)S(1)} %add_add_fusion.1), channel_id=1, source_target_pairs={{0,12},{1,13},{2,14},{3,15},{4,8},{5,9},{6,10},{7,11},{8,4},{9,5},... | collective-permute-start | bytes 36872 | tf_op jit(solution)/shard_map/ppermute | solution.py:423
  116.2 10.6 %collective-permute-start.17 = (f32[16,8192]{1,0:T(8,128)S(1)}, f32[16,8192]{1,0:T(8,128)S(1)}, u32[]{:S(2)}, u32[]{:S(2)}) collective-permute-start(f32[16,8192]{1,0:T(8,128)S(1)} %get-tuple-element.50), channel_id=1, source_target_pairs={{0,16},{16,0},{1,17},{17,1},{2,18},{18,2},{3,19},{19,3},{4,20},{20... | collective-permute-start | bytes 1572872 | tf_op jit(solution)/shard_map/ppermute | solution.py:423
  117.9 1.2 copy-start.5

commit v3 on v2

--- a/solution.py
+++ b/solution.py
@@ -135,8 +135,8 @@
     refs = list(refs)
     groups = [[refs.pop(0) for _ in range(count)] for count in counts]
     acc_refs = [refs.pop(0) for _ in range(n_acc)]
-    out_ref, token_ref, s_ref, s2_ref, out_buf, out_sems = refs[:6]
-    acc_bufs, acc_sems = refs[6:-1], refs[-1]
+    out_ref, token_ref, s_ref, s2_ref, kept_ref, out_buf, out_sems = refs[:7]
+    acc_bufs, acc_sems = refs[7:-1], refs[-1]
     token_ref[...] = earlier_ref[:8, :]
     loads = [
         pltpu.make_async_copy(ref, buf, acc_sems.at[i])
@@ -156,6 +156,7 @@
 
     t = t_ref[...]
     a, b = fields()
+    kept_ref[0], kept_ref[1] = a, b
     forward_zy(first, t * a, t * b, along_z, along_y, s_ref)
 
     base = kernel_base()
@@ -169,12 +170,11 @@
 
     for load in loads:
         load.wait()
-    a, b = fields()
     stores = []
     for c in range(NGRID // GROUP):
         rows = slice(c * GROUP * SLAB, (c + 1) * GROUP * SLAB)
         sa, sb = backward_yz(first, c * GROUP, GROUP, NGRID, back_y, along_z, s2_ref)
-        added = -(a[rows] * sa + b[rows] * sb)
+        added = -(kept_ref[0, rows, :] * sa + kept_ref[1, rows, :] * sb)
         for buf in acc_bufs:
             added = added + buf[rows, :]
         if cut:
@@ -253,6 +253,7 @@
         in_specs=[SMEM] * 2 + [VMEM] * len(operands) + [ANY] * len(accs),
         out_specs=(VMEM if cut else ANY, VMEM),
         scratch_shapes=[pltpu.VMEM((NGRID * NGRID, LANES), f32)] * 2
+        + [pltpu.VMEM((2, ROWS, LANES), f32)]
         + [pltpu.VMEM((ROWS, LANES), f32), pltpu.SemaphoreType.DMA((2,))]
         + [pltpu.VMEM((ROWS, LANES), f32)] * len(accs)
         + [pltpu.SemaphoreType.DMA((max(len(accs), 1),))],
@@ -478,7 +479,7 @@
     v = lax.dynamic_slice_in_dim(potential.reshape(n_grp * part, LANES), group * part, part, 0)
     gram, t_half = gram_step(group, x_half, t_low, t_high, t_other, v, n, part)
     rest = [b for b in (1 << k for k in range(2, 30)) if b < n_orb]
-    for step in [[1], [2, n_orb]] + [rest[k : k + 2] for k in range(0, len(rest), 2)]:
+    for step in [[1]] + [rest[k : k + 2] for k in range(0, len(rest), 2)] + [[2, n_orb]]:
         gram = summed_over(gram, step)
     partner, mix = partner_step(group, gram, x_half, t_half, v, n, part, n_orb)
     update = own_step(group, mix, x_half, t_half, v, n, part, n_orb)

time: 128 us -> 128 us (level)
  no operation moved by 1% of the time
where the time goes in v3:
time: 128 us
  waiting for transfers between devices  54.4 us (42%)
  starting transfers between devices  35.8 us (28%)
  Pallas kernels  31.3 us (24%)
  local copies, waits for them, and re-layouts  6.04 us (5%)
    ppermute x18, waiting for transfers between devices, moved(): return lax.ppermute(x, axes, [(i, target(i)) for i in range(size)])  51.4 us
    ppermute x18, starting transfers between devices, moved(): return lax.ppermute(x, axes, [(i, target(i)) for i in range(size)])  20.3 us
    pallas_call x2, Pallas kernels, pair_step(): pl.pallas_call(functools.partial(pair_kernel, counts, len(accs), cut, n_g...  17.1 us
    all_to_all x2, starting transfers between devices, owned(): lax.all_to_all(piece, ('orb',), split_axis=0, concat_axis=0)  10.2 us
    pallas_call x1, Pallas kernels, single_step(): pl.pallas_call(single_kernel, out_shape=(FIELD, TOKEN), in_specs=[SMEM] +...  5.8 us
    all_to_all x1, starting transfers between devices, spread(): lax.all_to_all(value.reshape(n, part, LANES), ('grp', 'orb'), split_axis=...  5.18 us
    pallas_call x1, Pallas kernels, partner_step(): pl.pallas_call(functools.partial(partner_kernel, n, part, out_rows), out_...  4.05 us
    all_to_all x1, waiting for transfers between devices, spread(): lax.all_to_all(value.reshape(n, part, LANES), ('grp', 'orb'), split_axis=...  2.92 us
  transfers between devices with their start and end apart: 21, of which 13 were waited for; matrix products, arithmetic and copies ran while one was open for 2% of the time, Pallas kernels for 19%

profile of v3, /device:TPU:0, one launch (start us, length us, event | category | flops | bytes accessed | tf_op | source)
XLA Modules:
  0.0 127.7 jit_solution(11572756257829515647)
XLA Ops:
  0.0 0.0 copy-start
  0.0 0.5 collective-permute-start.3
  0.5 1.1 constant_dynamic-slice_fusion.1
  1.5 2.6 %collective-permute-start = (f32[1024,128]{1,0:T(8,128)S(1)}, f32[1024,128]{1,0:T(8,128)}, u32[]{:S(2)}, u32[]{:S(2)}) collective-permute-start(f32[1024,128]{1,0:T(8,128)S(1)} %constant_dynamic-slice_fusion.1), channel_id=1, source_target_pairs={{0,2},{1,3},{2,0},{3,1},{4,6},{5,7},{6,4},{7,5},{8,10},{9,11},{10,... | collective-permute-start | bytes 1572872 | tf_op jit(solution)/shard_map/ppermute | solution.py:424
  4.2 0.0 copy-done
  4.2 0.8 slice.8
  5.0 0.0 copy-start.2
  5.0 0.0 copy-start.3
  5.0 5.1 %all-to-all-start = ((f32[16,64,128]{2,1,0:T(8,128)}), f32[16,64,128]{2,1,0:T(8,128)S(1)}, u32[]{:S(2)}, u32[]{:S(2)}) async-start(f32[16,64,128]{2,1,0:T(8,128)} %slice.8), calls=%async_computation | async-start | bytes 1048576 | tf_op jit(solution)/shard_map/all_to_all | solution.py:460
  10.1 9.2 %collective-permute-done.own_ref = f32[1024,128]{1,0:T(8,128)} collective-permute-done((f32[1024,128]{1,0:T(8,128)S(1)}, f32[1024,128]{1,0:T(8,128)}, u32[]{:S(2)}, u32[]{:S(2)}) %collective-permute-start) | collective-permute-done | bytes 524320 | tf_op jit(solution)/shard_map/ppermute | solution.py:424
  19.3 1.8 %collective-permute-start.1 = (f32[1024,128]{1,0:T(8,128)}, f32[1024,128]{1,0:T(8,128)S(1)}, u32[]{:S(2)}, u32[]{:S(2)}) collective-permute-start(f32[1024,128]{1,0:T(8,128)} %collective-permute-done.own_ref), channel_id=1, source_target_pairs={{0,4},{1,5},{2,14},{3,15},{4,8},{5,9},{6,2},{7,3},{8,12},{9,13},{1... | collective-permute-start | bytes 1572872 | tf_op jit(solution)/shard_map/ppermute | solution.py:424
  21.1 1.5 %collective-permute-start.2 = (f32[1024,128]{1,0:T(8,128)}, f32[1024,128]{1,0:T(8,128)}, u32[]{:S(2)}, u32[]{:S(2)}) collective-permute-start(f32[1024,128]{1,0:T(8,128)} %collective-permute-done.own_ref), channel_id=1, source_target_pairs={{0,16},{16,0},{1,17},{17,1},{2,18},{18,2},{3,19},{19,3},{4,20},{20... | collective-permute-start | bytes 1572872 | tf_op jit(solution)/shard_map/ppermute | solution.py:424
  22.7 0.0 collective-permute-done.3.refs_1_
  22.7 0.0 copy-done.2
  22.7 0.0 copy-done.3
  22.7 0.0 copy-start.1
  22.7 1.2 copy-done.1
  23.9 7.5 %shard_map.64 = (f32[2048,128]{1,0:T(8,128)}, f32[8,128]{1,0:T(8,128)S(1)}) custom-call(f32[1]{0:T(128)} %constant.11.clone.1.flag_ref, s32[1]{0:T(128)} %bitcast.group_ref.place_ref, f32[128,128]{1,0:T(8,128)S(1)} %bitcast.26, bf16[448,256]{1,0:T(8,128)(2,1)S(1)} %copy-done.2, f32[2048,128]{1,0:T(8,128)S(1)} %bitcast.12, f32[2048,128]{1,0:T(8,128)S(1)} %bitcast.25, ...), custom_call_target="tpu_custom_call" | custom-call | flops 8000000000 | bytes 262144 | tf_op jit(solution)/shard_map/pallas_call | solution.py:250
  31.4 0.0 all-to-all-done
  31.5 4.4 %collective-permute-done.1.refs_0_ = f32[1024,128]{1,0:T(8,128)S(1)} collective-permute-done((f32[1024,128]{1,0:T(8,128)}, f32[1024,128]{1,0:T(8,128)S(1)}, u32[]{:S(2)}, u32[]{:S(2)}) %collective-permute-start.1) | collective-permute-done | bytes 524320 | tf_op jit(solution)/shard_map/ppermute | solution.py:424
  35.9 0.0 collective-permute-done.2.other_ref
  35.9 1.5 %collective-permute-start.4 = (f32[1024,128]{1,0:T(8,128)S(1)}, f32[1024,128]{1,0:T(8,128)S(1)}, u32[]{:S(2)}, u32[]{:S(2)}) collective-permute-start(f32[1024,128]{1,0:T(8,128)S(1)} %collective-permute-done.1.refs_0_), channel_id=1, source_target_pairs={{0,16},{16,0},{1,17},{17,1},{2,18},{18,2},{3,19},{19,3},{4,20},{20... | collective-permute-start | bytes 1572872 | tf_op jit(solution)/shard_map/ppermute | solution.py:424
  37.4 0.0 collective-permute-start.5
  37.4 0.5 collective-permute-start.6
  37.9 0.8 slice.9
  38.7 5.1 %all-to-all-start.1 = ((f32[16,64,128]{2,1,0:T(8,128)}), f32[16,64,128]{2,1,0:T(8,128)S(1)}, u32[]{:S(2)}, u32[]{:S(2)}) async-start(f32[16,64,128]{2,1,0:T(8,128)} %slice.9), calls=%async_computation.1 | async-start | bytes 1048576 | tf_op jit(solution)/shard_map/all_to_all | solution.py:460
  43.9 5.8 %shard_map.65 = (f32[2048,128]{1,0:T(8,128)}, f32[8,128]{1,0:T(8,128)S(1)}) custom-call(s32[1]{0:T(128)} %bitcast.group_ref.place_ref, f32[8,128]{1,0:T(8,128)S(1)} %get-tuple-element.32.earlier_ref, bf16[448,256]{1,0:T(8,128)(2,1)S(1)} %copy-done.2, f32[2048,128]{1,0:T(8,128)S(1)} %bitcast.14, f32[1024,128]{1,0:T(8,128)} %collective-permute-done.own_ref, ...), custom_call_target="tpu_custom_call" | custom-call | flops 10000000000 | bytes 4194304 | tf_op jit(solution)/shard_map/pallas_call | solution.py:266
  49.7 0.0 collective-permute-done.4.refs_1_
  49.7 0.5 collective-permute-start.7
  50.1 0.1 collective-permute-start.8
  50.3 0.0 collective-permute-done.5.refs_2_
  50.3 0.0 collective-permute-done.6.refs_3_
  50.3 1.6 %collective-permute-done.7.refs_4_ = f32[1024,128]{1,0:T(8,128)} collective-permute-done((f32[1024,128]{1,0:T(8,128)S(1)}, f32[1024,128]{1,0:T(8,128)}, u32[]{:S(2)}, u32[]{:S(2)}) %collective-permute-start.7) | collective-permute-done | bytes 524320 | tf_op jit(solution)/shard_map/ppermute | solution.py:424
  51.8 0.7 collective-permute-done.8.refs_5_
  52.6 9.6 %shard_map.66 = (f32[2048,128]{1,0:T(8,128)}, f32[8,128]{1,0:T(8,128)}) custom-call(f32[1]{0:T(128)} %bitcast.1.flag_ref, s32[1]{0:T(128)} %bitcast.group_ref.place_ref, f32[8,128]{1,0:T(8,128)S(1)} %get-tuple-element.36.earlier_ref, bf16[448,256]{1,0:T(8,128)(2,1)S(1)} %copy-done.2, f32[2048,128]{1,0:T(8,128)S(1)} %bitcast.15, ...), custom_call_target="tpu_custom_call" | custom-call | flops 100000000 | bytes 262144 | tf_op jit(solution)/shard_map/pallas_call | solution.py:250
  62.2 0.0 all-to-all-done.1
  62.2 5.2 %all-to-all-start.2 = ((f32[32,64,128]{2,1,0:T(8,128)}), f32[32,64,128]{2,1,0:T(8,128)S(1)}, u32[]{:S(2)}, u32[]{:S(2)}) async-start(f32[32,64,128]{2,1,0:T(8,128)} %bitcast.9), calls=%async_computation.2 | async-start | bytes 2097152 | tf_op jit(solution)/shard_map/all_to_all | solution.py:444
  67.4 0.1 broadcast_select_fusion
  67.4 1.6 %collective-permute-start.9 = (f32[1024,128]{1,0:T(8,128)S(1)}, f32[1024,128]{1,0:T(8,128)S(1)}, u32[]{:S(2)}, u32[]{:S(2)}) collective-permute-start(f32[1024,128]{1,0:T(8,128)S(1)} %broadcast_select_fusion), channel_id=1, source_target_pairs={{0,16},{16,0},{1,17},{17,1},{2,18},{18,2},{3,19},{19,3},{4,20},{20... | collective-permute-start | bytes 1572872 | tf_op jit(solution)/shard_map/ppermute | solution.py:424
  69.1 22.4 %collective-permute-done.9.th_ref = f32[1024,128]{1,0:T(8,128)S(1)} collective-permute-done((f32[1024,128]{1,0:T(8,128)S(1)}, f32[1024,128]{1,0:T(8,128)S(1)}, u32[]{:S(2)}, u32[]{:S(2)}) %collective-permute-start.9) | collective-permute-done | bytes 524320 | tf_op jit(solution)/shard_map/ppermute | solution.py:424
  91.4 2.9 %all-to-all-done.2 = f32[32,64,128]{2,1,0:T(8,128)S(1)} async-done(((f32[32,64,128]{2,1,0:T(8,128)}), f32[32,64,128]{2,1,0:T(8,128)S(1)}, u32[]{:S(2)}, u32[]{:S(2)}) %all-to-all-start.2) | async-done | bytes 1048608 | tf_op jit(solution)/shard_map/all_to_all | solution.py:444
  94.3 2.5 %shard_map.67 = (f32[32,96]{1,0:T(8,128)S(1)}, f32[32,8192]{1,0:T(8,128)S(1)}) custom-call(s32[1]{0:T(128)} %bitcast.group_ref.place_ref, f32[2048,128]{1,0:T(8,128)S(1)} %bitcast.20, f32[1024,128]{1,0:T(8,128)S(1)} %bitcast.17, f32[1024,128]{1,0:T(8,128)S(1)} %bitcast.19, f32[1024,128]{1,0:T(8,128)S(1)} %collective-permute-done.9.th_ref, ...), custom_call_target="tpu_custom_call" | custom-call | flops 1000000000 | bytes 2097152 | tf_op jit(solution)/shard_map/pallas_call | solution.py:305
  96.8 0.0 copy-start.4
  96.8 0.1 collective-permute-start.10
  96.9 1.2 collective-permute-done.10
  98.1 0.2 collective-permute-start.11
  98.2 2.0 %collective-permute-start.12 = (f32[32,96]{1,0:T(8,128)S(1)}, f32[32,96]{1,0:T(8,128)S(1)}, u32[]{:S(2)}, u32[]{:S(2)}) collective-permute-start(f32[32,96]{1,0:T(8,128)S(1)} %add.32), channel_id=1, source_target_pairs={{0,8},{1,9},{2,10},{3,11},{4,12},{5,13},{6,14},{7,15},{8,0},{9,1},... | collective-permute-start | bytes 36872 | tf_op jit(solution)/shard_map/ppermute | solution.py:424
  100.2 2.3 %collective-permute-start.13 = (f32[32,96]{1,0:T(8,128)S(1)}, f32[32,96]{1,0:T(8,128)S(1)}, u32[]{:S(2)}, u32[]{:S(2)}) collective-permute-start(f32[32,96]{1,0:T(8,128)S(1)} %add.32), channel_id=1, source_target_pairs={{0,12},{1,13},{2,14},{3,15},{4,8},{5,9},{6,10},{7,11},{8,4},{9,5},... | collective-permute-start | bytes 36872 | tf_op jit(solution)/shard_map/ppermute | solution.py:424
  102.5 0.0 collective-permute-done.11
  102.5 0.4 collective-permute-done.12
  102.9 2.9 %collective-permute-done.13 = f32[32,96]{1,0:T(8,128)S(1)} collective-permute-done((f32[32,96]{1,0:T(8,128)S(1)}, f32[32,96]{1,0:T(8,128)S(1)}, u32[]{:S(2)}, u32[]{:S(2)}) %collective-permute-start.13) | collective-permute-done | bytes 12320 | tf_op jit(solution)/shard_map/ppermute | solution.py:424
  105.7 1.3 %collective-permute-start.14 = (f32[32,96]{1,0:T(8,128)S(1)}, f32[32,96]{1,0:T(8,128)S(1)}, u32[]{:S(2)}, u32[]{:S(2)}) collective-permute-start(f32[32,96]{1,0:T(8,128)S(1)} %add_add_fusion.1), channel_id=1, source_target_pairs={{0,2},{1,3},{2,0},{3,1},{4,6},{5,7},{6,4},{7,5},{8,10},{9,11},{10,... | collective-permute-start | bytes 36872 | tf_op jit(solution)/shard_map/ppermute | solution.py:424
  107.1 0.4 collective-permute-start.15
  107.4 1.8 %collective-permute-start.16 = (f32[32,96]{1,0:T(8,128)S(1)}, f32[32,96]{1,0:T(8,128)S(1)}, u32[]{:S(2)}, u32[]{:S(2)}) collective-permute-start(f32[32,96]{1,0:T(8,128)S(1)} %add_add_fusion.1), channel_id=1, source_target_pairs={{0,18},{1,19},{2,16},{3,17},{4,22},{5,23},{6,20},{7,21},{8,26},{9,... | collective-permute-start | bytes 36872 | tf_op jit(solution)/shard_map/ppermute | solution.py:424
  109.2 0.2 collective-permute-done.14
  109.5 1.3 %collective-permute-done.15 = f32[32,96]{1,0:T(8,128)S(1)} collective-permute-done((f32[32,96]{1,0:T(8,128)S(1)}, f32[32,96]{1,0:T(8,128)S(1)}, u32[]{:S(2)}, u32[]{:S(2)}) %collective-permute-start.15) | collective-permute-done | bytes 12320 | tf_op jit(solution)/shard_map/ppermute | solution.py:424
  110.8 1.3 collective-permute-done.16
  112.1 4.1 %shard_map.68 = (f32[16,8192]{1,0:T(8,128)S(1)}, bf16[32,128]{1,0:T(8,128)(2,1)S(1)}) custom-call(s32[1]{0:T(128)} %bitcast.group_ref.place_ref, f32[32,96]{1,0:T(8,128)S(1)} %add_add_fusion.g_ref, f32[2048,128]{1,0:T(8,128)S(1)} %bitcast.21, f32[32,8192]{1,0:T(8,128)S(1)} %get-tuple-element.48.t_ref, f32[64,128]{1,0:T(8,128)S(1)} %constant_dynamic-slice_fusion.v_ref), custom_call_target="tpu_custom_call" | custom-call | flops 4000000000 | bytes 2097152 | tf_op jit(solution)/shard_map/pallas_call | solution.py:386
  116.1 0.0 copy-done.4
  116.1 1.7 %collective-permute-start.17 = (f32[16,8192]{1,0:T(8,128)S(1)}, f32[16,8192]{1,0:T(8,128)S(1)}, u32[]{:S(2)}, u32[]{:S(2)}) collective-permute-start(f32[16,8192]{1,0:T(8,128)S(1)} %get-tuple-element.50), channel_id=1, source_target_pairs={{0,16},{16,0},{1,17},{17,1},{2,18},{18,2},{3,19},{19,3},{4,20},{20... | collective-permute-start | bytes 1572872 | tf_op jit(solution)/shard_map/ppermute | solution.py:424
  117.9 1.2 copy-done.5
  119.1 1.8 %shard_map.69 = f32[16,16384]{1,0:T(8,128)} custom-call(s32[1]{0:T(128)} %bitcast.group_ref.place_ref, bf16[32,128]{1,0:T(8,128)(2,1)S(1)} %get-tuple-element.49.mix_ref, f32[2048,128]{1,0:T(8,128)S(1)} %bitcast.22, f32[32,8192]{1,0:T(8,128)S(1)} %copy-done.5, f32[64,128]{1,0:T(8,128)S(1)} %constant_dynamic-slice_fusion.v_ref), custom_call_target="tpu_custom_call" | custom-call | flops 4000000000 | bytes 2097152 | tf_op jit(solution)/shard_map/pallas_call | solution.py:410
  120.9 5.9 %collective-permute-done.17 = f32[16,8192]{1,0:T(8,128)S(1)} collective-permute-done((f32[16,8192]{1,0:T(8,128)S(1)}, f32[16,8192]{1,0:T(8,128)S(1)}, u32[]{:S(2)}, u32[]{:S(2)}) %collective-permute-start.17) | collective-permute-done | bytes 524320 | tf_op jit(solution)/shard_map/ppermute | solution.py:424
  126.9 0.8 constant_dynamic-update-slice_fusion
  (5 shorter events, 0.0 us)
Async XLA Ops:
  0.0 4.2 %copy-start = (f32[1,262144]{1,0:T(1,128)S(1)}, f32[1,262144]{1,0:T(1,128)}, u32[]{:S(2)}) copy-start(f32[1,262144]{1,0:T(1,128)} %param.7) | copy-start | bytes 3145732
  0.0 22.7 %collective-permute-start.3 = (f32[2048,128]{1,0:T(8,128)}, f32[2048,128]{1,0:T(8,128)}, u32[]{:S(2)}, u32[]{:S(2)}) collective-permute-start(f32[2048,128]{1,0:T(8,128)} %bitcast.23), channel_id=1, source_target_pairs={{0,1},{1,0},{2,3},{3,2},{4,5},{5,4},{6,7},{7,6},{8,9},{9,8},{10,11... | collective-permute-start | bytes 3145736 | tf_op jit(solution)/shard_map/ppermute | solution.py:424
  1.5 17.8 %collective-permute-start = (f32[1024,128]{1,0:T(8,128)S(1)}, f32[1024,128]{1,0:T(8,128)}, u32[]{:S(2)}, u32[]{:S(2)}) collective-permute-start(f32[1024,128]{1,0:T(8,128)S(1)} %constant_dynamic-slice_fusion.1), channel_id=1, source_target_pairs={{0,2},{1,3},{2,0},{3,1},{4,6},{5,7},{6,4},{7,5},{8,10},{9,11},{10,... | collective-permute-start | bytes 1572872 | tf_op jit(solution)/shard_map/ppermute | solution.py:424
  5.0 17.6 %copy-start.2 = (bf16[448,256]{1,0:T(8,128)(2,1)S(1)}, bf16[448,256]{1,0:T(8,128)(2,1)}, u32[]{:S(2)}) copy-start(bf16[448,256]{1,0:T(8,128)(2,1)} %constant.29.clone.table_ref) | copy-start | bytes 688132
  5.0 17.6 %copy-start.3 = (f32[16384]{0:T(1024)S(1)}, f32[16384]{0:T(1024)}, u32[]{:S(2)}) copy-start(f32[16384]{0:T(1024)} %param.8) | copy-start | bytes 196612
  5.0 26.4 %all-to-all-start = ((f32[16,64,128]{2,1,0:T(8,128)}), f32[16,64,128]{2,1,0:T(8,128)S(1)}, u32[]{:S(2)}, u32[]{:S(2)}) async-start(f32[16,64,128]{2,1,0:T(8,128)} %slice.8), calls=%async_computation | async-start | bytes 1048576 | tf_op jit(solution)/shard_map/all_to_all | solution.py:460
  19.3 16.6 %collective-permute-start.1 = (f32[1024,128]{1,0:T(8,128)}, f32[1024,128]{1,0:T(8,128)S(1)}, u32[]{:S(2)}, u32[]{:S(2)}) collective-permute-start(f32[1024,128]{1,0:T(8,128)} %collective-permute-done.own_ref), channel_id=1, source_target_pairs={{0,4},{1,5},{2,14},{3,15},{4,8},{5,9},{6,2},{7,3},{8,12},{9,13},{1... | collective-permute-start | bytes 1572872 | tf_op jit(solution)/shard_map/ppermute | solution.py:424
  21.1 14.7 %collective-permute-start.2 = (f32[1024,128]{1,0:T(8,128)}, f32[1024,128]{1,0:T(8,128)}, u32[]{:S(2)}, u32[]{:S(2)}) collective-permute-start(f32[1024,128]{1,0:T(8,128)} %collective-permute-done.own_ref), channel_id=1, source_target_pairs={{0,16},{16,0},{1,17},{17,1},{2,18},{18,2},{3,19},{19,3},{4,20},{20... | collective-permute-start | bytes 1572872 | tf_op jit(solution)/shard_map/ppermute | solution.py:424
  22.7 1.2 copy-start.1
  35.9 13.8 %collective-permute-start.4 = (f32[1024,128]{1,0:T(8,128)S(1)}, f32[1024,128]{1,0:T(8,128)S(1)}, u32[]{:S(2)}, u32[]{:S(2)}) collective-permute-start(f32[1024,128]{1,0:T(8,128)S(1)} %collective-permute-done.1.refs_0_), channel_id=1, source_target_pairs={{0,16},{16,0},{1,17},{17,1},{2,18},{18,2},{3,19},{19,3},{4,20},{20... | collective-permute-start | bytes 1572872 | tf_op jit(solution)/shard_map/ppermute | solution.py:424
  37.4 12.9 %collective-permute-start.5 = (f32[1024,128]{1,0:T(8,128)}, f32[1024,128]{1,0:T(8,128)}, u32[]{:S(2)}, u32[]{:S(2)}) collective-permute-start(f32[1024,128]{1,0:T(8,128)} %collective-permute-done.own_ref), channel_id=1, source_target_pairs={{0,1},{1,0},{2,3},{3,2},{4,5},{5,4},{6,7},{7,6},{8,9},{9,8},{10,11... | collective-permute-start | bytes 1572872 | tf_op jit(solution)/shard_map/ppermute | solution.py:424
  37.4 12.9 %collective-permute-start.6 = (f32[1024,128]{1,0:T(8,128)}, f32[1024,128]{1,0:T(8,128)}, u32[]{:S(2)}, u32[]{:S(2)}) collective-permute-start(f32[1024,128]{1,0:T(8,128)} %collective-permute-done.2.other_ref), channel_id=1, source_target_pairs={{0,1},{1,0},{2,3},{3,2},{4,5},{5,4},{6,7},{7,6},{8,9},{9,8},{10,11... | collective-permute-start | bytes 1572872 | tf_op jit(solution)/shard_map/ppermute | solution.py:424
  38.7 23.4 %all-to-all-start.1 = ((f32[16,64,128]{2,1,0:T(8,128)}), f32[16,64,128]{2,1,0:T(8,128)S(1)}, u32[]{:S(2)}, u32[]{:S(2)}) async-start(f32[16,64,128]{2,1,0:T(8,128)} %slice.9), calls=%async_computation.1 | async-start | bytes 1048576 | tf_op jit(solution)/shard_map/all_to_all | solution.py:460
  49.7 2.1 %collective-permute-start.7 = (f32[1024,128]{1,0:T(8,128)S(1)}, f32[1024,128]{1,0:T(8,128)}, u32[]{:S(2)}, u32[]{:S(2)}) collective-permute-start(f32[1024,128]{1,0:T(8,128)S(1)} %collective-permute-done.1.refs_0_), channel_id=1, source_target_pairs={{0,1},{1,0},{2,3},{3,2},{4,5},{5,4},{6,7},{7,6},{8,9},{9,8},{10,11... | collective-permute-start | bytes 1572872 | tf_op jit(solution)/shard_map/ppermute | solution.py:424
  50.1 2.4 %collective-permute-start.8 = (f32[1024,128]{1,0:T(8,128)S(1)}, f32[1024,128]{1,0:T(8,128)}, u32[]{:S(2)}, u32[]{:S(2)}) collective-permute-start(f32[1024,128]{1,0:T(8,128)S(1)} %collective-permute-done.4.refs_1_), channel_id=1, source_target_pairs={{0,1},{1,0},{2,3},{3,2},{4,5},{5,4},{6,7},{7,6},{8,9},{9,8},{10,11... | collective-permute-start | bytes 1572872 | tf_op jit(solution)/shard_map/ppermute | solution.py:424
  62.2 32.2 %all-to-all-start.2 = ((f32[32,64,128]{2,1,0:T(8,128)}), f32[32,64,128]{2,1,0:T(8,128)S(1)}, u32[]{:S(2)}, u32[]{:S(2)}) async-start(f32[32,64,128]{2,1,0:T(8,128)} %bitcast.9), calls=%async_computation.2 | async-start | bytes 2097152 | tf_op jit(solution)/shard_map/all_to_all | solution.py:444
  67.4 24.0 %collective-permute-start.9 = (f32[1024,128]{1,0:T(8,128)S(1)}, f32[1024,128]{1,0:T(8,128)S(1)}, u32[]{:S(2)}, u32[]{:S(2)}) collective-permute-start(f32[1024,128]{1,0:T(8,128)S(1)} %broadcast_select_fusion), channel_id=1, source_target_pairs={{0,16},{16,0},{1,17},{17,1},{2,18},{18,2},{3,19},{19,3},{4,20},{20... | collective-permute-start | bytes 1572872 | tf_op jit(solution)/shard_map/ppermute | solution.py:424
  96.8 19.3 %copy-start.4 = (f32[32,8192]{1,0:T(8,128)}, f32[32,8192]{1,0:T(8,128)S(1)}, u32[]{:S(2)}) copy-start(f32[32,8192]{1,0:T(8,128)S(1)} %get-tuple-element.48.t_ref) | copy-start | bytes 3145732
  96.8 1.2 collective-permute-start.10
  98.1 4.4 %collective-permute-start.11 = (f32[32,96]{1,0:T(8,128)S(1)}, f32[32,96]{1,0:T(8,128)S(1)}, u32[]{:S(2)}, u32[]{:S(2)}) collective-permute-start(f32[32,96]{1,0:T(8,128)S(1)} %add.32), channel_id=1, source_target_pairs={{0,4},{1,5},{2,6},{3,7},{4,0},{5,1},{6,2},{7,3},{8,12},{9,13},{10,... | collective-permute-start | bytes 36872 | tf_op jit(solution)/shard_map/ppermute | solution.py:424
  98.2 4.6 %collective-permute-start.12 = (f32[32,96]{1,0:T(8,128)S(1)}, f32[32,96]{1,0:T(8,128)S(1)}, u32[]{:S(2)}, u32[]{:S(2)}) collective-permute-start(f32[32,96]{1,0:T(8,128)S(1)} %add.32), channel_id=1, source_target_pairs={{0,8},{1,9},{2,10},{3,11},{4,12},{5,13},{6,14},{7,15},{8,0},{9,1},... | collective-permute-start | bytes 36872 | tf_op jit(solution)/shard_map/ppermute | solution.py:424
  100.2 5.5 %collective-permute-start.13 = (f32[32,96]{1,0:T(8,128)S(1)}, f32[32,96]{1,0:T(8,128)S(1)}, u32[]{:S(2)}, u32[]{:S(2)}) collective-permute-start(f32[32,96]{1,0:T(8,128)S(1)} %add.32), channel_id=1, source_target_pairs={{0,12},{1,13},{2,14},{3,15},{4,8},{5,9},{6,10},{7,11},{8,4},{9,5},... | collective-permute-start | bytes 36872 | tf_op jit(solution)/shard_map/ppermute | solution.py:424
  105.7 3.7 %collective-permute-start.14 = (f32[32,96]{1,0:T(8,128)S(1)}, f32[32,96]{1,0:T(8,128)S(1)}, u32[]{:S(2)}, u32[]{:S(2)}) collective-permute-start(f32[32,96]{1,0:T(8,128)S(1)} %add_add_fusion.1), channel_id=1, source_target_pairs={{0,2},{1,3},{2,0},{3,1},{4,6},{5,7},{6,4},{7,5},{8,10},{9,11},{10,... | collective-permute-start | bytes 36872 | tf_op jit(solution)/shard_map/ppermute | solution.py:424
  107.1 3.7 %collective-permute-start.15 = (f32[32,96]{1,0:T(8,128)S(1)}, f32[32,96]{1,0:T(8,128)S(1)}, u32[]{:S(2)}, u32[]{:S(2)}) collective-permute-start(f32[32,96]{1,0:T(8,128)S(1)} %add_add_fusion.1), channel_id=1, source_target_pairs={{0,16},{1,17},{2,18},{3,19},{4,20},{5,21},{6,22},{7,23},{8,24},{9,... | collective-permute-start | bytes 36872 | tf_op jit(solution)/shard_map/ppermute | solution.py:424
  107.4 4.6 %collective-permute-start.16 = (f32[32,96]{1,0:T(8,128)S(1)}, f32[32,96]{1,0:T(8,128)S(1)}, u32[]{:S(2)}, u32[]{:S(2)}) collective-permute-start(f32[32,96]{1,0:T(8,128)S(1)} %add_add_fusion.1), channel_id=1, source_target_pairs={{0,18},{1,19},{2,16},{3,17},{4,22},{5,23},{6,20},{7,21},{8,26},{9,... | collective-permute-start | bytes 36872 | tf_op jit(solution)/shard_map/ppermute | solution.py:424
  116.1 10.7 %collective-permute-start.17 = (f32[16,8192]{1,0:T(8,128)S(1)}, f32[16,8192]{1,0:T(8,128)S(1)}, u32[]{:S(2)}, u32[]{:S(2)}) collective-permute-start(f32[16,8192]{1,0:T(8,128)S(1)} %get-tuple-element.50), channel_id=1, source_target_pairs={{0,16},{16,0},{1,17},{17,1},{2,18},{18,2},{3,19},{19,3},{4,20},{20... | collective-permute-start | bytes 1572872 | tf_op jit(solution)/shard_map/ppermute | solution.py:424
  117.9 1.2 copy-start.5

commit v4 on v3

--- a/solution.py
+++ b/solution.py
@@ -465,12 +465,13 @@
     far = moved(near, ("orb",), lambda i: (i + (-4 if i & 2 else 4)) % n_orb)
     near = [near, swapped(near)]
     far, near, late, token, t_low = lax.optimization_barrier((far, near, target, token, t_low))
+    far_mate = mates([far])
     far = [far, swapped(far)]
     near_mate = mates(near)
     t_high = owned(late, part)
     going, token = single_step(group, token, target, near)
     far, token = lax.optimization_barrier((far, token))
-    fields = [far, near_mate, mates(far)]
+    fields = [far, near_mate, far_mate + mates(far[1:])]
     acc, token = pair_step(crossed, group, token, target, fields, [begun, going], True, n_grp, n_orb)
     acc, t_low, t_high = lax.optimization_barrier((acc, t_low, t_high))
     t_other = swapped(jnp.where(group == 0, t_high, t_low))

time: 128 us -> 128 us (level)
  transfers between devices with their start and end apart: 21 -> 21, of which waited for: 13 -> 12; matrix products, arithmetic and copies ran while one was open for 2% -> 2% of each run, Pallas kernels for 19% -> 20%
where the time goes in v4:
time: 128 us; the launch traced here: 127 us
  waiting for transfers between devices  53.7 us (42%)
  starting transfers between devices  35.7 us (28%)
  Pallas kernels  31.3 us (24%)
  local copies, waits for them, and re-layouts  6.04 us (5%)
    ppermute x18, waiting for transfers between devices, moved(): return lax.ppermute(x, axes, [(i, target(i)) for i in range(size)])  50.8 us
    ppermute x18, starting transfers between devices, moved(): return lax.ppermute(x, axes, [(i, target(i)) for i in range(size)])  20.2 us
    pallas_call x2, Pallas kernels, pair_step(): pl.pallas_call(functools.partial(pair_kernel, counts, len(accs), cut, n_g...  17.2 us
    all_to_all x2, starting transfers between devices, owned(): lax.all_to_all(piece, ('orb',), split_axis=0, concat_axis=0)  10.3 us
    pallas_call x1, Pallas kernels, single_step(): pl.pallas_call(single_kernel, out_shape=(FIELD, TOKEN), in_specs=[SMEM] +...  5.8 us
    all_to_all x1, starting transfers between devices, spread(): lax.all_to_all(value.reshape(n, part, LANES), ('grp', 'orb'), split_axis=...  5.17 us
    pallas_call x1, Pallas kernels, partner_step(): pl.pallas_call(functools.partial(partner_kernel, n, part, out_rows), out_...  4.05 us
    all_to_all x1, waiting for transfers between devices, spread(): lax.all_to_all(value.reshape(n, part, LANES), ('grp', 'orb'), split_axis=...  2.92 us
  transfers between devices with their start and end apart: 21, of which 12 were waited for; matrix products, arithmetic and copies ran while one was open for 2% of the time, Pallas kernels for 20%

profile of v4, /device:TPU:0, one launch (start us, length us, event | category | flops | bytes accessed | tf_op | source)
XLA Modules:
  0.0 127.1 jit_solution(6144504416221819145)
XLA Ops:
  0.0 0.0 copy-start
  0.0 0.5 collective-permute-start.3
  0.5 1.1 constant_dynamic-slice_fusion.1
  1.5 2.6 %collective-permute-start = (f32[1024,128]{1,0:T(8,128)S(1)}, f32[1024,128]{1,0:T(8,128)}, u32[]{:S(2)}, u32[]{:S(2)}) collective-permute-start(f32[1024,128]{1,0:T(8,128)S(1)} %constant_dynamic-slice_fusion.1), channel_id=1, source_target_pairs={{0,2},{1,3},{2,0},{3,1},{4,6},{5,7},{6,4},{7,5},{8,10},{9,11},{10,... | collective-permute-start | bytes 1572872 | tf_op jit(solution)/shard_map/ppermute | solution.py:424
  4.2 0.0 copy-done
  4.2 0.8 slice.8
  5.0 0.0 copy-start.2
  5.0 0.0 copy-start.3
  5.0 5.1 %all-to-all-start = ((f32[16,64,128]{2,1,0:T(8,128)}), f32[16,64,128]{2,1,0:T(8,128)S(1)}, u32[]{:S(2)}, u32[]{:S(2)}) async-start(f32[16,64,128]{2,1,0:T(8,128)} %slice.8), calls=%async_computation | async-start | bytes 1048576 | tf_op jit(solution)/shard_map/all_to_all | solution.py:460
  10.1 9.2 %collective-permute-done.own_ref = f32[1024,128]{1,0:T(8,128)} collective-permute-done((f32[1024,128]{1,0:T(8,128)S(1)}, f32[1024,128]{1,0:T(8,128)}, u32[]{:S(2)}, u32[]{:S(2)}) %collective-permute-start) | collective-permute-done | bytes 524320 | tf_op jit(solution)/shard_map/ppermute | solution.py:424
  19.3 1.8 %collective-permute-start.1 = (f32[1024,128]{1,0:T(8,128)}, f32[1024,128]{1,0:T(8,128)S(1)}, u32[]{:S(2)}, u32[]{:S(2)}) collective-permute-start(f32[1024,128]{1,0:T(8,128)} %collective-permute-done.own_ref), channel_id=1, source_target_pairs={{0,4},{1,5},{2,14},{3,15},{4,8},{5,9},{6,2},{7,3},{8,12},{9,13},{1... | collective-permute-start | bytes 1572872 | tf_op jit(solution)/shard_map/ppermute | solution.py:424
  21.1 1.5 %collective-permute-start.2 = (f32[1024,128]{1,0:T(8,128)}, f32[1024,128]{1,0:T(8,128)}, u32[]{:S(2)}, u32[]{:S(2)}) collective-permute-start(f32[1024,128]{1,0:T(8,128)} %collective-permute-done.own_ref), channel_id=1, source_target_pairs={{0,16},{16,0},{1,17},{17,1},{2,18},{18,2},{3,19},{19,3},{4,20},{20... | collective-permute-start | bytes 1572872 | tf_op jit(solution)/shard_map/ppermute | solution.py:424
  22.7 0.0 collective-permute-done.3.refs_1_
  22.7 0.0 copy-done.2
  22.7 0.0 copy-done.3
  22.7 0.0 copy-start.1
  22.7 1.2 copy-done.1
  23.9 7.5 %shard_map.64 = (f32[2048,128]{1,0:T(8,128)}, f32[8,128]{1,0:T(8,128)S(1)}) custom-call(f32[1]{0:T(128)} %constant.11.clone.1.flag_ref, s32[1]{0:T(128)} %bitcast.group_ref.place_ref, f32[128,128]{1,0:T(8,128)S(1)} %bitcast.26, bf16[448,256]{1,0:T(8,128)(2,1)S(1)} %copy-done.2, f32[2048,128]{1,0:T(8,128)S(1)} %bitcast.12, f32[2048,128]{1,0:T(8,128)S(1)} %bitcast.25, ...), custom_call_target="tpu_custom_call" | custom-call | flops 8000000000 | bytes 262144 | tf_op jit(solution)/shard_map/pallas_call | solution.py:250
  31.4 0.0 all-to-all-done
  31.5 4.4 %collective-permute-done.1.refs_0_ = f32[1024,128]{1,0:T(8,128)S(1)} collective-permute-done((f32[1024,128]{1,0:T(8,128)}, f32[1024,128]{1,0:T(8,128)S(1)}, u32[]{:S(2)}, u32[]{:S(2)}) %collective-permute-start.1) | collective-permute-done | bytes 524320 | tf_op jit(solution)/shard_map/ppermute | solution.py:424
  35.9 0.0 collective-permute-done.2.other_ref
  35.9 1.5 %collective-permute-start.4 = (f32[1024,128]{1,0:T(8,128)S(1)}, f32[1024,128]{1,0:T(8,128)S(1)}, u32[]{:S(2)}, u32[]{:S(2)}) collective-permute-start(f32[1024,128]{1,0:T(8,128)S(1)} %collective-permute-done.1.refs_0_), channel_id=1, source_target_pairs={{0,16},{16,0},{1,17},{17,1},{2,18},{18,2},{3,19},{19,3},{4,20},{20... | collective-permute-start | bytes 1572872 | tf_op jit(solution)/shard_map/ppermute | solution.py:424
  37.4 0.0 collective-permute-start.7
  37.4 0.5 collective-permute-start.5
  37.9 0.0 collective-permute-start.6
  37.9 0.8 slice.9
  38.7 5.2 %all-to-all-start.1 = ((f32[16,64,128]{2,1,0:T(8,128)}), f32[16,64,128]{2,1,0:T(8,128)S(1)}, u32[]{:S(2)}, u32[]{:S(2)}) async-start(f32[16,64,128]{2,1,0:T(8,128)} %slice.9), calls=%async_computation.1 | async-start | bytes 1048576 | tf_op jit(solution)/shard_map/all_to_all | solution.py:460
  44.0 5.8 %shard_map.65 = (f32[2048,128]{1,0:T(8,128)}, f32[8,128]{1,0:T(8,128)S(1)}) custom-call(s32[1]{0:T(128)} %bitcast.group_ref.place_ref, f32[8,128]{1,0:T(8,128)S(1)} %get-tuple-element.32.earlier_ref, bf16[448,256]{1,0:T(8,128)(2,1)S(1)} %copy-done.2, f32[2048,128]{1,0:T(8,128)S(1)} %bitcast.14, f32[1024,128]{1,0:T(8,128)} %collective-permute-done.own_ref, ...), custom_call_target="tpu_custom_call" | custom-call | flops 10000000000 | bytes 4194304 | tf_op jit(solution)/shard_map/pallas_call | solution.py:266
  49.8 0.0 collective-permute-done.4.refs_1_
  49.8 0.5 collective-permute-start.8
  50.3 0.0 collective-permute-done.7.refs_4_
  50.3 0.0 collective-permute-done.5.refs_2_
  50.3 0.0 collective-permute-done.6.refs_3_
  50.3 1.7 %collective-permute-done.8.refs_5_ = f32[1024,128]{1,0:T(8,128)} collective-permute-done((f32[1024,128]{1,0:T(8,128)S(1)}, f32[1024,128]{1,0:T(8,128)}, u32[]{:S(2)}, u32[]{:S(2)}) %collective-permute-start.8) | collective-permute-done | bytes 524320 | tf_op jit(solution)/shard_map/ppermute | solution.py:424
  51.9 9.6 %shard_map.66 = (f32[2048,128]{1,0:T(8,128)}, f32[8,128]{1,0:T(8,128)}) custom-call(f32[1]{0:T(128)} %bitcast.1.flag_ref, s32[1]{0:T(128)} %bitcast.group_ref.place_ref, f32[8,128]{1,0:T(8,128)S(1)} %get-tuple-element.36.earlier_ref, bf16[448,256]{1,0:T(8,128)(2,1)S(1)} %copy-done.2, f32[2048,128]{1,0:T(8,128)S(1)} %bitcast.15, ...), custom_call_target="tpu_custom_call" | custom-call | flops 100000000 | bytes 262144 | tf_op jit(solution)/shard_map/pallas_call | solution.py:250
  61.5 0.0 all-to-all-done.1
  61.6 5.2 %all-to-all-start.2 = ((f32[32,64,128]{2,1,0:T(8,128)}), f32[32,64,128]{2,1,0:T(8,128)S(1)}, u32[]{:S(2)}, u32[]{:S(2)}) async-start(f32[32,64,128]{2,1,0:T(8,128)} %bitcast.9), calls=%async_computation.2 | async-start | bytes 2097152 | tf_op jit(solution)/shard_map/all_to_all | solution.py:444
  66.7 0.1 broadcast_select_fusion
  66.8 1.6 %collective-permute-start.9 = (f32[1024,128]{1,0:T(8,128)S(1)}, f32[1024,128]{1,0:T(8,128)S(1)}, u32[]{:S(2)}, u32[]{:S(2)}) collective-permute-start(f32[1024,128]{1,0:T(8,128)S(1)} %broadcast_select_fusion), channel_id=1, source_target_pairs={{0,16},{16,0},{1,17},{17,1},{2,18},{18,2},{3,19},{19,3},{4,20},{20... | collective-permute-start | bytes 1572872 | tf_op jit(solution)/shard_map/ppermute | solution.py:424
  68.4 22.4 %collective-permute-done.9.th_ref = f32[1024,128]{1,0:T(8,128)S(1)} collective-permute-done((f32[1024,128]{1,0:T(8,128)S(1)}, f32[1024,128]{1,0:T(8,128)S(1)}, u32[]{:S(2)}, u32[]{:S(2)}) %collective-permute-start.9) | collective-permute-done | bytes 524320 | tf_op jit(solution)/shard_map/ppermute | solution.py:424
  90.8 2.9 %all-to-all-done.2 = f32[32,64,128]{2,1,0:T(8,128)S(1)} async-done(((f32[32,64,128]{2,1,0:T(8,128)}), f32[32,64,128]{2,1,0:T(8,128)S(1)}, u32[]{:S(2)}, u32[]{:S(2)}) %all-to-all-start.2) | async-done | bytes 1048608 | tf_op jit(solution)/shard_map/all_to_all | solution.py:444
  93.7 2.5 %shard_map.67 = (f32[32,96]{1,0:T(8,128)S(1)}, f32[32,8192]{1,0:T(8,128)S(1)}) custom-call(s32[1]{0:T(128)} %bitcast.group_ref.place_ref, f32[2048,128]{1,0:T(8,128)S(1)} %bitcast.20, f32[1024,128]{1,0:T(8,128)S(1)} %bitcast.17, f32[1024,128]{1,0:T(8,128)S(1)} %bitcast.19, f32[1024,128]{1,0:T(8,128)S(1)} %collective-permute-done.9.th_ref, ...), custom_call_target="tpu_custom_call" | custom-call | flops 1000000000 | bytes 2097152 | tf_op jit(solution)/shard_map/pallas_call | solution.py:305
  96.2 0.0 copy-start.4
  96.2 0.1 collective-permute-start.10
  96.3 1.2 collective-permute-done.10
  97.5 0.2 collective-permute-start.11
  97.6 2.0 %collective-permute-start.12 = (f32[32,96]{1,0:T(8,128)S(1)}, f32[32,96]{1,0:T(8,128)S(1)}, u32[]{:S(2)}, u32[]{:S(2)}) collective-permute-start(f32[32,96]{1,0:T(8,128)S(1)} %add.32), channel_id=1, source_target_pairs={{0,8},{1,9},{2,10},{3,11},{4,12},{5,13},{6,14},{7,15},{8,0},{9,1},... | collective-permute-start | bytes 36872 | tf_op jit(solution)/shard_map/ppermute | solution.py:424
  99.6 2.3 %collective-permute-start.13 = (f32[32,96]{1,0:T(8,128)S(1)}, f32[32,96]{1,0:T(8,128)S(1)}, u32[]{:S(2)}, u32[]{:S(2)}) collective-permute-start(f32[32,96]{1,0:T(8,128)S(1)} %add.32), channel_id=1, source_target_pairs={{0,12},{1,13},{2,14},{3,15},{4,8},{5,9},{6,10},{7,11},{8,4},{9,5},... | collective-permute-start | bytes 36872 | tf_op jit(solution)/shard_map/ppermute | solution.py:424
  101.8 0.0 collective-permute-done.11
  101.8 0.4 collective-permute-done.12
  102.3 2.9 %collective-permute-done.13 = f32[32,96]{1,0:T(8,128)S(1)} collective-permute-done((f32[32,96]{1,0:T(8,128)S(1)}, f32[32,96]{1,0:T(8,128)S(1)}, u32[]{:S(2)}, u32[]{:S(2)}) %collective-permute-start.13) | collective-permute-done | bytes 12320 | tf_op jit(solution)/shard_map/ppermute | solution.py:424
  105.1 1.3 %collective-permute-start.14 = (f32[32,96]{1,0:T(8,128)S(1)}, f32[32,96]{1,0:T(8,128)S(1)}, u32[]{:S(2)}, u32[]{:S(2)}) collective-permute-start(f32[32,96]{1,0:T(8,128)S(1)} %add_add_fusion.1), channel_id=1, source_target_pairs={{0,2},{1,3},{2,0},{3,1},{4,6},{5,7},{6,4},{7,5},{8,10},{9,11},{10,... | collective-permute-start | bytes 36872 | tf_op jit(solution)/shard_map/ppermute | solution.py:424
  106.4 0.4 collective-permute-start.15
  106.8 1.8 %collective-permute-start.16 = (f32[32,96]{1,0:T(8,128)S(1)}, f32[32,96]{1,0:T(8,128)S(1)}, u32[]{:S(2)}, u32[]{:S(2)}) collective-permute-start(f32[32,96]{1,0:T(8,128)S(1)} %add_add_fusion.1), channel_id=1, source_target_pairs={{0,18},{1,19},{2,16},{3,17},{4,22},{5,23},{6,20},{7,21},{8,26},{9,... | collective-permute-start | bytes 36872 | tf_op jit(solution)/shard_map/ppermute | solution.py:424
  108.6 0.2 collective-permute-done.14
  108.9 1.3 %collective-permute-done.15 = f32[32,96]{1,0:T(8,128)S(1)} collective-permute-done((f32[32,96]{1,0:T(8,128)S(1)}, f32[32,96]{1,0:T(8,128)S(1)}, u32[]{:S(2)}, u32[]{:S(2)}) %collective-permute-start.15) | collective-permute-done | bytes 12320 | tf_op jit(solution)/shard_map/ppermute | solution.py:424
  110.2 1.3 collective-permute-done.16
  111.5 4.1 %shard_map.68 = (f32[16,8192]{1,0:T(8,128)S(1)}, bf16[32,128]{1,0:T(8,128)(2,1)S(1)}) custom-call(s32[1]{0:T(128)} %bitcast.group_ref.place_ref, f32[32,96]{1,0:T(8,128)S(1)} %add_add_fusion.g_ref, f32[2048,128]{1,0:T(8,128)S(1)} %bitcast.21, f32[32,8192]{1,0:T(8,128)S(1)} %get-tuple-element.48.t_ref, f32[64,128]{1,0:T(8,128)S(1)} %constant_dynamic-slice_fusion.v_ref), custom_call_target="tpu_custom_call" | custom-call | flops 4000000000 | bytes 2097152 | tf_op jit(solution)/shard_map/pallas_call | solution.py:386
  115.5 0.0 copy-done.4
  115.5 1.7 %collective-permute-start.17 = (f32[16,8192]{1,0:T(8,128)S(1)}, f32[16,8192]{1,0:T(8,128)S(1)}, u32[]{:S(2)}, u32[]{:S(2)}) collective-permute-start(f32[16,8192]{1,0:T(8,128)S(1)} %get-tuple-element.50), channel_id=1, source_target_pairs={{0,16},{16,0},{1,17},{17,1},{2,18},{18,2},{3,19},{19,3},{4,20},{20... | collective-permute-start | bytes 1572872 | tf_op jit(solution)/shard_map/ppermute | solution.py:424
  117.2 1.2 copy-done.5
  118.5 1.8 %shard_map.69 = f32[16,16384]{1,0:T(8,128)} custom-call(s32[1]{0:T(128)} %bitcast.group_ref.place_ref, bf16[32,128]{1,0:T(8,128)(2,1)S(1)} %get-tuple-element.49.mix_ref, f32[2048,128]{1,0:T(8,128)S(1)} %bitcast.22, f32[32,8192]{1,0:T(8,128)S(1)} %copy-done.5, f32[64,128]{1,0:T(8,128)S(1)} %constant_dynamic-slice_fusion.v_ref), custom_call_target="tpu_custom_call" | custom-call | flops 4000000000 | bytes 2097152 | tf_op jit(solution)/shard_map/pallas_call | solution.py:410
  120.3 5.9 %collective-permute-done.17 = f32[16,8192]{1,0:T(8,128)S(1)} collective-permute-done((f32[16,8192]{1,0:T(8,128)S(1)}, f32[16,8192]{1,0:T(8,128)S(1)}, u32[]{:S(2)}, u32[]{:S(2)}) %collective-permute-start.17) | collective-permute-done | bytes 524320 | tf_op jit(solution)/shard_map/ppermute | solution.py:424
  126.2 0.8 constant_dynamic-update-slice_fusion
  (5 shorter events, 0.0 us)
Async XLA Ops:
  0.0 4.2 %copy-start = (f32[1,262144]{1,0:T(1,128)S(1)}, f32[1,262144]{1,0:T(1,128)}, u32[]{:S(2)}) copy-start(f32[1,262144]{1,0:T(1,128)} %param.7) | copy-start | bytes 3145732
  0.0 22.7 %collective-permute-start.3 = (f32[2048,128]{1,0:T(8,128)}, f32[2048,128]{1,0:T(8,128)}, u32[]{:S(2)}, u32[]{:S(2)}) collective-permute-start(f32[2048,128]{1,0:T(8,128)} %bitcast.23), channel_id=1, source_target_pairs={{0,1},{1,0},{2,3},{3,2},{4,5},{5,4},{6,7},{7,6},{8,9},{9,8},{10,11... | collective-permute-start | bytes 3145736 | tf_op jit(solution)/shard_map/ppermute | solution.py:424
  1.5 17.8 %collective-permute-start = (f32[1024,128]{1,0:T(8,128)S(1)}, f32[1024,128]{1,0:T(8,128)}, u32[]{:S(2)}, u32[]{:S(2)}) collective-permute-start(f32[1024,128]{1,0:T(8,128)S(1)} %constant_dynamic-slice_fusion.1), channel_id=1, source_target_pairs={{0,2},{1,3},{2,0},{3,1},{4,6},{5,7},{6,4},{7,5},{8,10},{9,11},{10,... | collective-permute-start | bytes 1572872 | tf_op jit(solution)/shard_map/ppermute | solution.py:424
  5.0 17.6 %copy-start.2 = (bf16[448,256]{1,0:T(8,128)(2,1)S(1)}, bf16[448,256]{1,0:T(8,128)(2,1)}, u32[]{:S(2)}) copy-start(bf16[448,256]{1,0:T(8,128)(2,1)} %constant.29.clone.table_ref) | copy-start | bytes 688132
  5.0 17.6 %copy-start.3 = (f32[16384]{0:T(1024)S(1)}, f32[16384]{0:T(1024)}, u32[]{:S(2)}) copy-start(f32[16384]{0:T(1024)} %param.8) | copy-start | bytes 196612
  5.0 26.4 %all-to-all-start = ((f32[16,64,128]{2,1,0:T(8,128)}), f32[16,64,128]{2,1,0:T(8,128)S(1)}, u32[]{:S(2)}, u32[]{:S(2)}) async-start(f32[16,64,128]{2,1,0:T(8,128)} %slice.8), calls=%async_computation | async-start | bytes 1048576 | tf_op jit(solution)/shard_map/all_to_all | solution.py:460
  19.3 16.6 %collective-permute-start.1 = (f32[1024,128]{1,0:T(8,128)}, f32[1024,128]{1,0:T(8,128)S(1)}, u32[]{:S(2)}, u32[]{:S(2)}) collective-permute-start(f32[1024,128]{1,0:T(8,128)} %collective-permute-done.own_ref), channel_id=1, source_target_pairs={{0,4},{1,5},{2,14},{3,15},{4,8},{5,9},{6,2},{7,3},{8,12},{9,13},{1... | collective-permute-start | bytes 1572872 | tf_op jit(solution)/shard_map/ppermute | solution.py:424
  21.1 14.7 %collective-permute-start.2 = (f32[1024,128]{1,0:T(8,128)}, f32[1024,128]{1,0:T(8,128)}, u32[]{:S(2)}, u32[]{:S(2)}) collective-permute-start(f32[1024,128]{1,0:T(8,128)} %collective-permute-done.own_ref), channel_id=1, source_target_pairs={{0,16},{16,0},{1,17},{17,1},{2,18},{18,2},{3,19},{19,3},{4,20},{20... | collective-permute-start | bytes 1572872 | tf_op jit(solution)/shard_map/ppermute | solution.py:424
  22.7 1.2 copy-start.1
  35.9 13.9 %collective-permute-start.4 = (f32[1024,128]{1,0:T(8,128)S(1)}, f32[1024,128]{1,0:T(8,128)S(1)}, u32[]{:S(2)}, u32[]{:S(2)}) collective-permute-start(f32[1024,128]{1,0:T(8,128)S(1)} %collective-permute-done.1.refs_0_), channel_id=1, source_target_pairs={{0,16},{16,0},{1,17},{17,1},{2,18},{18,2},{3,19},{19,3},{4,20},{20... | collective-permute-start | bytes 1572872 | tf_op jit(solution)/shard_map/ppermute | solution.py:424
  37.4 12.9 %collective-permute-start.7 = (f32[1024,128]{1,0:T(8,128)S(1)}, f32[1024,128]{1,0:T(8,128)}, u32[]{:S(2)}, u32[]{:S(2)}) collective-permute-start(f32[1024,128]{1,0:T(8,128)S(1)} %collective-permute-done.1.refs_0_), channel_id=1, source_target_pairs={{0,1},{1,0},{2,3},{3,2},{4,5},{5,4},{6,7},{7,6},{8,9},{9,8},{10,11... | collective-permute-start | bytes 1572872 | tf_op jit(solution)/shard_map/ppermute | solution.py:424
  37.4 12.9 %collective-permute-start.5 = (f32[1024,128]{1,0:T(8,128)}, f32[1024,128]{1,0:T(8,128)}, u32[]{:S(2)}, u32[]{:S(2)}) collective-permute-start(f32[1024,128]{1,0:T(8,128)} %collective-permute-done.own_ref), channel_id=1, source_target_pairs={{0,1},{1,0},{2,3},{3,2},{4,5},{5,4},{6,7},{7,6},{8,9},{9,8},{10,11... | collective-permute-start | bytes 1572872 | tf_op jit(solution)/shard_map/ppermute | solution.py:424
  37.9 12.4 %collective-permute-start.6 = (f32[1024,128]{1,0:T(8,128)}, f32[1024,128]{1,0:T(8,128)}, u32[]{:S(2)}, u32[]{:S(2)}) collective-permute-start(f32[1024,128]{1,0:T(8,128)} %collective-permute-done.2.other_ref), channel_id=1, source_target_pairs={{0,1},{1,0},{2,3},{3,2},{4,5},{5,4},{6,7},{7,6},{8,9},{9,8},{10,11... | collective-permute-start | bytes 1572872 | tf_op jit(solution)/shard_map/ppermute | solution.py:424
  38.7 22.8 %all-to-all-start.1 = ((f32[16,64,128]{2,1,0:T(8,128)}), f32[16,64,128]{2,1,0:T(8,128)S(1)}, u32[]{:S(2)}, u32[]{:S(2)}) async-start(f32[16,64,128]{2,1,0:T(8,128)} %slice.9), calls=%async_computation.1 | async-start | bytes 1048576 | tf_op jit(solution)/shard_map/all_to_all | solution.py:460
  49.8 2.1 %collective-permute-start.8 = (f32[1024,128]{1,0:T(8,128)S(1)}, f32[1024,128]{1,0:T(8,128)}, u32[]{:S(2)}, u32[]{:S(2)}) collective-permute-start(f32[1024,128]{1,0:T(8,128)S(1)} %collective-permute-done.4.refs_1_), channel_id=1, source_target_pairs={{0,1},{1,0},{2,3},{3,2},{4,5},{5,4},{6,7},{7,6},{8,9},{9,8},{10,11... | collective-permute-start | bytes 1572872 | tf_op jit(solution)/shard_map/ppermute | solution.py:424
  61.6 32.1 %all-to-all-start.2 = ((f32[32,64,128]{2,1,0:T(8,128)}), f32[32,64,128]{2,1,0:T(8,128)S(1)}, u32[]{:S(2)}, u32[]{:S(2)}) async-start(f32[32,64,128]{2,1,0:T(8,128)} %bitcast.9), calls=%async_computation.2 | async-start | bytes 2097152 | tf_op jit(solution)/shard_map/all_to_all | solution.py:444
  66.8 24.0 %collective-permute-start.9 = (f32[1024,128]{1,0:T(8,128)S(1)}, f32[1024,128]{1,0:T(8,128)S(1)}, u32[]{:S(2)}, u32[]{:S(2)}) collective-permute-start(f32[1024,128]{1,0:T(8,128)S(1)} %broadcast_select_fusion), channel_id=1, source_target_pairs={{0,16},{16,0},{1,17},{17,1},{2,18},{18,2},{3,19},{19,3},{4,20},{20... | collective-permute-start | bytes 1572872 | tf_op jit(solution)/shard_map/ppermute | solution.py:424
  96.2 19.3 %copy-start.4 = (f32[32,8192]{1,0:T(8,128)}, f32[32,8192]{1,0:T(8,128)S(1)}, u32[]{:S(2)}) copy-start(f32[32,8192]{1,0:T(8,128)S(1)} %get-tuple-element.48.t_ref) | copy-start | bytes 3145732
  96.2 1.2 collective-permute-start.10
  97.5 4.4 %collective-permute-start.11 = (f32[32,96]{1,0:T(8,128)S(1)}, f32[32,96]{1,0:T(8,128)S(1)}, u32[]{:S(2)}, u32[]{:S(2)}) collective-permute-start(f32[32,96]{1,0:T(8,128)S(1)} %add.32), channel_id=1, source_target_pairs={{0,4},{1,5},{2,6},{3,7},{4,0},{5,1},{6,2},{7,3},{8,12},{9,13},{10,... | collective-permute-start | bytes 36872 | tf_op jit(solution)/shard_map/ppermute | solution.py:424
  97.6 4.6 %collective-permute-start.12 = (f32[32,96]{1,0:T(8,128)S(1)}, f32[32,96]{1,0:T(8,128)S(1)}, u32[]{:S(2)}, u32[]{:S(2)}) collective-permute-start(f32[32,96]{1,0:T(8,128)S(1)} %add.32), channel_id=1, source_target_pairs={{0,8},{1,9},{2,10},{3,11},{4,12},{5,13},{6,14},{7,15},{8,0},{9,1},... | collective-permute-start | bytes 36872 | tf_op jit(solution)/shard_map/ppermute | solution.py:424
  99.6 5.5 %collective-permute-start.13 = (f32[32,96]{1,0:T(8,128)S(1)}, f32[32,96]{1,0:T(8,128)S(1)}, u32[]{:S(2)}, u32[]{:S(2)}) collective-permute-start(f32[32,96]{1,0:T(8,128)S(1)} %add.32), channel_id=1, source_target_pairs={{0,12},{1,13},{2,14},{3,15},{4,8},{5,9},{6,10},{7,11},{8,4},{9,5},... | collective-permute-start | bytes 36872 | tf_op jit(solution)/shard_map/ppermute | solution.py:424
  105.1 3.7 %collective-permute-start.14 = (f32[32,96]{1,0:T(8,128)S(1)}, f32[32,96]{1,0:T(8,128)S(1)}, u32[]{:S(2)}, u32[]{:S(2)}) collective-permute-start(f32[32,96]{1,0:T(8,128)S(1)} %add_add_fusion.1), channel_id=1, source_target_pairs={{0,2},{1,3},{2,0},{3,1},{4,6},{5,7},{6,4},{7,5},{8,10},{9,11},{10,... | collective-permute-start | bytes 36872 | tf_op jit(solution)/shard_map/ppermute | solution.py:424
  106.4 3.7 %collective-permute-start.15 = (f32[32,96]{1,0:T(8,128)S(1)}, f32[32,96]{1,0:T(8,128)S(1)}, u32[]{:S(2)}, u32[]{:S(2)}) collective-permute-start(f32[32,96]{1,0:T(8,128)S(1)} %add_add_fusion.1), channel_id=1, source_target_pairs={{0,16},{1,17},{2,18},{3,19},{4,20},{5,21},{6,22},{7,23},{8,24},{9,... | collective-permute-start | bytes 36872 | tf_op jit(solution)/shard_map/ppermute | solution.py:424
  106.8 4.6 %collective-permute-start.16 = (f32[32,96]{1,0:T(8,128)S(1)}, f32[32,96]{1,0:T(8,128)S(1)}, u32[]{:S(2)}, u32[]{:S(2)}) collective-permute-start(f32[32,96]{1,0:T(8,128)S(1)} %add_add_fusion.1), channel_id=1, source_target_pairs={{0,18},{1,19},{2,16},{3,17},{4,22},{5,23},{6,20},{7,21},{8,26},{9,... | collective-permute-start | bytes 36872 | tf_op jit(solution)/shard_map/ppermute | solution.py:424
  115.5 10.7 %collective-permute-start.17 = (f32[16,8192]{1,0:T(8,128)S(1)}, f32[16,8192]{1,0:T(8,128)S(1)}, u32[]{:S(2)}, u32[]{:S(2)}) collective-permute-start(f32[16,8192]{1,0:T(8,128)S(1)} %get-tuple-element.50), channel_id=1, source_target_pairs={{0,16},{16,0},{1,17},{17,1},{2,18},{18,2},{3,19},{19,3},{4,20},{20... | collective-permute-start | bytes 1572872 | tf_op jit(solution)/shard_map/ppermute | solution.py:424
  117.2 1.2 copy-start.5
